TPU v7x, 32 devices: a whole 2x2x4 slice. The times are simulated.
32 devices in a mesh: rep: 16 (over z, x, core), exp: 2 (over y).
Axes of the slice: x: 2, y: 2, z: 4, core: 2. Of those that a mesh axis runs over, the one named last changes fastest.
Arguments:
- tokens: float32 [128, 197, 512], P(('rep', 'exp')), may hold values from -6 to 6
- ln1_gain: float32 [2, 512], replicated, may hold values from 0.25 to 1.75
- ln1_bias: float32 [2, 512], replicated, may hold values from -1.75 to 1.75
- w_qkv: bfloat16 [2, 512, 1536], replicated, may hold values from -0.25 to 0.25
- w_attn_out: bfloat16 [2, 512, 512], replicated, may hold values from -2 to 2
- ln2_gain: float32 [2, 512], replicated, may hold values from 0.25 to 1.75
- ln2_bias: float32 [2, 512], replicated, may hold values from -1.75 to 1.75
- w_router: bfloat16 [2, 512, 8], replicated, may hold values from -0.1875 to 0.1875
- w_in: bfloat16 [2, 8, 512, 2048], P(None, 'exp'), may hold values from -0.25 to 0.25
- w_out: bfloat16 [2, 8, 2048, 512], P(None, 'exp'), may hold values from -3 to 3
- routes: int32 [2, 25216, 2], P(None, ('rep', 'exp')), may hold values from 0 to 7, all different within a row
- priority: int32 [2, 25216, 2], P(None, ('rep', 'exp')), may hold values from 0 to 1575, as said below
- cotangent: float32 [128, 197, 512], P(('rep', 'exp')), may hold values from -6 to 6
Outputs:
- block_out: float32 [128, 197, 512], P(('rep', 'exp'))
- grad_tokens: float32 [128, 197, 512], P(('rep', 'exp'))
- grad_ln1_gain: float32 [2, 512], P(None, 'exp')
- grad_ln1_bias: float32 [2, 512], P(None, 'exp')
- grad_w_qkv: float32 [2, 512, 1536], P(None, 'exp')
- grad_w_attn_out: float32 [2, 512, 512], P(None, 'exp')
- grad_ln2_gain: float32 [2, 512], P(None, 'exp')
- grad_ln2_bias: float32 [2, 512], P(None, 'exp')
- grad_w_router: float32 [2, 512, 8], P(None, 'exp')
- grad_w_in: float32 [2, 8, 512, 2048], P(None, 'exp', 'rep')
- grad_w_out: float32 [2, 8, 2048, 512], P(None, 'exp', 'rep')
Inputs may be any that keep to these rules, and one draw needn't show every extreme that they name: `priority`: within each layer, the pairs of one device's 788 tokens hold each rank of 0 to 1575 once. `routes`: the two experts of a token differ.
All inputs are finite; a program needn't handle non-finite values.
Results may differ from a plain program's by a relative error of at most 0.028.
Values may be sent and summed in bfloat16 or wider, within the bound.
No kernel may reach another device: no remote copies, remote signals or barrier semaphores. Data moves between devices by JAX's collectives and lax.ppermute only.
A program may use at most 320 MiB of HBM per device.

v0:
```python
from functools import partial

import jax
import jax.numpy as jnp
from jax import lax
from jax.sharding import PartitionSpec as P

HEADS = 8
HEAD_DIM = 64


EPSILON = 1e-06


def shortened(value):

    def short(part):
        return part.astype(jnp.bfloat16) if part.dtype == jnp.float32 else part

    return jax.tree.map(short, value)


def layer_norm(values, scales, shifts):
    average = jnp.mean(values, axis=-1, keepdims=True)
    centred = values - average
    spread = jnp.mean(centred * centred, axis=-1, keepdims=True)
    return centred * lax.rsqrt(spread + EPSILON) * scales + shifts


def slot_tables(route_block, rank_block, capacity, expert_count):
    expert_ids = route_block.reshape(-1)
    rank_ids = rank_block.reshape(-1)
    matching = expert_ids[:, None] == expert_ids[None, :]
    earlier = rank_ids[None, :] < rank_ids[:, None]
    position = jnp.sum(jnp.where(matching & earlier, 1, 0).astype(jnp.int32), axis=1)
    kept_mask = position < capacity
    slot_index = expert_ids * capacity + jnp.minimum(position, capacity - 1)
    target = jnp.where(kept_mask, slot_index, expert_count * capacity)
    pair_ids = jnp.arange(expert_ids.shape[0], dtype=jnp.int32)
    owners = jnp.full((expert_count * capacity + 1,), -1, jnp.int32).at[target].set(pair_ids)
    return (slot_index, kept_mask, owners[: expert_count * capacity])


def router_gates(logit_values, route_ids):
    return jnp.take_along_axis(jax.nn.softmax(logit_values, axis=-1), route_ids, axis=1)


def attention_scores(joined, images):
    split_heads = joined.reshape(images, -1, 3, HEADS, HEAD_DIM)
    queries = split_heads[:, :, 0]
    keys_part = split_heads[:, :, 1]
    values_part = split_heads[:, :, 2]
    scores = jnp.einsum(
        "bqhd,bkhd->bhqk", queries, keys_part, preferred_element_type=jnp.float32
    ) * HEAD_DIM ** (-0.5)
    return (queries, keys_part, values_part, scores)


def attention_forward(joined, images):
    queries, keys_part, values_part, scores = attention_scores(joined, images)
    largest = jnp.max(scores, axis=-1, keepdims=True)
    raised = jnp.exp(scores - largest)
    totals = jnp.sum(raised, axis=-1, keepdims=True)
    probs_low = (raised / totals).astype(jnp.bfloat16)
    mixed = jnp.einsum(
        "bhqk,bkhd->bqhd", probs_low, values_part, preferred_element_type=jnp.float32
    )
    return (
        mixed.reshape(joined.shape[0], HEADS * HEAD_DIM).astype(jnp.bfloat16),
        largest + jnp.log(totals),
    )


def attention_backward(joined, log_totals, d_attended, images):
    queries, keys_part, values_part, scores = attention_scores(joined, images)
    attn_probs = jnp.exp(scores - log_totals)
    probs_low = attn_probs.astype(jnp.bfloat16)
    d_heads = d_attended.reshape(images, -1, HEADS, HEAD_DIM)
    d_probs = jnp.einsum(
        "bqhd,bkhd->bhqk", d_heads, values_part, preferred_element_type=jnp.float32
    )
    d_values = jnp.einsum("bhqk,bqhd->bkhd", probs_low, d_heads, preferred_element_type=jnp.float32)
    d_scores = (
        attn_probs * (d_probs - jnp.sum(d_probs * attn_probs, axis=-1, keepdims=True))
    ).astype(jnp.bfloat16)
    score_scale = HEAD_DIM ** (-0.5)
    d_queries = (
        jnp.einsum("bhqk,bkhd->bqhd", d_scores, keys_part, preferred_element_type=jnp.float32)
        * score_scale
    )
    d_keys = (
        jnp.einsum("bhqk,bqhd->bkhd", d_scores, queries, preferred_element_type=jnp.float32)
        * score_scale
    )
    return (
        jnp.stack((d_queries, d_keys, d_values), axis=2).reshape(joined.shape).astype(jnp.bfloat16)
    )


def local(
    tokens,
    ln1_gain,
    ln1_bias,
    w_qkv,
    w_attn_out,
    ln2_gain,
    ln2_bias,
    w_router,
    w_in,
    w_out,
    routes,
    priority,
    cotangent,
):
    images, seq_len, model_width = tokens.shape
    tok_count = images * seq_len
    layer_count = w_qkv.shape[0]
    expert_count = lax.axis_size("exp") * w_in.shape[1]
    capacity = 2 * tok_count // expert_count
    residual = tokens.reshape(tok_count, model_width)
    kept_cache = []
    for layer_index in range(layer_count):
        slot_index, kept_mask, owners = slot_tables(
            routes[layer_index], priority[layer_index], capacity, expert_count
        )
        valid_slots = owners >= 0
        owner_pair = jnp.maximum(owners, 0)
        layer_in = residual
        normed = layer_norm(residual, ln1_gain[layer_index], ln1_bias[layer_index]).astype(
            jnp.bfloat16
        )
        joined = jnp.dot(normed, w_qkv[layer_index], preferred_element_type=jnp.float32).astype(
            jnp.bfloat16
        )
        attended, log_totals = attention_forward(joined, images)
        middle = residual + jnp.dot(
            attended, w_attn_out[layer_index], preferred_element_type=jnp.float32
        )
        moe_in = layer_norm(middle, ln2_gain[layer_index], ln2_bias[layer_index]).astype(
            jnp.bfloat16
        )
        logits = jnp.dot(moe_in, w_router[layer_index], preferred_element_type=jnp.float32)
        gate_values = router_gates(logits, routes[layer_index])
        dispatched = jnp.where(
            valid_slots[:, None], moe_in[owner_pair // 2], jnp.zeros((), jnp.bfloat16)
        )
        received = lax.all_to_all(
            dispatched.reshape(expert_count, capacity, model_width),
            "exp",
            split_axis=0,
            concat_axis=1,
            tiled=True,
        )
        pre_act = jnp.einsum(
            "erd,edh->erh", received, w_in[layer_index], preferred_element_type=jnp.float32
        )
        activated = jax.nn.gelu(pre_act, approximate=False).astype(jnp.bfloat16)
        produced = jnp.einsum(
            "erh,ehd->erd", activated, w_out[layer_index], preferred_element_type=jnp.float32
        ).astype(jnp.bfloat16)
        returned = lax.all_to_all(produced, "exp", split_axis=1, concat_axis=0, tiled=True).reshape(
            expert_count * capacity, model_width
        )
        picked = returned[slot_index].astype(jnp.float32).reshape(tok_count, 2, model_width)
        kept_pairs = kept_mask.reshape(tok_count, 2).astype(jnp.float32)
        weights = gate_values * kept_pairs
        residual = middle + jnp.sum(weights[:, :, None] * picked, axis=1)
        kept_cache.append(
            (
                layer_in,
                normed,
                joined,
                log_totals,
                attended,
                middle,
                moe_in,
                logits,
                slot_index,
                kept_pairs,
                valid_slots,
                owner_pair,
                received,
                pre_act,
                activated,
                picked,
                weights,
            )
        )
    block_out = residual.reshape(images, seq_len, model_width)
    grad_state = cotangent.reshape(tok_count, model_width)
    dense_list = []
    expert_list = []
    for layer_index in reversed(range(layer_count)):
        (
            layer_in,
            normed,
            joined,
            log_totals,
            attended,
            middle,
            moe_in,
            logits,
            slot_index,
            kept_pairs,
            valid_slots,
            owner_pair,
            received,
            pre_act,
            activated,
            picked,
            weights,
        ) = kept_cache[layer_index]
        d_gates = kept_pairs * jnp.sum(grad_state[:, None, :] * picked, axis=2)
        d_pairs = (weights[:, :, None] * grad_state[:, None, :]).reshape(2 * tok_count, model_width)
        d_slots = jnp.where(valid_slots[:, None], d_pairs[owner_pair], 0.0).astype(jnp.bfloat16)
        d_produced = lax.all_to_all(
            d_slots.reshape(expert_count, capacity, model_width),
            "exp",
            split_axis=0,
            concat_axis=1,
            tiled=True,
        )
        grad_w_out = jnp.einsum(
            "erh,erd->ehd", activated, d_produced, preferred_element_type=jnp.float32
        )
        d_act = jnp.einsum(
            "erd,ehd->erh", d_produced, w_out[layer_index], preferred_element_type=jnp.float32
        )
        gelu_pull = jax.vjp(partial(jax.nn.gelu, approximate=False), pre_act)[1]
        d_pre = gelu_pull(d_act)[0].astype(jnp.bfloat16)
        grad_w_in = jnp.einsum("erd,erh->edh", received, d_pre, preferred_element_type=jnp.float32)
        d_received = jnp.einsum(
            "erh,edh->erd", d_pre, w_in[layer_index], preferred_element_type=jnp.float32
        ).astype(jnp.bfloat16)
        d_dispatched = lax.all_to_all(
            d_received, "exp", split_axis=1, concat_axis=0, tiled=True
        ).reshape(expert_count * capacity, model_width)
        d_from_experts = jnp.sum(
            d_dispatched[slot_index].astype(jnp.float32).reshape(tok_count, 2, model_width)
            * kept_pairs[:, :, None],
            axis=1,
        )
        route_ids = routes[layer_index]
        logits_pull = jax.vjp(lambda logit_values: router_gates(logit_values, route_ids), logits)[1]
        d_logits = logits_pull(d_gates)[0].astype(jnp.bfloat16)
        grad_router = jnp.einsum("td,te->de", moe_in, d_logits, preferred_element_type=jnp.float32)
        d_moe_in = (
            jnp.einsum(
                "te,de->td", d_logits, w_router[layer_index], preferred_element_type=jnp.float32
            )
            + d_from_experts
        )
        norm_pull = jax.vjp(layer_norm, middle, ln2_gain[layer_index], ln2_bias[layer_index])[1]
        d_norm_in, grad_gain_two, grad_bias_two = norm_pull(d_moe_in)
        d_middle = grad_state + d_norm_in
        d_branch = d_middle.astype(jnp.bfloat16)
        grad_attn_out = jnp.einsum(
            "td,te->de", attended, d_branch, preferred_element_type=jnp.float32
        )
        d_attended = jnp.einsum(
            "te,de->td", d_branch, w_attn_out[layer_index], preferred_element_type=jnp.float32
        ).astype(jnp.bfloat16)
        d_joined = attention_backward(joined, log_totals, d_attended, images)
        grad_qkv = jnp.einsum("td,te->de", normed, d_joined, preferred_element_type=jnp.float32)
        d_normed = jnp.einsum(
            "te,de->td", d_joined, w_qkv[layer_index], preferred_element_type=jnp.float32
        )
        norm_pull = jax.vjp(layer_norm, layer_in, ln1_gain[layer_index], ln1_bias[layer_index])[1]
        d_layer_in, grad_gain_one, grad_bias_one = norm_pull(d_normed)
        grad_state = d_middle + d_layer_in
        dense_terms = (
            grad_gain_one,
            grad_bias_one,
            grad_qkv,
            grad_attn_out,
            grad_gain_two,
            grad_bias_two,
            grad_router,
        )
        expert_terms = (grad_w_in, grad_w_out)
        dense_list.append(dense_terms)
        expert_list.append(expert_terms)
    dense_list = dense_list[::-1]
    expert_list = expert_list[::-1]
    dense_stack = tuple(
        (jnp.stack([term_set[member] for term_set in dense_list]) for member in range(7))
    )
    expert_stack = tuple(
        (jnp.stack([term_set[member] for term_set in expert_list]) for member in range(2))
    )
    dense_shares = jax.tree.map(
        lambda part: part.astype(jnp.float32),
        lax.psum_scatter(shortened(dense_stack), "exp", scatter_dimension=1, tiled=True),
    )
    dense_stack = jax.tree.map(
        lambda part: part.astype(jnp.float32), lax.psum(shortened(dense_shares), "rep")
    )
    expert_stack = jax.tree.map(
        lambda part: part.astype(jnp.float32),
        lax.psum_scatter(shortened(expert_stack), "rep", scatter_dimension=2, tiled=True),
    )
    grad_tokens = grad_state.reshape(images, seq_len, model_width)
    return (
        block_out,
        grad_tokens,
        dense_stack[0],
        dense_stack[1],
        dense_stack[2],
        dense_stack[3],
        dense_stack[4],
        dense_stack[5],
        dense_stack[6],
        expert_stack[0],
        expert_stack[1],
    )


def solution(mesh):
    return jax.shard_map(
        local,
        mesh=mesh,
        in_specs=(
            P(("rep", "exp"), None, None),
            P(),
            P(),
            P(),
            P(),
            P(),
            P(),
            P(),
            P(None, "exp", None, None),
            P(None, "exp", None, None),
            P(None, ("rep", "exp"), None),
            P(None, ("rep", "exp"), None),
            P(("rep", "exp"), None, None),
        ),
        out_specs=(
            P(("rep", "exp"), None, None),
            P(("rep", "exp"), None, None),
            P(None, "exp"),
            P(None, "exp"),
            P(None, "exp", None),
            P(None, "exp", None),
            P(None, "exp"),
            P(None, "exp"),
            P(None, "exp", None),
            P(None, "exp", "rep", None),
            P(None, "exp", "rep", None),
        ),
        check_vma=False,
    )
```

profile of v0, /device:TPU:0, one launch (start us, length us, event | category | flops | bytes accessed | tf_op | source)
XLA Modules:
  0.0 1300.8 jit_solution(13352833486442984690)
XLA Ops:
  12.5 8.8 scatter_custom_fusion
  92.5 8.8 scatter_custom_fusion.1
  112.8 10.2 fusion.50
  123.0 30.7 %multiply_convert_fusion.1 = (bf16[4,394,2048]{2,1,0:T(8,128)(2,1)}, f32[4,394,2048]{2,1,0:T(8,128)}) fusion(f32[4,394,2048]{2,1,0:T(8,128)S(1)} %get-tuple-element.160, u8[394,2048]{1,0:T(8,128)(4,1)S(1)} %get-tuple-element.81, u8[394,2048]{1,0:T(8,128)(4,1)S(1)} %get-tuple-element.80), kind=kLoop, calls=%fused_computation.44 | loop fusion | flops 225935360 | bytes 33890304 | tf_op jit(solution)/shard_map/convert_element_type | solution.py:157
  153.7 8.8 fusion.63
  183.3 15.3 %gather_fusion.8 = f32[1576]{0:T(1024)S(1)} fusion(f32[788,8]{0,1:T(8,128)S(1)} %fusion.133, s32[1576]{0:T(1024)S(1)} %reshape.777), kind=kCustom, calls=%fused_computation.clone | custom fusion | bytes 25216 | tf_op jit(solution)/shard_map/jit(take_along_axis)/gather | solution.py:45
  212.4 18.6 %multiply_reduce_fusion.9 = f32[788,512]{1,0:T(8,128)S(1)} fusion(f32[788,2,512]{2,1,0:T(2,128)S(1)} %reshape.654, f32[788,2]{1,0:T(8,128)} %select_select_fusion.1), kind=kLoop, calls=%fused_computation.125 | loop fusion | flops 1210368 | bytes 4847776 | tf_op jit(solution)/shard_map/reduce_sum | solution.py:167
  264.7 15.3 %gather_fusion.9 = f32[1576]{0:T(1024)S(1)} fusion(f32[788,8]{0,1:T(8,128)S(1)} %fusion.135, s32[1576]{0:T(1024)S(1)} %copy-done.6), kind=kCustom, calls=%fused_computation.1.clone | custom fusion | bytes 25216 | tf_op jit(solution)/shard_map/jit(take_along_axis)/gather | solution.py:45
  303.6 22.3 %all_to_all.132 = bf16[8,197,512]{2,1,0:T(8,128)(2,1)S(1)} all-to-all(bf16[8,197,512]{2,1,0:T(8,128)(2,1)S(1)} %get-tuple-element.154), channel_id=1, replica_groups=mesh['rep'=16,'exp'=2] {'exp'}, dimensions={0} | all-to-all | bytes 3227648 | tf_op jit(solution)/shard_map/all_to_all | solution.py:216
  336.2 11.5 all-to-all-done.2
  348.2 10.7 fusion.51
  359.0 30.7 %multiply_convert_fusion = (bf16[4,394,2048]{2,1,0:T(8,128)(2,1)}, f32[4,394,2048]{2,1,0:T(8,128)}) fusion(f32[4,394,2048]{2,1,0:T(8,128)S(1)} %get-tuple-element.169, u8[394,2048]{1,0:T(8,128)(4,1)S(1)} %get-tuple-element.79, u8[394,2048]{1,0:T(8,128)(4,1)S(1)} %get-tuple-element.78), kind=kLoop, calls=%fused_computation.31 | loop fusion | flops 225935360 | bytes 33890304 | tf_op jit(solution)/shard_map/convert_element_type | solution.py:157
  389.7 17.4 %add_convert_fusion.1 = bf16[4,394,2048]{2,1,0:T(8,128)(2,1)} fusion(f32[4,394,2048]{2,1,0:T(8,128)} %get-tuple-element.120, f32[4,394,2048]{2,1,0:T(8,128)} %copy-done.31, bf16[4,394,512]{2,1,0:T(8,128)(2,1)S(1)} %copy-done.61, bf16[2,4,2048,512]{3,2,1,0:T(8,128)(2,1)} %param.24), kind=kOutput, calls=%fused_computation.30 | convolution fusion | flops 3350298624 | bytes 42672128 | tf_op jit(solution)/shard_map/erd,ehd->erh/dot_general | solution.py:226
  407.1 8.8 fusion.66
  422.1 8.8 fusion.69
  473.2 11.3 multiply_reduce_fusion.7
  486.5 10.0 scatter_custom_fusion.2
  496.7 18.0 %multiply_reduce_fusion.6 = f32[788,512]{1,0:T(8,128)S(1)} fusion(f32[788,2,512]{2,1,0:T(2,128)} %reshape.656, f32[788,2]{1,0:T(8,128)} %convert_element_type.268), kind=kLoop, calls=%fused_computation.122 | loop fusion | flops 1210368 | bytes 4847776 | tf_op jit(solution)/shard_map/reduce_sum | solution.py:238
  588.4 10.2 scatter_custom_fusion.3
  600.7 17.6 %add_convert_fusion = bf16[4,394,2048]{2,1,0:T(8,128)(2,1)} fusion(f32[4,394,2048]{2,1,0:T(8,128)} %get-tuple-element.124, f32[4,394,2048]{2,1,0:T(8,128)} %copy-done.30, bf16[4,394,512]{2,1,0:T(8,128)(2,1)S(1)} %all_to_all.120, bf16[2,4,2048,512]{3,2,1,0:T(8,128)(2,1)} %param.24), kind=kOutput, calls=%fused_computation.29 | convolution fusion | flops 3350298624 | bytes 42672128 | tf_op jit(solution)/shard_map/erd,ehd->erh/dot_general | solution.py:226
  618.3 8.8 fusion.60
  661.9 17.6 %multiply_reduce_fusion.4 = f32[788,512]{1,0:T(8,128)S(1)} fusion(f32[788,2,512]{2,1,0:T(2,128)S(1)} %reshape.657, f32[788,2]{1,0:T(8,128)} %convert_element_type.281), kind=kLoop, calls=%fused_computation.120 | loop fusion | flops 1210368 | bytes 4847776 | tf_op jit(solution)/shard_map/reduce_sum | solution.py:238
  730.3 11.2 convert_bitcast_fusion
  741.4 20.3 %reduce-scatter.18.cloned.1.call-done = bf16[2,256,1536]{2,1,0:T(8,128)(2,1)} async-done(((bf16[2,512,1536]{2,1,0:T(8,128)(2,1)}), bf16[2,256,1536]{2,1,0:T(8,128)(2,1)}) %reduce-scatter.18.cloned.1.call-update) | async-done | bytes 1572880 | tf_op jit(solution)/shard_map/reduce_scatter | solution.py:293
  761.8 11.2 convert_bitcast_fusion.1
  773.0 13.8 %pad_maximum_fusion.1 = bf16[2,4,2048,512]{3,2,1,0:T(8,128)(2,1)} fusion(bf16[1,4,2048,512]{3,2,1,0:T(8,128)(2,1)} %convert_bitcast_fusion, bf16[1,4,2048,512]{3,2,1,0:T(8,128)(2,1)} %convert_bitcast_fusion.1), kind=kLoop, calls=%fused_computation.17 | loop fusion | flops 8388608 | bytes 33554432 | tf_op jit(solution)/shard_map/stack | solution.py:289
  795.1 9.7 convert_bitcast_fusion.3
  804.8 10.5 pad_maximum_fusion
  829.0 61.9 %all-reduce = (bf16[2,256]{1,0:T(2,128)(2,1)S(1)}, bf16[2,256]{1,0:T(2,128)(2,1)S(1)}, bf16[2,256]{1,0:T(2,128)(2,1)S(1)}, bf16[2,256]{1,0:T(2,128)(2,1)S(1)}, bf16[2,256,8]{1,2,0:T(8,128)(2,1)S(1)}) all-reduce(bf16[2,256]{1,0:T(2,128)(2,1)S(1)} %copy.344, bf16[2,256]{1,0:T(2,128)(2,1)S(1)} %copy.346, ...), channel_id=1, replica_groups=mesh['rep'=16,'exp'=2] {'rep'}, use_global_device_ids=true, to_apply=%region_43.45 | all-reduce | flops 6144 | bytes 24576 | tf_op jit(solution)/shard_map/psum | solution.py:296
  893.8 32.5 %all-reduce.4.cloned.1.call-done = (bf16[2,256,1536]{2,1,0:T(8,128)(2,1)}, bf16[2,256,512]{2,1,0:T(8,128)(2,1)}) async-done(((bf16[2,256,1536]{2,1,0:T(8,128)(2,1)}, bf16[2,256,512]{2,1,0:T(8,128)(2,1)}), (bf16[2,256,1536]{2,1,0:T(8,128)(2,1)}, bf16[2,256,512]{2,1,0:T(8,128)(2,1)})) %all-reduce.4.cloned.1.call-update) | async-done | bytes 2097168 | tf_op jit(solution)/shard_map/psum | solution.py:296
  931.8 177.0 %reduce-scatter.26.cloned.1.call-done = bf16[2,4,128,512]{3,2,1,0:T(8,128)(2,1)} async-done(((bf16[2,4,2048,512]{3,2,1,0:T(8,128)(2,1)}), bf16[2,4,128,512]{3,2,1,0:T(8,128)(2,1)}) %reduce-scatter.26.cloned.1.call-update) | async-done | bytes 1048592 | tf_op jit(solution)/shard_map/reduce_scatter | solution.py:300
  1111.7 179.3 %reduce-scatter.24.cloned.1.call-done = bf16[2,4,32,2048]{3,2,1,0:T(8,128)(2,1)} async-done(((bf16[2,4,512,2048]{3,2,1,0:T(8,128)(2,1)}), bf16[2,4,32,2048]{3,2,1,0:T(8,128)(2,1)}) %reduce-scatter.24.cloned.1.call-update) | async-done | bytes 1048592 | tf_op jit(solution)/shard_map/reduce_scatter | solution.py:300
  (585 shorter events, 436.3 us)
Async XLA Ops:
  8.2 93.1 %copy-start.36 = (s32[1,788,2]{2,1,0:T(8,128)}, s32[1,788,2]{2,1,0:T(8,128)S(1)}, u32[]{:S(2)}) copy-start(s32[1,788,2]{2,1,0:T(8,128)S(1)} %copy.362) | copy-start | bytes 18916
  25.4 48.2 %copy-start.109 = (f32[1,512]{1,0:T(1,128)}, f32[1,512]{1,0:T(1,128)S(1)}, u32[]{:S(2)}) copy-start(f32[1,512]{1,0:T(1,128)S(1)} %get-tuple-element.147) | copy-start | bytes 6148
  30.3 51.6 %copy-start.120 = (pred[8,197]{1,0:T(8,128)(4,1)}, pred[8,197]{1,0:T(8,128)(4,1)S(1)}, u32[]{:S(2)}) copy-start(pred[8,197]{1,0:T(8,128)(4,1)S(1)} %ge.20) | copy-start | bytes 4732
  33.9 36.4 %copy-start.28 = (f32[788,512]{1,0:T(8,128)}, f32[788,512]{1,0:T(8,128)S(1)}, u32[]{:S(2)}) copy-start(f32[788,512]{1,0:T(8,128)S(1)} %reshape.625) | copy-start | bytes 4841476
  83.3 26.5 %all-to-all-start = ((bf16[8,197,512]{2,1,0:T(8,128)(2,1)}), bf16[8,197,512]{2,1,0:T(8,128)(2,1)}, u32[]{:S(2)}, u32[]{:S(2)}) async-start(bf16[8,197,512]{2,1,0:T(8,128)(2,1)} %broadcast_select_fusion.1), calls=%async_computation | async-start | bytes 3276800 | tf_op jit(solution)/shard_map/all_to_all | solution.py:147
  122.9 30.8 %copy-start.30 = (f32[4,394,2048]{2,1,0:T(8,128)}, f32[4,394,2048]{2,1,0:T(8,128)S(1)}, u32[]{:S(2)}) copy-start(f32[4,394,2048]{2,1,0:T(8,128)S(1)} %get-tuple-element.160) | copy-start | bytes 38731780
  164.9 35.6 %all-to-all-start.1 = ((bf16[4,394,512]{2,0,1:T(4,128)(2,1)}), bf16[4,394,512]{2,0,1:T(4,128)(2,1)}, u32[]{:S(2)}, u32[]{:S(2)}) async-start(bf16[4,394,512]{2,0,1:T(4,128)(2,1)} %copy.283), calls=%async_computation.1 | async-start | bytes 3227648 | tf_op jit(solution)/shard_map/all_to_all | solution.py:161
  171.3 28.3 %copy-start.64 = (pred[788,2]{1,0:T(8,128)(4,1)}, pred[788,2]{1,0:T(8,128)(4,1)S(1)}, u32[]{:S(2)}) copy-start(pred[788,2]{1,0:T(8,128)(4,1)S(1)} %lt.159) | copy-start | bytes 4732
  263.1 28.6 %copy-start.2 = (bf16[788,512]{1,0:T(8,128)(2,1)}, bf16[788,512]{1,0:T(8,128)(2,1)S(1)}, u32[]{:S(2)}) copy-start(bf16[788,512]{1,0:T(8,128)(2,1)S(1)} %add_convert_fusion.2) | copy-start | bytes 2420740
  303.6 28.5 %copy-start.131 = (s32[2]{0:T(128)S(1)}, s32[2]{0:T(128)}, u32[]{:S(2)}) copy-start(s32[2]{0:T(128)} %constant.167) | copy-start | bytes 28
  325.9 21.8 %all-to-all-start.2 = ((bf16[8,197,512]{2,1,0:T(8,128)(2,1)}), bf16[8,197,512]{2,1,0:T(8,128)(2,1)S(1)}, u32[]{:S(2)}, u32[]{:S(2)}) async-start(bf16[8,197,512]{2,1,0:T(8,128)(2,1)} %get-tuple-element.155), calls=%async_computation.2 | async-start | bytes 3276800 | tf_op jit(solution)/shard_map/all_to_all | solution.py:147
  359.0 30.7 %copy-start.31 = (f32[4,394,2048]{2,1,0:T(8,128)}, f32[4,394,2048]{2,1,0:T(8,128)S(1)}, u32[]{:S(2)}) copy-start(f32[4,394,2048]{2,1,0:T(8,128)S(1)} %get-tuple-element.169) | copy-start | bytes 38731780
  359.0 30.7 %copy-start.61 = (bf16[4,394,512]{2,1,0:T(8,128)(2,1)S(1)}, bf16[4,394,512]{2,1,0:T(8,128)(2,1)}, u32[]{:S(2)}) copy-start(bf16[4,394,512]{2,1,0:T(8,128)(2,1)} %all_to_all.113) | copy-start | bytes 4841476
  418.4 20.6 %all-to-all-start.5 = ((bf16[4,394,512]{2,0,1:T(4,128)(2,1)}), bf16[4,394,512]{2,0,1:T(4,128)(2,1)S(1)}, u32[]{:S(2)}, u32[]{:S(2)}) async-start(bf16[4,394,512]{2,0,1:T(4,128)(2,1)} %copy.302), calls=%async_computation.5 | async-start | bytes 3227648 | tf_op jit(solution)/shard_map/all_to_all | solution.py:235
  439.0 20.9 %all-to-all-start.3 = ((bf16[4,394,512]{2,0,1:T(4,128)(2,1)}), bf16[4,394,512]{2,0,1:T(4,128)(2,1)}, u32[]{:S(2)}, u32[]{:S(2)}) async-start(bf16[4,394,512]{2,0,1:T(4,128)(2,1)} %copy.295), calls=%async_computation.3 | async-start | bytes 3227648 | tf_op jit(solution)/shard_map/all_to_all | solution.py:161
  484.5 30.3 %copy-start.11 = (f32[788,512]{1,0:T(8,128)S(1)}, f32[788,512]{1,0:T(8,128)}, u32[]{:S(2)}) copy-start(f32[788,512]{1,0:T(8,128)} %copy-done.10) | copy-start | bytes 4841476
  484.5 30.3 %copy-start.81 = (f32[788]{0:T(1024)S(1)}, f32[788]{0:T(1024)}, u32[]{:S(2)}) copy-start(f32[788]{0:T(1024)} %copy-done.80) | copy-start | bytes 9460
  484.5 30.3 %copy-start.91 = (f32[788]{0:T(1024)S(1)}, f32[788]{0:T(1024)}, u32[]{:S(2)}) copy-start(f32[788]{0:T(1024)} %copy-done.90) | copy-start | bytes 9460
  484.5 30.3 %copy-start.94 = (bf16[2,512,8]{1,2,0:T(8,128)(2,1)S(1)}, bf16[2,512,8]{1,2,0:T(8,128)(2,1)}, u32[]{:S(2)}) copy-start(bf16[2,512,8]{1,2,0:T(8,128)(2,1)} %param.22) | copy-start | bytes 49156
  484.5 30.3 %copy-start.112 = (f32[1,512]{1,0:T(1,128)S(1)}, f32[1,512]{1,0:T(1,128)}, u32[]{:S(2)}) copy-start(f32[1,512]{1,0:T(1,128)} %get-tuple-element.146) | copy-start | bytes 6148
  577.2 21.5 %all-to-all-start.6 = ((bf16[8,197,512]{2,1,0:T(8,128)(2,1)}), bf16[8,197,512]{2,1,0:T(8,128)(2,1)}, u32[]{:S(2)}, u32[]{:S(2)}) async-start(bf16[8,197,512]{2,1,0:T(8,128)(2,1)} %select_convert_fusion), calls=%async_computation.6 | async-start | bytes 3276800 | tf_op jit(solution)/shard_map/all_to_all | solution.py:216
  629.6 20.0 %all-to-all-start.7 = ((bf16[4,394,512]{2,0,1:T(4,128)(2,1)}), bf16[4,394,512]{2,0,1:T(4,128)(2,1)}, u32[]{:S(2)}, u32[]{:S(2)}) async-start(bf16[4,394,512]{2,0,1:T(4,128)(2,1)} %copy.315), calls=%async_computation.7 | async-start | bytes 3227648 | tf_op jit(solution)/shard_map/all_to_all | solution.py:235
  634.3 107.1 %reduce-scatter.20.cloned.1.call-start = ((), (), s32[]{:S(2)}) async-start(), calls=%async_computation.18 | async-start | bytes 1572864 | tf_op jit(solution)/shard_map/reduce_scatter | solution.py:293
  685.5 76.3 %reduce-scatter.18.cloned.1.call-start = ((), (), s32[]{:S(2)}) async-start(), calls=%async_computation.17 | async-start | bytes 4718592 | tf_op jit(solution)/shard_map/reduce_scatter | solution.py:293
  719.1 106.1 %reduce-scatter.34.cloned.1.call-start = ((), (), s32[]{:S(2)}) async-start(), calls=%async_computation.25 | async-start | bytes 196608
  721.3 104.8 %reduce-scatter.32.cloned.1.call-start = ((), (), s32[]{:S(2)}) async-start(), calls=%async_computation.24 | async-start | bytes 196608
  727.6 99.4 %reduce-scatter.30.cloned.1.call-start = ((), (), s32[]{:S(2)}) async-start(), calls=%async_computation.23 | async-start | bytes 196608
  728.5 99.5 %reduce-scatter.28.cloned.1.call-start = ((), (), s32[]{:S(2)}) async-start(), calls=%async_computation.22 | async-start | bytes 196608
  729.4 99.5 %reduce-scatter.22.cloned.1.call-start = ((), (), s32[]{:S(2)}) async-start(), calls=%async_computation.19 | async-start | bytes 24576 | tf_op jit(solution)/shard_map/reduce_scatter | solution.py:293
  730.2 196.0 %all-reduce.4.cloned.1.call-start = ((), (), s32[]{:S(2)}) async-start(), calls=%async_computation.26 | async-start | bytes 4194304 | tf_op jit(solution)/shard_map/psum | solution.py:296
  761.8 347.1 %reduce-scatter.26.cloned.1.call-start = ((), (), s32[]{:S(2)}) async-start(), calls=%async_computation.21 | async-start | bytes 17825792 | tf_op jit(solution)/shard_map/reduce_scatter | solution.py:300
  786.8 504.2 %reduce-scatter.24.cloned.1.call-start = ((), (), s32[]{:S(2)}) async-start(), calls=%async_computation.20 | async-start | bytes 17825792 | tf_op jit(solution)/shard_map/reduce_scatter | solution.py:300
  (123 other events, 836.6 us)
Sparse Core Ops, SparseCore 0:
  685.6 19.2 reduce-scatter.19
  719.2 42.4 reduce-scatter.17
  764.0 10.2 reduce-scatter.33
  776.3 10.2 reduce-scatter.31
  788.6 10.2 reduce-scatter.29
  801.6 10.2 reduce-scatter.27
  814.6 9.7 reduce-scatter.21
  828.1 98.1 all-reduce.3
  930.9 177.9 reduce-scatter.25
  1113.4 177.5 reduce-scatter.23
where the time goes:
time: 1310 us; the launch traced here: 1300 us
  waiting for transfers between devices  444 us (34%)
  local copies, waits for them, and re-layouts  287 us (22%)
  other arithmetic  239 us (18%)
  matrix products  197 us (15%)
  blocking collectives  84.1 us (6%)
  starting transfers between devices  31.9 us (2%)
  between operations  16.9 us (1%)
    reduce_scatter x2, waiting for transfers between devices, local(): lax.psum_scatter(shortened(expert_stack), 'rep', scatter_dimension=2, til...  356 us
    psum x1, blocking collectives, local(): lax.psum(shortened(dense_shares), 'rep')  61.9 us
    convert_element_type x2, other arithmetic, local(): activated = jax.nn.gelu(pre_act, approximate=False).astype(jnp.bfloat16)  61.5 us
    unnamed x302, local copies, waits for them, and re-layouts  47.7 us
    reduce_sum x2, other arithmetic, local(): jnp.sum(d_dispatched[slot_index].astype(jnp.float32).reshape(tok_count, 2...  35.6 us
    dot_general x2, matrix products, local(): jnp.einsum('erd,ehd->erh', d_produced, w_out[layer_index], preferred_elem...  34.9 us
    psum x1, waiting for transfers between devices, local(): lax.psum(shortened(dense_shares), 'rep')  32.5 us
    gather x6, local copies, waits for them, and re-layouts, router_gates(): jnp.take_along_axis(jax.nn.softmax(logit_values, axis=-1), route_ids, axi...  32.4 us
  transfers between devices with their start and end apart: 17, of which 9 were waited for; matrix products, arithmetic and copies ran while one was open for 18% of the time, Pallas kernels for 0%

commit v1 on v0

v1 whole, which is shorter than its diff:
```python
from functools import partial

import jax
import jax.numpy as jnp
from jax import lax
from jax.experimental import pallas as pl
from jax.experimental.pallas import tpu as pltpu
from jax.sharding import PartitionSpec as P

HEADS = 8
HEAD_DIM = 64
EPSILON = 1e-06
LANES = 128
WIDE = 256
F32 = jnp.float32
BF16 = jnp.bfloat16
VMEM_LIMIT = 60 * 1024 * 1024


def round_up(value, multiple):
    return -(-value // multiple) * multiple


def nn(a, b):
    return lax.dot_general(a, b, (((1,), (0,)), ((), ())), preferred_element_type=F32)


def nt(a, b):
    return lax.dot_general(a, b, (((1,), (1,)), ((), ())), preferred_element_type=F32)


def tn(a, b):
    return lax.dot_general(a, b, (((0,), (0,)), ((), ())), preferred_element_type=F32)


def iota(shape, dim):
    return lax.broadcasted_iota(jnp.int32, shape, dim)


def row_to_col(row, rows):
    shape = (rows, row.shape[1])
    return jnp.sum(jnp.where(iota(shape, 0) == iota(shape, 1), row, 0.0), axis=1, keepdims=True)


def col_to_row(col, lanes):
    shape = (col.shape[0], lanes)
    return jnp.sum(jnp.where(iota(shape, 0) == iota(shape, 1), col, 0.0), axis=0, keepdims=True)


def normalized(values):
    average = jnp.mean(values, axis=-1, keepdims=True)
    centred = values - average
    spread = jnp.mean(centred * centred, axis=-1, keepdims=True)
    factor = lax.rsqrt(spread + EPSILON)
    return centred * factor, factor


def norm_back(grad, gain, xhat, factor):
    scaled = grad * gain
    mean_e = jnp.mean(scaled, axis=-1, keepdims=True)
    mean_x = jnp.mean(scaled * xhat, axis=-1, keepdims=True)
    return factor * (scaled - mean_e - xhat * mean_x)


def gelu_both(x):
    z = x * 0.7071067811865476
    size = jnp.abs(z)
    denom = 1.0 + 0.3275911 * size
    guess = pl.reciprocal(denom, approx=True)
    t = guess * (2.0 - denom * guess)
    raised = jnp.exp(-(z * z))
    poly = t * (
        0.127414796
        + t * (-0.142248368 + t * (0.7107068705 + t * (-0.7265760135 + t * 0.5307027145)))
    )
    tail = poly * raised
    phi = jnp.where(x >= 0.0, 1.0 - tail, tail)
    return x * phi, phi + x * raised * 0.3989422804014327


def route_kernel(ids, r_ref, p_ref, row_ref, col_ref, tall, wide, *, n, per, cap, cp, images, seq):
    tokens = images * seq
    bits = (2 * tokens - 1).bit_length()
    me = ids[0]
    key = (r_ref[0] << bits) + p_ref[0]
    tall[...] = jnp.full(tall.shape, -1, jnp.int32)
    tall[0:tokens, 0:2] = key
    flipped = tall[...].T
    lanes = tall.shape[0]
    slots = []
    experts = []
    for k in range(2):
        mine = flipped[k : k + 1, :]
        expert = mine >> bits
        least = expert << bits
        count = jnp.zeros((1, lanes), jnp.int32)
        for other in range(2):
            theirs = key[:, other : other + 1]
            hit = jnp.logical_and(theirs >= least, theirs < mine)
            count = count + jnp.sum(jnp.where(hit, 1, 0), axis=0, keepdims=True)
        group = jnp.zeros((1, lanes), jnp.int32)
        for q in range(1, n):
            group = group + jnp.where(expert >= q * per, 1, 0)
        ahead = group - me
        ahead = jnp.where(ahead < 0, ahead + n, ahead)
        slot = (ahead * per + (expert - group * per)) * cp + count
        kept = count < cap
        slots.append(jnp.where(kept, slot, -1))
        experts.append(jnp.where(kept, expert, -1))
    table = jnp.concatenate(slots + experts + [jnp.full((4, lanes), -1, jnp.int32)], axis=0)
    sp = col_ref.shape[2]
    for i in range(images):
        moved = table if i == 0 else pltpu.roll(table, lanes - seq * i, axis=1)
        piece = moved[:, :WIDE]
        piece = jnp.where(iota(piece.shape, 1) < seq, piece, -1)
        row_ref[0, :, i * WIDE : (i + 1) * WIDE] = piece
        wide[0:8, :] = piece
        col_ref[0, i] = wide[...].T[0:sp, :]


def spread_rows(me, row_ref, rhs, outs, n, per, cp, width, experts):
    slots0 = row_ref[0, 0:1, :]
    slots1 = row_ref[0, 1:2, :]
    shape = (per * cp, row_ref.shape[2])
    for d in list(range(1, n)) + [0]:
        place = iota(shape, 0) + d * per * cp
        pick = jnp.where(jnp.logical_or(place == slots0, place == slots1), 1.0, 0.0).astype(BF16)
        rows = nn(pick, rhs[...])
        base = lax.rem(me + d, n) * per
        for j in range(per):
            part = rows[j * cp : (j + 1) * cp, :]
            data = part[:, :width]
            if experts:
                both = part[:, width : width + LANES] + part[:, width + LANES :]
                gate = jnp.sum(
                    jnp.where(iota(both.shape, 1) == base + j, both, 0.0), axis=1, keepdims=True
                )
                line = col_to_row(gate, width)
                high = line.astype(BF16).astype(F32)
                where = iota(data.shape, 0)
                data = jnp.where(where == cp - 1, high, data)
                data = jnp.where(where == cp - 2, line - high, data)
            outs[d][j][...] = data.astype(BF16)


def gathered(c0, c1, v0, v1, back, n, per, cp):
    shape = (c0.shape[0], cp)
    place = iota(shape, 1)
    total = None
    for d in range(n):
        for j in range(per):
            base = (d * per + j) * cp
            pick = jnp.where(c0 - base == place, v0, 0.0) + jnp.where(c1 - base == place, v1, 0.0)
            term = nn(pick.astype(BF16), back[d][j][...])
            total = term if total is None else total + term
    return total


def take(it, n, per):
    return [[next(it) for _ in range(per)] for _ in range(n)]


def head_masks():
    lane = iota((1, LANES), 1)
    low = jnp.where(lane < HEAD_DIM, 1.0, 0.0).astype(BF16)
    high = jnp.where(lane < HEAD_DIM, 0.0, 1.0).astype(BF16)
    return low, high


def forward_kernel(*refs, first, layer, n, per, cp, images, seq, experts):
    it = iter(refs)
    ids = next(it)
    if first:
        x_ref = next(it)
    else:
        mid_in, gate_in, col_in = next(it), next(it), next(it)
        back = take(it, n, per)
    g1, b1, wqkv, wo, g2, b2, wr, col, row = (next(it) for _ in range(9))
    if not first:
        state_out = next(it)
    joined_out, probs_out, attended_out, middle_out, moe_out, rp_out, gate_out = (
        next(it) for _ in range(7)
    )
    disp = take(it, n, per)
    rhs = next(it)
    i = pl.program_id(0)
    sp = middle_out.shape[1]
    width = middle_out.shape[2]

    @pl.when(i == 0)
    def _():
        rhs[...] = jnp.zeros(rhs.shape, BF16)

    if first:
        xs = next(it)

        @pl.when(i == 0)
        def _():
            xs[...] = jnp.zeros(xs.shape, F32)

        xs[0:seq, :] = x_ref[0]
        state = xs[...]
    else:
        state = mid_in[0] + gathered(
            col_in[0, 0, :, 0:1],
            col_in[0, 0, :, 1:2],
            gate_in[0, :, 0:1],
            gate_in[0, :, 1:2],
            back,
            n,
            per,
            cp,
        )
        state_out[0] = state
    xhat, _ = normalized(state)
    normed = (xhat * g1[layer : layer + 1, :] + b1[layer : layer + 1, :]).astype(BF16)
    joined = nn(normed, wqkv[0]).astype(BF16)
    joined_out[0] = joined
    masks = head_masks()
    valid = iota((1, sp), 1) < seq
    pieces = []
    for pair in range(HEADS // 2):
        at = pair * LANES
        q = joined[:, at : at + LANES]
        k = joined[:, width + at : width + at + LANES]
        v = joined[:, 2 * width + at : 2 * width + at + LANES]
        mixed = None
        for half in range(2):
            scores = jnp.where(valid, nt(q, k * masks[half]), -1e30)
            top = jnp.max(scores, axis=-1, keepdims=True)
            raised = jnp.exp((scores - top) * HEAD_DIM ** (-0.5))
            total = jnp.sum(raised, axis=-1, keepdims=True)
            probs = (raised * (1.0 / total)).astype(BF16)
            probs_out[0, 2 * pair + half] = probs
            term = nn(probs, v * masks[half])
            mixed = term if mixed is None else mixed + term
        pieces.append(mixed.astype(BF16))
    attended = jnp.concatenate(pieces, axis=1)
    attended_out[0] = attended
    middle = state + nn(attended, wo[0])
    middle_out[0] = middle
    xhat, _ = normalized(middle)
    moe_in = (xhat * g2[layer : layer + 1, :] + b2[layer : layer + 1, :]).astype(BF16)
    moe_out[0] = moe_in
    logits = nn(moe_in, wr[0])
    lane = iota(logits.shape, 1)
    logits = jnp.where(lane < experts, logits, -1e30)
    raised = jnp.exp(logits - jnp.max(logits, axis=-1, keepdims=True))
    router = raised * (1.0 / jnp.sum(raised, axis=-1, keepdims=True))
    rp_out[0] = router
    gates = []
    for k in range(2):
        chosen = col[0, 0, :, 2 + k : 3 + k]
        gates.append(jnp.sum(jnp.where(lane == chosen, router, 0.0), axis=1, keepdims=True))
    gate_out[0] = jnp.where(lane == 0, gates[0], jnp.where(lane == 1, gates[1], 0.0))
    high = router.astype(BF16)
    low = (router - high.astype(F32)).astype(BF16)
    at = pl.multiple_of(i * WIDE, WIDE)
    rhs[pl.ds(at, sp), 0:width] = moe_in
    rhs[pl.ds(at, sp), width : width + LANES] = high
    rhs[pl.ds(at, sp), width + LANES : width + 2 * LANES] = low

    @pl.when(i == images - 1)
    def _():
        spread_rows(ids[0], row, rhs, disp, n, per, cp, width, experts)


def cotangent_kernel(*refs, n, per, cp, images, seq):
    it = iter(refs)
    ids, g_ref, row = next(it), next(it), next(it)
    outs = take(it, n, per)
    rhs = next(it)
    rhs[...] = jnp.zeros(rhs.shape, BF16)
    for i in range(images):
        rhs[i * WIDE : i * WIDE + seq, :] = g_ref[i].astype(BF16)
    spread_rows(ids[0], row, rhs, outs, n, per, cp, rhs.shape[1], 0)


def out_kernel(*refs, n, per, cp, seq):
    it = iter(refs)
    mid, gate, col = next(it), next(it), next(it)
    back = take(it, n, per)
    out = next(it)
    state = mid[0] + gathered(
        col[0, 0, :, 0:1], col[0, 0, :, 1:2], gate[0, :, 0:1], gate[0, :, 1:2], back, n, per, cp
    )
    out[0] = state[0:seq, :]


def expert_kernel(*refs, n, cp, tiles, forward, backward, sizes):
    it = iter(refs)
    ids = next(it)
    xs = [next(it) for _ in range(n)]
    if backward:
        gs = [next(it) for _ in range(n)]
        if not forward:
            made = [next(it) for _ in range(n)]
            act_in, slope_in = next(it), next(it)
    w_in, w_out = next(it), next(it)
    if forward:
        prod = [next(it) for _ in range(n)]
        if not backward:
            act_out, slope_out = next(it), next(it)
    if backward:
        dx = [next(it) for _ in range(n)]
        wire = next(it)
    xcat = next(it)
    if forward:
        acc_p = next(it)
    if backward:
        dprod, acc_d = next(it), next(it)
    h = pl.program_id(0)
    width = xcat.shape[1]

    @pl.when(h == 0)
    def _():
        for d in range(n):
            xcat[d * cp : (d + 1) * cp, :] = xs[d][...]
            if backward:
                tail = xs[d][cp - 16 : cp, 0:WIDE].astype(F32)
                line = jnp.sum(jnp.where(iota(tail.shape, 0) >= 14, tail, 0.0), axis=0, keepdims=True)
                gate = row_to_col(line, cp)
                dprod[d * cp : (d + 1) * cp, :] = (gate * gs[d][...].astype(F32)).astype(BF16)

    if forward:
        pre = nn(xcat[...], w_in[0, 0])
        value, slope = gelu_both(pre)
        act = value.astype(BF16)
        if not backward:
            act_out[...] = act
            slope_out[...] = slope.astype(BF16)
        term = nn(act, w_out[0, 0])

        @pl.when(h == 0)
        def _():
            acc_p[...] = term

        @pl.when(h > 0)
        def _():
            acc_p[...] += term
    else:
        act = act_in[...]
        slope = slope_in[...].astype(F32)
    if backward:
        zs, xs_, cores, rows_in, rows_out = sizes
        core = ids[1]
        d_act = nt(dprod[...], w_out[0, 0])
        d_pre = (d_act * slope).astype(BF16)
        grad_out = tn(act, dprod[...]).astype(BF16)
        for x in range(xs_):
            for c in range(cores):
                at = (x * cores + c) * rows_out
                wire[lax.rem(c + core, cores), x, h, tiles * rows_in :, :] = grad_out[
                    at : at + rows_out, :
                ]
        grad_in = tn(xcat[...], d_pre).astype(BF16)
        spot = pl.multiple_of(h * rows_in, rows_in)
        for z in range(zs):
            for x in range(xs_):
                for c in range(cores):
                    at = ((z * xs_ + x) * cores + c) * rows_in
                    wire[lax.rem(c + core, cores), x, z, pl.ds(spot, rows_in), :] = grad_in[
                        at : at + rows_in, :
                    ]
        term_d = nt(d_pre, w_in[0, 0])

        @pl.when(h == 0)
        def _():
            acc_d[...] = term_d

        @pl.when(h > 0)
        def _():
            acc_d[...] += term_d

    @pl.when(h == tiles - 1)
    def _():
        for d in range(n):
            rows = pl.ds(d * cp, cp)
            if forward:
                result = acc_p[rows, :].astype(BF16)
                prod[d][...] = result
            if backward:
                if not forward:
                    result = made[d][...]
                d_gate = jnp.sum(
                    result.astype(F32) * gs[d][...].astype(F32), axis=1, keepdims=True
                )
                line = col_to_row(d_gate, width)
                data = acc_d[rows, :]
                dx[d][...] = jnp.where(iota(data.shape, 0) == cp - 1, line, data).astype(BF16)


def backward_kernel(*refs, first, last, layer, n, per, cp, images, seq, experts):
    it = iter(refs)
    ids, g_ref, s_ref = next(it), next(it), next(it)
    joined_in, probs_in, attended_in, middle_in, moe_in, rp_in, col = (next(it) for _ in range(7))
    back = take(it, n, per)
    g1, b1, wqkv, wo, g2, wr = (next(it) for _ in range(6))
    if not first:
        row = next(it)
    g_out, dense = next(it), next(it)
    if not first:
        outs = take(it, n, per)
    d_cols, a_qkv, a_out, a_router, stats, flip, d_join = (next(it) for _ in range(7))
    if last:
        g_pad = next(it)
    if first:
        s_pad = next(it)
    else:
        rhs = next(it)
    i = pl.program_id(0)
    sp = middle_in.shape[1]
    width = middle_in.shape[2]
    me = ids[0]

    @pl.when(i == 0)
    def _():
        a_qkv[...] = jnp.zeros(a_qkv.shape, F32)
        a_out[...] = jnp.zeros(a_out.shape, F32)
        a_router[...] = jnp.zeros(a_router.shape, F32)
        stats[...] = jnp.zeros(stats.shape, F32)
        flip[...] = jnp.zeros(flip.shape, F32)
        if last:
            g_pad[...] = jnp.zeros(g_pad.shape, F32)
        if first:
            s_pad[...] = jnp.zeros(s_pad.shape, F32)
        else:
            rhs[...] = jnp.zeros(rhs.shape, BF16)
        for d in range(n):
            base = lax.rem(me + d, n) * per
            for j in range(per):
                tail = back[d][j][cp - 16 : cp, 0:WIDE].astype(F32)
                line = jnp.sum(jnp.where(iota(tail.shape, 0) == 15, tail, 0.0), axis=0, keepdims=True)
                column = row_to_col(line, cp)
                d_cols[d, j] = jnp.where(iota((cp, LANES), 1) == base + j, column, 0.0).astype(BF16)

    if last:
        g_pad[0:seq, :] = g_ref[0]
        g = g_pad[...]
    else:
        g = g_ref[0]
    if first:
        s_pad[0:seq, :] = s_ref[0]
        state = s_pad[...]
    else:
        state = s_ref[0]

    c0 = col[0, 0, :, 0:1]
    c1 = col[0, 0, :, 1:2]
    place = iota((sp, cp), 1)
    d_moe = None
    d_rp = None
    for d in range(n):
        for j in range(per):
            base = (d * per + j) * cp
            pick = jnp.where(jnp.logical_or(c0 - base == place, c1 - base == place), 1.0, 0.0)
            pick = pick.astype(BF16)
            term = nn(pick, back[d][j][...])
            small = nn(pick, d_cols[d, j])
            d_moe = term if d_moe is None else d_moe + term
            d_rp = small if d_rp is None else d_rp + small
    router = rp_in[0]
    d_logits = router * (d_rp - jnp.sum(d_rp * router, axis=-1, keepdims=True))
    d_logits = d_logits.astype(BF16)
    a_router[...] += tn(moe_in[0], d_logits)
    d_moe = d_moe + nt(d_logits, wr[0])
    xhat, factor = normalized(middle_in[0])
    stats[2:3, :] += jnp.sum(d_moe * xhat, axis=0, keepdims=True)
    stats[3:4, :] += jnp.sum(d_moe, axis=0, keepdims=True)
    d_middle = g + norm_back(d_moe, g2[layer : layer + 1, :], xhat, factor)
    d_branch = d_middle.astype(BF16)
    a_out[...] += tn(attended_in[0], d_branch)
    d_att = nt(d_branch, wo[0]).astype(BF16)
    masks = head_masks()
    scale = HEAD_DIM ** (-0.5)
    for pair in range(HEADS // 2):
        at = pair * LANES
        q = joined_in[0, :, at : at + LANES]
        k = joined_in[0, :, width + at : width + at + LANES]
        v = joined_in[0, :, 2 * width + at : 2 * width + at + LANES]
        do = d_att[:, at : at + LANES]
        dq = dk = dv = None
        for half in range(2):
            low = probs_in[0, 2 * pair + half]
            probs = low.astype(F32)
            dp = nt(do, v * masks[half])
            ds = (probs * (dp - jnp.sum(dp * probs, axis=-1, keepdims=True))).astype(BF16)
            terms = (
                nn(ds, k * masks[half]),
                tn(ds, q * masks[half]),
                tn(low, do * masks[half]),
            )
            if half == 0:
                dq, dk, dv = terms
            else:
                dq, dk, dv = dq + terms[0], dk + terms[1], dv + terms[2]
        d_join[:, at : at + LANES] = (dq * scale).astype(BF16)
        d_join[:, width + at : width + at + LANES] = (dk * scale).astype(BF16)
        d_join[:, 2 * width + at : 2 * width + at + LANES] = dv.astype(BF16)
    xhat, factor = normalized(state)
    normed = (xhat * g1[layer : layer + 1, :] + b1[layer : layer + 1, :]).astype(BF16)
    a_qkv[...] += tn(normed, d_join[...])
    d_normed = nt(d_join[...], wqkv[0])
    stats[0:1, :] += jnp.sum(d_normed * xhat, axis=0, keepdims=True)
    stats[1:2, :] += jnp.sum(d_normed, axis=0, keepdims=True)
    result = d_middle + norm_back(d_normed, g1[layer : layer + 1, :], xhat, factor)
    if first:
        g_out[0] = result[0:seq, :]
    else:
        g_out[0] = result
        rhs[pl.ds(pl.multiple_of(i * WIDE, WIDE), sp), :] = result.astype(BF16)

    @pl.when(i == images - 1)
    def _():
        if not first:
            spread_rows(me, row, rhs, outs, n, per, cp, width, 0)
        flip[experts : experts + 8, :] = stats[...]
        dense[:, 0 : 3 * width] = a_qkv[...].astype(BF16)
        dense[:, 3 * width : 4 * width] = a_out[...].astype(BF16)
        dense[:, 4 * width :] = (a_router[...] + flip[...].T).astype(BF16)


def spec(shape, index):
    return pl.BlockSpec(shape, index)


def whole(array):
    zeros = (0,) * len(array.shape)
    return pl.BlockSpec(tuple(array.shape), lambda *_: zeros)


def smem():
    return pl.BlockSpec(memory_space=pltpu.SMEM)


def shape_of(shape, dtype):
    return jax.ShapeDtypeStruct(tuple(shape), dtype)


def cost(flops, moved, special=0):
    return pl.CostEstimate(flops=int(flops), bytes_accessed=int(moved), transcendentals=int(special))


def per_image(shape):
    rest = (0,) * (len(shape) - 1)
    return pl.BlockSpec((1,) + tuple(shape[1:]), lambda i: (i,) + rest)


def of_layer(array, layer):
    rest = (0,) * (len(array.shape) - 1)
    return pl.BlockSpec((1,) + tuple(array.shape[1:]), lambda *_: (layer,) + rest)


def pairs_along(stride, length, total, valid, step):
    pairs = []
    for source in range(total):
        spot = (source // stride) % length
        target = spot + step
        if 0 <= target < length and valid(spot):
            pairs.append((source, source + step * stride))
    return pairs


def line_sum(parts, axis, stride, length, total, spot):
    def part(at):
        return lax.dynamic_index_in_dim(parts, jnp.clip(at, 0, length - 1), 0, keepdims=False).astype(
            F32
        )

    if length == 2:
        swap = pairs_along(stride, length, total, lambda s: True, 1) + pairs_along(
            stride, length, total, lambda s: True, -1
        )
        got = lax.ppermute(part(1 - spot).astype(BF16), axis, swap)
        return part(spot) + got.astype(F32)
    rising = part(length - 1 + spot)
    falling = part(1 - length + spot)
    for step in range(1, length):
        up = pairs_along(stride, length, total, lambda s: s <= step - 1, 1)
        down = pairs_along(stride, length, total, lambda s: length - 1 - s <= step - 1, -1)
        got_up = lax.ppermute(rising.astype(BF16), axis, up).astype(F32)
        got_down = lax.ppermute(falling.astype(BF16), axis, down).astype(F32)
        if step < length - 1:
            rising = got_up + part(length - step - 1 + spot)
            falling = got_down + part(step + 1 - length + spot)
    return part(spot) + got_up + got_down


def expert_sum(wire, rep_sizes):
    zs, xs, cores = rep_sizes
    total = zs * xs * cores
    index = lax.axis_index("rep")
    core_swap = [(r, r ^ 1) for r in range(total)]
    got = lax.ppermute(wire[1], "rep", core_swap)
    both = (wire[0].astype(F32) + got.astype(F32)).astype(BF16)
    along_x = line_sum(both, "rep", cores, xs, total, (index // cores) % xs).astype(BF16)
    return line_sum(along_x, "rep", cores * xs, zs, total, index // (cores * xs))


def local(
    tokens,
    ln1_gain,
    ln1_bias,
    w_qkv,
    w_attn_out,
    ln2_gain,
    ln2_bias,
    w_router,
    w_in,
    w_out,
    routes,
    priority,
    cotangent,
    n,
    reps,
):
    images, seq, width = tokens.shape
    tok_count = images * seq
    layers, per, _, hidden = w_in.shape
    experts = n * per
    cap = 2 * tok_count // experts
    cp = round_up(cap + 2, 16)
    sp = round_up(seq, 16)
    zs, cores = 4, 2
    xs = reps // (zs * cores)
    rep_sizes = (zs, xs, cores)
    tiles = zs
    tile = hidden // tiles
    rows_in = width // reps
    rows_out = hidden // reps
    rows = tiles * rows_in + rows_out
    me = lax.axis_index("exp")
    core = lax.axis_index("rep") % cores
    ids = jnp.stack([me, core]).astype(jnp.int32)
    router_wide = jnp.pad(w_router, ((0, 0), (0, 0), (0, LANES - experts)))
    params = pltpu.CompilerParams(
        vmem_limit_bytes=VMEM_LIMIT, dimension_semantics=("arbitrary",)
    )
    dims = dict(n=n, per=per, cp=cp)

    lanes = round_up(tok_count, LANES)
    row, col = pl.pallas_call(
        partial(route_kernel, cap=cap, images=images, seq=seq, **dims),
        grid=(layers,),
        in_specs=[smem()] + [spec((1, tok_count, 2), lambda l: (l, 0, 0))] * 2,
        out_specs=[
            spec((1, 8, images * WIDE), lambda l: (l, 0, 0)),
            spec((1, images, sp, LANES), lambda l: (l, 0, 0, 0)),
        ],
        out_shape=[
            shape_of((layers, 8, images * WIDE), jnp.int32),
            shape_of((layers, images, sp, LANES), jnp.int32),
        ],
        scratch_shapes=[pltpu.VMEM((lanes, LANES), jnp.int32), pltpu.VMEM((LANES, WIDE), jnp.int32)],
        compiler_params=params,
        cost_estimate=cost(4e7, 1e6),
        name="route",
    )(ids, routes, priority)

    slot_shape = shape_of((cp, width), BF16)
    slot_shapes = [slot_shape] * (n * per)
    slot_specs = [whole(slot_shape)] * (n * per)

    def nested(flat):
        return [list(flat[d * per : (d + 1) * per]) for d in range(n)]

    def flat_of(lists):
        return [part for group in lists for part in group]

    def send(lists):
        result = [lists[0]]
        for d in range(1, n):
            pairs = [(s, (s + d) % n) for s in range(n)]
            result.append([lax.ppermute(part, "exp", pairs) for part in lists[d]])
        return result

    def send_back(lists):
        result = [lists[0]]
        for d in range(1, n):
            pairs = [(s, (s - d) % n) for s in range(n)]
            result.append([lax.ppermute(part, "exp", pairs) for part in lists[d]])
        return result

    def col_spec(layer):
        return spec((1, 1, sp, LANES), lambda i: (layer, i, 0, 0))

    row_spec_of = lambda layer: spec((1, 8, images * WIDE), lambda *_: (layer, 0, 0))

    top = layers - 1
    g_rows = nested(
        pl.pallas_call(
            partial(cotangent_kernel, images=images, seq=seq, **dims),
            grid=(1,),
            in_specs=[smem(), whole(cotangent), row_spec_of(top)],
            out_specs=slot_specs,
            out_shape=slot_shapes,
            scratch_shapes=[pltpu.VMEM((images * WIDE, width), BF16)],
            compiler_params=params,
            cost_estimate=cost(4 * n * per * cp * images * WIDE * width // 2, 4e6),
            name="spread_cotangent",
        )(ids, cotangent, row)
    )
    g_rows = send(g_rows)

    def run_forward(layer, previous):
        first = layer == 0
        args = [ids]
        specs = [smem()]
        if first:
            args += [tokens]
            specs += [per_image(tokens.shape)]
        else:
            middle, gate, back = previous
            args += [middle, gate, col] + flat_of(back)
            specs += [per_image(middle.shape), per_image(gate.shape), col_spec(layer - 1)] + slot_specs
        args += [ln1_gain, ln1_bias, w_qkv, w_attn_out, ln2_gain, ln2_bias, router_wide, col, row]
        specs += [
            whole(ln1_gain),
            whole(ln1_bias),
            of_layer(w_qkv, layer),
            of_layer(w_attn_out, layer),
            whole(ln2_gain),
            whole(ln2_bias),
            of_layer(router_wide, layer),
            col_spec(layer),
            row_spec_of(layer),
        ]
        shapes = [] if first else [shape_of((images, sp, width), F32)]
        shapes += [
            shape_of((images, sp, 3 * width), BF16),
            shape_of((images, HEADS, sp, sp), BF16),
            shape_of((images, sp, width), BF16),
            shape_of((images, sp, width), F32),
            shape_of((images, sp, width), BF16),
            shape_of((images, sp, LANES), F32),
            shape_of((images, sp, LANES), F32),
        ]
        out_specs = [per_image(s.shape) for s in shapes] + slot_specs
        scratch = [pltpu.VMEM((images * WIDE, width + 2 * LANES), BF16)]
        if first:
            scratch.append(pltpu.VMEM((sp, width), F32))
        out = pl.pallas_call(
            partial(
                forward_kernel,
                first=first,
                layer=layer,
                images=images,
                seq=seq,
                experts=experts,
                **dims,
            ),
            grid=(images,),
            in_specs=specs,
            out_specs=out_specs,
            out_shape=shapes + slot_shapes,
            scratch_shapes=scratch,
            compiler_params=params,
            cost_estimate=cost(6e9, 2e7, 1e6),
            name="forward",
        )(*args)
        out = list(out)
        state = tokens if first else out.pop(0)
        return state, out[:7], nested(out[7:])

    act_shape = shape_of((n * cp, hidden), BF16)
    wire_shape = shape_of((cores, xs, zs, rows, width), BF16)

    def run_expert(layer, j, x, g, saved, forward, backward):
        args = [ids] + [x[d][j] for d in range(n)]
        specs = [smem()] + [whole(slot_shape)] * n
        tile_spec = spec((n * cp, tile), lambda h: (0, h))
        if backward:
            args += [g[d][j] for d in range(n)]
            specs += [whole(slot_shape)] * n
            if not forward:
                made, act, slope = saved
                args += list(made) + [act, slope]
                specs += [whole(slot_shape)] * n + [tile_spec] * 2
        args += [w_in, w_out]
        specs += [
            spec((1, 1, width, tile), lambda h: (layer, j, 0, h)),
            spec((1, 1, tile, width), lambda h: (layer, j, h, 0)),
        ]
        shapes = []
        out_specs = []
        scratch = [pltpu.VMEM((n * cp, width), BF16)]
        if forward:
            shapes += [slot_shape] * n
            out_specs += [whole(slot_shape)] * n
            if not backward:
                shapes += [act_shape] * 2
                out_specs += [tile_spec] * 2
            scratch += [pltpu.VMEM((n * cp, width), F32)]
        if backward:
            shapes += [slot_shape] * n + [wire_shape]
            out_specs += [whole(slot_shape)] * n + [whole(wire_shape)]
            scratch += [pltpu.VMEM((n * cp, width), BF16), pltpu.VMEM((n * cp, width), F32)]
        matmuls = (2 if forward else 0) + (4 if backward else 0)
        return list(
            pl.pallas_call(
                partial(
                    expert_kernel,
                    n=n,
                    cp=cp,
                    tiles=tiles,
                    forward=forward,
                    backward=backward,
                    sizes=(zs, xs, cores, rows_in, rows_out),
                ),
                grid=(tiles,),
                in_specs=specs,
                out_specs=out_specs,
                out_shape=shapes,
                scratch_shapes=scratch,
                compiler_params=params,
                cost_estimate=cost(2 * matmuls * n * cp * width * hidden, 6e6, 2e6 if forward else 0),
                name="expert",
            )(*args)
        )

    kept = []
    previous = None
    for layer in range(layers):
        state, cached, rows_sent = run_forward(layer, previous)
        x = send(rows_sent)
        made = [[None] * per for _ in range(n)]
        d_rows = [[None] * per for _ in range(n)]
        saved = []
        wires = []
        for j in range(per):
            if layer < top:
                out = run_expert(layer, j, x, None, None, True, False)
                saved.append((out[:n], out[n], out[n + 1]))
            else:
                out = run_expert(layer, j, x, g_rows, None, True, True)
                wires.append(out[2 * n])
                for d in range(n):
                    d_rows[d][j] = out[n + d]
            for d in range(n):
                made[d][j] = out[d]
        if layer == top:
            d_back = send_back(d_rows)
        back = send_back(made)
        kept.append((state, cached, x, saved))
        previous = (cached[3], cached[6], back)

    middle, gate, back = previous
    block_out = pl.pallas_call(
        partial(out_kernel, seq=seq, **dims),
        grid=(images,),
        in_specs=[per_image(middle.shape), per_image(gate.shape), col_spec(top)] + slot_specs,
        out_specs=per_image(tokens.shape),
        out_shape=shape_of(tokens.shape, F32),
        compiler_params=params,
        cost_estimate=cost(2 * images * sp * n * per * cp * width, 6e6),
        name="block_out",
    )(middle, gate, col, *flat_of(back))

    dense = [None] * layers
    summed = [None] * layers
    grad = cotangent
    for layer in reversed(range(layers)):
        first = layer == 0
        last = layer == top
        state, cached, x, saved = kept[layer]
        if not last:
            d_rows = [[None] * per for _ in range(n)]
            wires = []
            for j in range(per):
                out = run_expert(layer, j, x, g_rows, saved[j], False, True)
                wires.append(out[n])
                for d in range(n):
                    d_rows[d][j] = out[d]
            d_back = send_back(d_rows)
        summed[layer] = [expert_sum(wire, rep_sizes) for wire in wires]
        joined, probs, attended, middle, moe_in, router, gate = cached
        args = [ids, grad, state, joined, probs, attended, middle, moe_in, router, col]
        specs = [smem()] + [per_image(a.shape) for a in args[1:-1]] + [col_spec(layer)]
        args += flat_of(d_back)
        specs += slot_specs
        args += [ln1_gain, ln1_bias, w_qkv, w_attn_out, ln2_gain, router_wide]
        specs += [
            whole(ln1_gain),
            whole(ln1_bias),
            of_layer(w_qkv, layer),
            of_layer(w_attn_out, layer),
            whole(ln2_gain),
            of_layer(router_wide, layer),
        ]
        dense_shape = shape_of((width, 4 * width + LANES), BF16)
        grad_shape = tokens.shape if first else (images, sp, width)
        shapes = [shape_of(grad_shape, F32), dense_shape]
        out_specs = [per_image(grad_shape), whole(dense_shape)]
        scratch = [
            pltpu.VMEM((n, per, cp, LANES), BF16),
            pltpu.VMEM((width, 3 * width), F32),
            pltpu.VMEM((width, width), F32),
            pltpu.VMEM((width, LANES), F32),
            pltpu.VMEM((8, width), F32),
            pltpu.VMEM((LANES, width), F32),
            pltpu.VMEM((sp, 3 * width), BF16),
        ]
        if last:
            scratch.append(pltpu.VMEM((sp, width), F32))
        if first:
            scratch.append(pltpu.VMEM((sp, width), F32))
        else:
            args.append(row)
            specs.append(row_spec_of(layer - 1))
            shapes += slot_shapes
            out_specs += slot_specs
            scratch.append(pltpu.VMEM((images * WIDE, width), BF16))
        out = pl.pallas_call(
            partial(
                backward_kernel,
                first=first,
                last=last,
                layer=layer,
                images=images,
                seq=seq,
                experts=experts,
                **dims,
            ),
            grid=(images,),
            in_specs=specs,
            out_specs=out_specs,
            out_shape=shapes,
            scratch_shapes=scratch,
            compiler_params=params,
            cost_estimate=cost(1.2e10, 3e7, 0),
            name="backward",
        )(*args)
        grad = out[0]
        dense[layer] = out[1]
        if not first:
            g_rows = send(nested(out[2:]))

    stacked = jnp.stack(dense)
    shares = lax.psum_scatter(stacked, "exp", scatter_dimension=1, tiled=True)
    shares = lax.psum(shares, "rep").astype(F32)
    at = 4 * width
    columns = lambda k: shares[:, :, at + experts + k]
    grad_in = []
    grad_out = []
    for layer in range(layers):
        for total in summed[layer]:
            part = total[: tiles * rows_in].reshape(tiles, rows_in, tile)
            grad_in.append(part.transpose(1, 0, 2).reshape(rows_in, hidden))
            grad_out.append(total[tiles * rows_in :])
    grad_in = jnp.stack(grad_in).reshape(layers, per, rows_in, hidden)
    grad_out = jnp.stack(grad_out).reshape(layers, per, rows_out, width)
    return (
        block_out,
        grad,
        columns(0),
        columns(1),
        shares[:, :, 0 : 3 * width],
        shares[:, :, 3 * width : 4 * width],
        columns(2),
        columns(3),
        shares[:, :, at : at + experts],
        grad_in,
        grad_out,
    )


def solution(mesh):
    return jax.shard_map(
        partial(local, n=mesh.shape["exp"], reps=mesh.shape["rep"]),
        mesh=mesh,
        in_specs=(
            P(("rep", "exp"), None, None),
            P(),
            P(),
            P(),
            P(),
            P(),
            P(),
            P(),
            P(None, "exp", None, None),
            P(None, "exp", None, None),
            P(None, ("rep", "exp"), None),
            P(None, ("rep", "exp"), None),
            P(("rep", "exp"), None, None),
        ),
        out_specs=(
            P(("rep", "exp"), None, None),
            P(("rep", "exp"), None, None),
            P(None, "exp"),
            P(None, "exp"),
            P(None, "exp", None),
            P(None, "exp", None),
            P(None, "exp"),
            P(None, "exp"),
            P(None, "exp", None),
            P(None, "exp", "rep", None),
            P(None, "exp", "rep", None),
        ),
        check_vma=False,
    )
```

time: 1310 us -> 815 us (0.62)
  Pallas kernels: 0 us -> 249 us
  local copies, waits for them, and re-layouts: 287 us -> 77.7 us
  waiting for transfers between devices: 444 us -> 246 us
  matrix products: 197 us -> 0 us
  other arithmetic: 239 us -> 45 us
  starting transfers between devices: 31.9 us -> 169 us
  blocking collectives: 84.1 us -> 0 us
    reduce_scatter x5 -> x1, waiting for transfers between devices: 377 us -> 0.01 us  [local(): shares = lax.psum_scatter(stacked, 'exp', scatter_dimension=1, tiled=True)]
    pallas_call x0 -> x19, Pallas kernels: none -> 249 us  [the longest x12 134 us: run_expert(): pl.pallas_call(partial(expert_kernel, n=n, cp=cp, tiles=tiles, forward=fo...]
    dot_general x42 -> x0, matrix products: 197 us -> none  [the longest x2 34.9 us: local(): jnp.einsum('erd,ehd->erh', d_produced, w_out[layer_index], preferred_elem...]
    ppermute x0 -> x96, starting transfers between devices: none -> 169 us  [the longest x24 99.7 us: line_sum(): got_up = lax.ppermute(rising.astype(BF16), axis, up).astype(F32)]
    ppermute x0 -> x96, waiting for transfers between devices: none -> 152 us  [the longest x8 130 us: line_sum(): got = lax.ppermute(part(1 - spot).astype(BF16), axis, swap)]
    gather x18 -> x0, local copies, waits for them, and re-layouts: 89 us -> none  [the longest x6 32.4 us: router_gates(): jnp.take_along_axis(jax.nn.softmax(logit_values, axis=-1), route_ids, axi...]
    reduce_sum x23 -> x0, other arithmetic: 81.7 us -> none  [the longest x2 35.6 us: local(): jnp.sum(d_dispatched[slot_index].astype(jnp.float32).reshape(tok_count, 2...]
    psum x1 -> x0, blocking collectives: 61.9 us -> none  [local(): lax.psum(shortened(dense_shares), 'rep')]
  transfers between devices with their start and end apart: 17 -> 98, of which waited for: 9 -> 16; matrix products, arithmetic and copies ran while one was open for 18% -> 12% of each run, Pallas kernels for 0% -> 28%
where the time goes in v1:
time: 815 us; the launch traced here: 802 us
  Pallas kernels  249 us (31%)
  waiting for transfers between devices  246 us (30%)
  starting transfers between devices  169 us (21%)
  local copies, waits for them, and re-layouts  77.7 us (10%)
  other arithmetic  45 us (6%)
  between operations  15.9 us (2%)
    pallas_call x12, Pallas kernels, run_expert(): pl.pallas_call(partial(expert_kernel, n=n, cp=cp, tiles=tiles, forward=fo...  134 us
    ppermute x8, waiting for transfers between devices, line_sum(): got = lax.ppermute(part(1 - spot).astype(BF16), axis, swap)  130 us
    ppermute x24, starting transfers between devices, line_sum(): got_up = lax.ppermute(rising.astype(BF16), axis, up).astype(F32)  99.7 us
    psum x1, waiting for transfers between devices, local(): shares = lax.psum(shares, 'rep').astype(F32)  94.2 us
    pallas_call x2, Pallas kernels, local(): pl.pallas_call(partial(backward_kernel, first=first, last=last, layer=lay...  58.8 us
    pallas_call x2, Pallas kernels, run_forward(): pl.pallas_call(partial(forward_kernel, first=first, layer=layer, images=i...  39 us
    unnamed x176, local copies, waits for them, and re-layouts  31.5 us
    ppermute x24, starting transfers between devices, line_sum(): got_down = lax.ppermute(falling.astype(BF16), axis, down).astype(F32)  22.6 us
  transfers between devices with their start and end apart: 98, of which 16 were waited for; matrix products, arithmetic and copies ran while one was open for 12% of the time, Pallas kernels for 28%

profile of v1, /device:TPU:0, one launch (start us, length us, event | category | flops | bytes accessed | tf_op | source)
XLA Modules:
  0.0 802.5 jit_solution(1150323803364586254)
XLA Ops:
  15.1 6.8 route.1
  21.9 17.3 %forward.2 = (bf16[4,208,1536]{2,1,0:T(8,128)(2,1)}, bf16[4,8,208,208]{3,2,1,0:T(8,128)(2,1)}, bf16[4,208,512]{2,1,0:T(8,128)(2,1)}, f32[4,208,512]{2,1,0:T(8,12...) custom-call(s32[2]{0:T(128)} %pad_add_fusion.ids.refs_0_, ...), custom_call_target="tpu_custom_call" | custom-call | flops 6000000000 | bytes 20000000 | tf_op jit(solution)/shard_map/forward/pallas_call | solution.py:742
  49.3 8.5 %expert.15 = (bf16[208,512]{1,0:T(8,128)(2,1)}, bf16[208,512]{1,0:T(8,128)(2,1)}, bf16[416,2048]{1,0:T(8,128)(2,1)}, bf16[416,2048]{1,0:T(8,128)(2,1)}) custom-call(s32[2]{0:T(128)} %pad_add_fusion.ids.refs_0_, bf16[208,512]{1,0:T(8,128)(2,1)} %get-tuple-element.125.refs_1_, bf16[208,512]{1,0:T(8,128)(2,1)} %copy-done.31, bf16[2,4,512,2048]{3,2,1,0:T(8,128)(2,1)} %refs_9_.7, ...), custom_call_target="tpu_custom_call" | custom-call | flops 1744830464 | bytes 6000000 | tf_op jit(solution)/shard_map/expert/pallas_call | solution.py:800
  60.5 8.5 %expert.14 = (bf16[208,512]{1,0:T(8,128)(2,1)}, bf16[208,512]{1,0:T(8,128)(2,1)}, bf16[416,2048]{1,0:T(8,128)(2,1)}, bf16[416,2048]{1,0:T(8,128)(2,1)}) custom-call(s32[2]{0:T(128)} %pad_add_fusion.ids.refs_0_, bf16[208,512]{1,0:T(8,128)(2,1)} %get-tuple-element.122.refs_1_, bf16[208,512]{1,0:T(8,128)(2,1)} %copy-done.32, bf16[2,4,512,2048]{3,2,1,0:T(8,128)(2,1)} %refs_9_.7, ...), custom_call_target="tpu_custom_call" | custom-call | flops 1744830464 | bytes 6000000 | tf_op jit(solution)/shard_map/expert/pallas_call | solution.py:800
  69.7 8.7 %expert.13 = (bf16[208,512]{1,0:T(8,128)(2,1)}, bf16[208,512]{1,0:T(8,128)(2,1)}, bf16[416,2048]{1,0:T(8,128)(2,1)}, bf16[416,2048]{1,0:T(8,128)(2,1)}) custom-call(s32[2]{0:T(128)} %pad_add_fusion.ids.refs_0_, bf16[208,512]{1,0:T(8,128)(2,1)} %get-tuple-element.119.refs_1_, bf16[208,512]{1,0:T(8,128)(2,1)} %copy-done.33, bf16[2,4,512,2048]{3,2,1,0:T(8,128)(2,1)} %refs_9_.7, ...), custom_call_target="tpu_custom_call" | custom-call | flops 1744830464 | bytes 6000000 | tf_op jit(solution)/shard_map/expert/pallas_call | solution.py:800
  81.1 8.5 %expert.12 = (bf16[208,512]{1,0:T(8,128)(2,1)}, bf16[208,512]{1,0:T(8,128)(2,1)}, bf16[416,2048]{1,0:T(8,128)(2,1)}, bf16[416,2048]{1,0:T(8,128)(2,1)}) custom-call(s32[2]{0:T(128)} %pad_add_fusion.ids.refs_0_, bf16[208,512]{1,0:T(8,128)(2,1)} %get-tuple-element.116.refs_1_, bf16[208,512]{1,0:T(8,128)(2,1)} %copy-done.34, bf16[2,4,512,2048]{3,2,1,0:T(8,128)(2,1)} %refs_9_.7, ...), custom_call_target="tpu_custom_call" | custom-call | flops 1744830464 | bytes 6000000 | tf_op jit(solution)/shard_map/expert/pallas_call | solution.py:800
  98.5 21.7 %forward.3 = (f32[4,208,512]{2,1,0:T(8,128)}, bf16[4,208,1536]{2,1,0:T(8,128)(2,1)}, bf16[4,8,208,208]{3,2,1,0:T(8,128)(2,1)}, bf16[4,208,512]{2,1,0:T(8,128)(2,...) custom-call(s32[2]{0:T(128)} %pad_add_fusion.ids.refs_0_, ...), custom_call_target="tpu_custom_call" | custom-call | flops 6000000000 | bytes 20000000 | tf_op jit(solution)/shard_map/forward/pallas_call | solution.py:742
  129.3 15.4 %expert.19 = (bf16[208,512]{1,0:T(8,128)(2,1)}, bf16[208,512]{1,0:T(8,128)(2,1)}, bf16[208,512]{1,0:T(8,128)(2,1)}, bf16[208,512]{1,0:T(8,128)(2,1)}, bf16[2,2,4,256,512]{4,3,2,1,0:T(8,128)(2,1)}) custom-call(s32[2]{0:T(128)} %pad_add_fusion.ids.refs_0_, bf16[208,512]{1,0:T(8,128)(2,1)} %get-tuple-element.149.refs_1_, bf16[208,512]{1,0:T(8,128)(2,1)} %copy-done.39, ...), custom_call_target="tpu_custom_call" | custom-call | flops 5234491392 | bytes 6000000 | tf_op jit(solution)/shard_map/expert/pallas_call | solution.py:800
  146.1 5.3 collective-permute-done.12.refs_2_
  152.1 14.9 %expert.18 = (bf16[208,512]{1,0:T(8,128)(2,1)}, bf16[208,512]{1,0:T(8,128)(2,1)}, bf16[208,512]{1,0:T(8,128)(2,1)}, bf16[208,512]{1,0:T(8,128)(2,1)}, bf16[2,2,4,256,512]{4,3,2,1,0:T(8,128)(2,1)}) custom-call(s32[2]{0:T(128)} %pad_add_fusion.ids.refs_0_, bf16[208,512]{1,0:T(8,128)(2,1)} %get-tuple-element.144.refs_1_, bf16[208,512]{1,0:T(8,128)(2,1)} %copy-done.46, ...), custom_call_target="tpu_custom_call" | custom-call | flops 5234491392 | bytes 6000000 | tf_op jit(solution)/shard_map/expert/pallas_call | solution.py:800
  172.3 14.9 %expert.17 = (bf16[208,512]{1,0:T(8,128)(2,1)}, bf16[208,512]{1,0:T(8,128)(2,1)}, bf16[208,512]{1,0:T(8,128)(2,1)}, bf16[208,512]{1,0:T(8,128)(2,1)}, bf16[2,2,4,256,512]{4,3,2,1,0:T(8,128)(2,1)}) custom-call(s32[2]{0:T(128)} %pad_add_fusion.ids.refs_0_, bf16[208,512]{1,0:T(8,128)(2,1)} %get-tuple-element.139.refs_1_, bf16[208,512]{1,0:T(8,128)(2,1)} %copy-done.45, ...), custom_call_target="tpu_custom_call" | custom-call | flops 5234491392 | bytes 6000000 | tf_op jit(solution)/shard_map/expert/pallas_call | solution.py:800
  192.4 15.0 %expert.16 = (bf16[208,512]{1,0:T(8,128)(2,1)}, bf16[208,512]{1,0:T(8,128)(2,1)}, bf16[208,512]{1,0:T(8,128)(2,1)}, bf16[208,512]{1,0:T(8,128)(2,1)}, bf16[2,2,4,256,512]{4,3,2,1,0:T(8,128)(2,1)}) custom-call(s32[2]{0:T(128)} %pad_add_fusion.ids.refs_0_, bf16[208,512]{1,0:T(8,128)(2,1)} %get-tuple-element.134.refs_1_, bf16[208,512]{1,0:T(8,128)(2,1)} %copy-done.40, ...), custom_call_target="tpu_custom_call" | custom-call | flops 5234491392 | bytes 6000000 | tf_op jit(solution)/shard_map/expert/pallas_call | solution.py:800
  215.6 30.4 %backward.2 = (f32[4,208,512]{2,1,0:T(8,128)}, bf16[512,2176]{1,0:T(8,128)(2,1)}, bf16[208,512]{1,0:T(8,128)(2,1)}, bf16[208,512]{1,0:T(8,128)(2,1)}, bf16[208,5...) custom-call(s32[2]{0:T(128)} %pad_add_fusion.ids.refs_0_, ...), custom_call_target="tpu_custom_call" | custom-call | flops 12000000000 | bytes 30000000 | tf_op jit(solution)/shard_map/backward/pallas_call | solution.py:913
  251.1 6.2 block_out.1
  264.4 9.9 %expert.20 = (bf16[208,512]{1,0:T(8,128)(2,1)}, bf16[208,512]{1,0:T(8,128)(2,1)}, bf16[2,2,4,256,512]{4,3,2,1,0:T(8,128)(2,1)}) custom-call(s32[2]{0:T(128)} %pad_add_fusion.ids.refs_0_, bf16[208,512]{1,0:T(8,128)(2,1)} %get-tuple-element.116.refs_1_, bf16[208,512]{1,0:T(8,128)(2,1)} %copy-done.34, bf16[208,512]{1,0:T(8,128)(2,1)} %get-tuple-element.178.refs_3_, ...), custom_call_target="tpu_custom_call" | custom-call | flops 3489660928 | bytes 6000000 | tf_op jit(solution)/shard_map/expert/pallas_call | solution.py:800
  275.0 10.1 %expert.21 = (bf16[208,512]{1,0:T(8,128)(2,1)}, bf16[208,512]{1,0:T(8,128)(2,1)}, bf16[2,2,4,256,512]{4,3,2,1,0:T(8,128)(2,1)}) custom-call(s32[2]{0:T(128)} %pad_add_fusion.ids.refs_0_, bf16[208,512]{1,0:T(8,128)(2,1)} %get-tuple-element.119.refs_1_, bf16[208,512]{1,0:T(8,128)(2,1)} %copy-done.33, bf16[208,512]{1,0:T(8,128)(2,1)} %get-tuple-element.183.refs_3_, ...), custom_call_target="tpu_custom_call" | custom-call | flops 3489660928 | bytes 6000000 | tf_op jit(solution)/shard_map/expert/pallas_call | solution.py:800
  286.6 9.8 %expert.22 = (bf16[208,512]{1,0:T(8,128)(2,1)}, bf16[208,512]{1,0:T(8,128)(2,1)}, bf16[2,2,4,256,512]{4,3,2,1,0:T(8,128)(2,1)}) custom-call(s32[2]{0:T(128)} %pad_add_fusion.ids.refs_0_, bf16[208,512]{1,0:T(8,128)(2,1)} %get-tuple-element.122.refs_1_, bf16[208,512]{1,0:T(8,128)(2,1)} %copy-done.32, bf16[208,512]{1,0:T(8,128)(2,1)} %get-tuple-element.188.refs_3_, ...), custom_call_target="tpu_custom_call" | custom-call | flops 3489660928 | bytes 6000000 | tf_op jit(solution)/shard_map/expert/pallas_call | solution.py:800
  297.1 9.8 %expert.23 = (bf16[208,512]{1,0:T(8,128)(2,1)}, bf16[208,512]{1,0:T(8,128)(2,1)}, bf16[2,2,4,256,512]{4,3,2,1,0:T(8,128)(2,1)}) custom-call(s32[2]{0:T(128)} %pad_add_fusion.ids.refs_0_, bf16[208,512]{1,0:T(8,128)(2,1)} %get-tuple-element.125.refs_1_, bf16[208,512]{1,0:T(8,128)(2,1)} %copy-done.31, bf16[208,512]{1,0:T(8,128)(2,1)} %get-tuple-element.193.refs_3_, ...), custom_call_target="tpu_custom_call" | custom-call | flops 3489660928 | bytes 6000000 | tf_op jit(solution)/shard_map/expert/pallas_call | solution.py:800
  321.4 28.4 %backward.3 = (f32[4,197,512]{2,1,0:T(8,128)}, bf16[512,2176]{1,0:T(8,128)(2,1)}) custom-call(s32[2]{0:T(128)} %pad_add_fusion.ids.refs_0_, f32[4,208,512]{2,1,0:T(8,128)} %get-tuple-element.172.refs_1_, f32[4,197,512]{2,1,0:T(8,128)} %copy.37.refs_1_.refs_2_, bf16[4,208,1536]{2,1,0:T(8,128)(2,1)} %get-tuple-element.173.refs_3_, ...), custom_call_target="tpu_custom_call" | custom-call | flops 12000000000 | bytes 30000000 | tf_op jit(solution)/shard_map/backward/pallas_call | solution.py:913
  381.8 12.5 %collective-permute-done.89 = bf16[4,256,512]{2,1,0:T(8,128)(2,1)} collective-permute-done((bf16[4,256,512]{2,1,0:T(8,128)(2,1)}, bf16[4,256,512]{2,1,0:T(8,128)(2,1)}, u32[]{:S(2)}, u32[]{:S(2)}) %collective-permute-start.89) | collective-permute-done | bytes 1048608 | tf_op jit(solution)/shard_map/ppermute | solution.py:574
  399.4 17.3 %collective-permute-done.81 = bf16[4,256,512]{2,1,0:T(8,128)(2,1)} collective-permute-done((bf16[4,256,512]{2,1,0:T(8,128)(2,1)}, bf16[4,256,512]{2,1,0:T(8,128)(2,1)}, u32[]{:S(2)}, u32[]{:S(2)}) %collective-permute-start.81) | collective-permute-done | bytes 1048608 | tf_op jit(solution)/shard_map/ppermute | solution.py:574
  419.0 20.2 %collective-permute-done.73 = bf16[4,256,512]{2,1,0:T(8,128)(2,1)} collective-permute-done((bf16[4,256,512]{2,1,0:T(8,128)(2,1)S(1)}, bf16[4,256,512]{2,1,0:T(8,128)(2,1)}, u32[]{:S(2)}, u32[]{:S(2)}) %collective-permute-start.73) | collective-permute-done | bytes 1048608 | tf_op jit(solution)/shard_map/ppermute | solution.py:574
  444.3 17.3 %collective-permute-done.65 = bf16[4,256,512]{2,1,0:T(8,128)(2,1)S(1)} collective-permute-done((bf16[4,256,512]{2,1,0:T(8,128)(2,1)S(1)}, bf16[4,256,512]{2,1,0:T(8,128)(2,1)S(1)}, u32[]{:S(2)}, u32[]{:S(2)}) %collective-permute-start.65) | collective-permute-done | bytes 1048608 | tf_op jit(solution)/shard_map/ppermute | solution.py:574
  485.1 21.4 %collective-permute-done.41 = bf16[4,256,512]{2,1,0:T(8,128)(2,1)S(1)} collective-permute-done((bf16[4,256,512]{2,1,0:T(8,128)(2,1)S(1)}, bf16[4,256,512]{2,1,0:T(8,128)(2,1)S(1)}, u32[]{:S(2)}, u32[]{:S(2)}) %collective-permute-start.41) | collective-permute-done | bytes 1048608 | tf_op jit(solution)/shard_map/ppermute | solution.py:574
  510.6 18.4 %collective-permute-done.49 = bf16[4,256,512]{2,1,0:T(8,128)(2,1)S(1)} collective-permute-done((bf16[4,256,512]{2,1,0:T(8,128)(2,1)S(1)}, bf16[4,256,512]{2,1,0:T(8,128)(2,1)S(1)}, u32[]{:S(2)}, u32[]{:S(2)}) %collective-permute-start.49) | collective-permute-done | bytes 1048608 | tf_op jit(solution)/shard_map/ppermute | solution.py:574
  530.0 21.0 %collective-permute-done.57 = bf16[4,256,512]{2,1,0:T(8,128)(2,1)S(1)} collective-permute-done((bf16[4,256,512]{2,1,0:T(8,128)(2,1)S(1)}, bf16[4,256,512]{2,1,0:T(8,128)(2,1)S(1)}, u32[]{:S(2)}, u32[]{:S(2)}) %collective-permute-start.57) | collective-permute-done | bytes 1048608 | tf_op jit(solution)/shard_map/ppermute | solution.py:574
  585.5 5.3 collective-permute-start.84
  605.9 5.2 collective-permute-start.35
  651.3 5.2 collective-permute-start.44
  659.7 5.3 collective-permute-start.52
  667.2 5.3 collective-permute-start.60
  693.1 94.2 %all-reduce.3.cloned.1.call-done = bf16[2,256,2176]{2,1,0:T(8,128)(2,1)} async-done(((bf16[2,256,2176]{2,1,0:T(8,128)(2,1)}), bf16[2,256,2176]{2,1,0:T(8,128)(2,1)}) %all-reduce.3.cloned.1.call-update) | async-done | bytes 2228240 | tf_op jit(solution)/shard_map/psum | solution.py:940
  (462 shorter events, 288.0 us)
Async XLA Ops:
  7.2 682.3 %reduce-scatter.2.cloned.1.call-start = ((), (), s32[]{:S(2)}) async-start(), calls=%async_computation.1 | async-start | bytes 6684672 | tf_op jit(solution)/shard_map/reduce_scatter | solution.py:939
  42.4 38.1 %collective-permute-start = (bf16[208,512]{1,0:T(8,128)(2,1)}, bf16[208,512]{1,0:T(8,128)(2,1)S(1)}, u32[]{:S(2)}, u32[]{:S(2)}) collective-permute-start(bf16[208,512]{1,0:T(8,128)(2,1)} %get-tuple-element.117), channel_id=1, source_target_pairs={{0,1},{1,0},{2,3},{3,2},{4,5},{5,4},{6,7},{7,6},{8,9},{9,8},{10,11... | collective-permute-start | bytes 638984 | tf_op jit(solution)/shard_map/ppermute | solution.py:674
  57.7 39.8 %collective-permute-start.7 = (bf16[208,512]{1,0:T(8,128)(2,1)}, bf16[208,512]{1,0:T(8,128)(2,1)S(1)}, u32[]{:S(2)}, u32[]{:S(2)}) collective-permute-start(bf16[208,512]{1,0:T(8,128)(2,1)} %get-tuple-element.131.refs_6_), channel_id=1, source_target_pairs={{0,1},{1,0},{2,3},{3,2},{4,5},{5,4},{6,7},{7,6},{8,9},{9,8},{10,11... | collective-permute-start | bytes 638984 | tf_op jit(solution)/shard_map/ppermute | solution.py:681
  120.2 70.0 %collective-permute-start.9 = (bf16[208,512]{1,0:T(8,128)(2,1)S(1)}, bf16[208,512]{1,0:T(8,128)(2,1)S(1)}, u32[]{:S(2)}, u32[]{:S(2)}) collective-permute-start(bf16[208,512]{1,0:T(8,128)(2,1)S(1)} %copy-done.52), channel_id=1, source_target_pairs={{0,1},{1,0},{2,3},{3,2},{4,5},{5,4},{6,7},{7,6},{8,9},{9,8},{10,11... | collective-permute-start | bytes 638984 | tf_op jit(solution)/shard_map/ppermute | solution.py:674
  122.3 47.9 %collective-permute-start.11 = (bf16[208,512]{1,0:T(8,128)(2,1)S(1)}, bf16[208,512]{1,0:T(8,128)(2,1)S(1)}, u32[]{:S(2)}, u32[]{:S(2)}) collective-permute-start(bf16[208,512]{1,0:T(8,128)(2,1)S(1)} %copy-done.53), channel_id=1, source_target_pairs={{0,1},{1,0},{2,3},{3,2},{4,5},{5,4},{6,7},{7,6},{8,9},{9,8},{10,11... | collective-permute-start | bytes 638984 | tf_op jit(solution)/shard_map/ppermute | solution.py:674
  124.3 67.5 %collective-permute-start.8 = (bf16[208,512]{1,0:T(8,128)(2,1)}, bf16[208,512]{1,0:T(8,128)(2,1)S(1)}, u32[]{:S(2)}, u32[]{:S(2)}) collective-permute-start(bf16[208,512]{1,0:T(8,128)(2,1)} %get-tuple-element.135), channel_id=1, source_target_pairs={{0,1},{1,0},{2,3},{3,2},{4,5},{5,4},{6,7},{7,6},{8,9},{9,8},{10,11... | collective-permute-start | bytes 638984 | tf_op jit(solution)/shard_map/ppermute | solution.py:674
  151.4 98.4 %collective-permute-start.19 = (bf16[208,512]{1,0:T(8,128)(2,1)}, bf16[208,512]{1,0:T(8,128)(2,1)S(1)}, u32[]{:S(2)}, u32[]{:S(2)}) collective-permute-start(bf16[208,512]{1,0:T(8,128)(2,1)} %get-tuple-element.157), channel_id=1, source_target_pairs={{0,1},{1,0},{2,3},{3,2},{4,5},{5,4},{6,7},{7,6},{8,9},{9,8},{10,11... | collective-permute-start | bytes 638984 | tf_op jit(solution)/shard_map/ppermute | solution.py:681
  170.1 41.2 %collective-permute-start.23 = (bf16[208,512]{1,0:T(8,128)(2,1)S(1)}, bf16[208,512]{1,0:T(8,128)(2,1)S(1)}, u32[]{:S(2)}, u32[]{:S(2)}) collective-permute-start(bf16[208,512]{1,0:T(8,128)(2,1)S(1)} %copy-done.65), channel_id=1, source_target_pairs={{0,1},{1,0},{2,3},{3,2},{4,5},{5,4},{6,7},{7,6},{8,9},{9,8},{10,11... | collective-permute-start | bytes 638984 | tf_op jit(solution)/shard_map/ppermute | solution.py:681
  171.6 41.2 %collective-permute-start.22 = (bf16[208,512]{1,0:T(8,128)(2,1)S(1)}, bf16[208,512]{1,0:T(8,128)(2,1)S(1)}, u32[]{:S(2)}, u32[]{:S(2)}) collective-permute-start(bf16[208,512]{1,0:T(8,128)(2,1)S(1)} %copy-done.68), channel_id=1, source_target_pairs={{0,1},{1,0},{2,3},{3,2},{4,5},{5,4},{6,7},{7,6},{8,9},{9,8},{10,11... | collective-permute-start | bytes 638984 | tf_op jit(solution)/shard_map/ppermute | solution.py:681
  211.3 38.5 %collective-permute-start.18 = (bf16[208,512]{1,0:T(8,128)(2,1)S(1)}, bf16[208,512]{1,0:T(8,128)(2,1)S(1)}, u32[]{:S(2)}, u32[]{:S(2)}) collective-permute-start(bf16[208,512]{1,0:T(8,128)(2,1)S(1)} %copy-done.57), channel_id=1, source_target_pairs={{0,1},{1,0},{2,3},{3,2},{4,5},{5,4},{6,7},{7,6},{8,9},{9,8},{10,11... | collective-permute-start | bytes 638984 | tf_op jit(solution)/shard_map/ppermute | solution.py:681
  212.7 37.6 %collective-permute-start.17 = (bf16[208,512]{1,0:T(8,128)(2,1)S(1)}, bf16[208,512]{1,0:T(8,128)(2,1)S(1)}, u32[]{:S(2)}, u32[]{:S(2)}) collective-permute-start(bf16[208,512]{1,0:T(8,128)(2,1)S(1)} %copy-done.59), channel_id=1, source_target_pairs={{0,1},{1,0},{2,3},{3,2},{4,5},{5,4},{6,7},{7,6},{8,9},{9,8},{10,11... | collective-permute-start | bytes 638984 | tf_op jit(solution)/shard_map/ppermute | solution.py:681
  213.5 36.9 %collective-permute-start.16 = (bf16[208,512]{1,0:T(8,128)(2,1)S(1)}, bf16[208,512]{1,0:T(8,128)(2,1)S(1)}, u32[]{:S(2)}, u32[]{:S(2)}) collective-permute-start(bf16[208,512]{1,0:T(8,128)(2,1)S(1)} %copy-done.63), channel_id=1, source_target_pairs={{0,1},{1,0},{2,3},{3,2},{4,5},{5,4},{6,7},{7,6},{8,9},{9,8},{10,11... | collective-permute-start | bytes 638984 | tf_op jit(solution)/shard_map/ppermute | solution.py:681
  249.8 106.6 %collective-permute-start.88 = (bf16[2,4,256,512]{3,2,1,0:T(8,128)(2,1)}, bf16[2,4,256,512]{3,2,1,0:T(8,128)(2,1)}, u32[]{:S(2)}, u32[]{:S(2)}) collective-permute-start(bf16[2,4,256,512]{3,2,1,0:T(8,128)(2,1)} %slice_bitcast_fusion), channel_id=1, source_target_pairs={{0,2},{2,0},{4,6},{6,4},{8,10},{10,8},{12,14},{14,12},{16,18},{18,... | collective-permute-start | bytes 6291464 | tf_op jit(solution)/shard_map/ppermute | solution.py:594
  249.8 109.7 %collective-permute-start.80 = (bf16[2,4,256,512]{3,2,1,0:T(8,128)(2,1)}, bf16[2,4,256,512]{3,2,1,0:T(8,128)(2,1)}, u32[]{:S(2)}, u32[]{:S(2)}) collective-permute-start(bf16[2,4,256,512]{3,2,1,0:T(8,128)(2,1)} %slice_bitcast_fusion.1), channel_id=1, source_target_pairs={{0,2},{2,0},{4,6},{6,4},{8,10},{10,8},{12,14},{14,12},{16,18},{18,... | collective-permute-start | bytes 6291464 | tf_op jit(solution)/shard_map/ppermute | solution.py:594
  263.0 33.4 %collective-permute-start.27 = (bf16[208,512]{1,0:T(8,128)(2,1)S(1)}, bf16[208,512]{1,0:T(8,128)(2,1)S(1)}, u32[]{:S(2)}, u32[]{:S(2)}) collective-permute-start(bf16[208,512]{1,0:T(8,128)(2,1)S(1)} %copy-done.56), channel_id=1, source_target_pairs={{0,1},{1,0},{2,3},{3,2},{4,5},{5,4},{6,7},{7,6},{8,9},{9,8},{10,11... | collective-permute-start | bytes 638984 | tf_op jit(solution)/shard_map/ppermute | solution.py:674
  274.3 40.4 %collective-permute-start.28 = (bf16[208,512]{1,0:T(8,128)(2,1)}, bf16[208,512]{1,0:T(8,128)(2,1)S(1)}, u32[]{:S(2)}, u32[]{:S(2)}) collective-permute-start(bf16[208,512]{1,0:T(8,128)(2,1)} %get-tuple-element.198), channel_id=1, source_target_pairs={{0,1},{1,0},{2,3},{3,2},{4,5},{5,4},{6,7},{7,6},{8,9},{9,8},{10,11... | collective-permute-start | bytes 638984 | tf_op jit(solution)/shard_map/ppermute | solution.py:681
  317.7 45.3 %collective-permute-start.72 = (bf16[2,4,256,512]{3,2,1,0:T(8,128)(2,1)}, bf16[2,4,256,512]{3,2,1,0:T(8,128)(2,1)}, u32[]{:S(2)}, u32[]{:S(2)}) collective-permute-start(bf16[2,4,256,512]{3,2,1,0:T(8,128)(2,1)} %slice_bitcast_fusion.2), channel_id=1, source_target_pairs={{0,2},{2,0},{4,6},{6,4},{8,10},{10,8},{12,14},{14,12},{16,18},{18,... | collective-permute-start | bytes 6291464 | tf_op jit(solution)/shard_map/ppermute | solution.py:594
  317.8 50.1 %collective-permute-start.64 = (bf16[2,4,256,512]{3,2,1,0:T(8,128)(2,1)}, bf16[2,4,256,512]{3,2,1,0:T(8,128)(2,1)}, u32[]{:S(2)}, u32[]{:S(2)}) collective-permute-start(bf16[2,4,256,512]{3,2,1,0:T(8,128)(2,1)} %slice_bitcast_fusion.3), channel_id=1, source_target_pairs={{0,2},{2,0},{4,6},{6,4},{8,10},{10,8},{12,14},{14,12},{16,18},{18,... | collective-permute-start | bytes 6291464 | tf_op jit(solution)/shard_map/ppermute | solution.py:594
  320.8 51.3 %collective-permute-start.32 = (bf16[2,4,256,512]{3,2,1,0:T(8,128)(2,1)}, bf16[2,4,256,512]{3,2,1,0:T(8,128)(2,1)}, u32[]{:S(2)}, u32[]{:S(2)}) collective-permute-start(bf16[2,4,256,512]{3,2,1,0:T(8,128)(2,1)} %slice_bitcast_fusion.7), channel_id=1, source_target_pairs={{0,2},{2,0},{4,6},{6,4},{8,10},{10,8},{12,14},{14,12},{16,18},{18,... | collective-permute-start | bytes 6291464 | tf_op jit(solution)/shard_map/ppermute | solution.py:594
  356.3 430.9 %all-reduce.3.cloned.1.call-start = ((), (), s32[]{:S(2)}) async-start(), calls=%async_computation.2 | async-start | bytes 4456448 | tf_op jit(solution)/shard_map/psum | solution.py:940
  372.1 44.7 %collective-permute-start.81 = (bf16[4,256,512]{2,1,0:T(8,128)(2,1)}, bf16[4,256,512]{2,1,0:T(8,128)(2,1)}, u32[]{:S(2)}, u32[]{:S(2)}) collective-permute-start(bf16[4,256,512]{2,1,0:T(8,128)(2,1)} %dynamic-slice_bitcast_fusion.1), channel_id=1, source_target_pairs={{0,4},{2,6},{8,12},{10,14},{16,20},{18,22},{24,28},{26,30},{4,0},{... | collective-permute-start | bytes 3145736 | tf_op jit(solution)/shard_map/ppermute | solution.py:574
  376.0 63.2 %collective-permute-start.73 = (bf16[4,256,512]{2,1,0:T(8,128)(2,1)S(1)}, bf16[4,256,512]{2,1,0:T(8,128)(2,1)}, u32[]{:S(2)}, u32[]{:S(2)}) collective-permute-start(bf16[4,256,512]{2,1,0:T(8,128)(2,1)S(1)} %dynamic-slice_bitcast_fusion.2), channel_id=1, source_target_pairs={{0,4},{2,6},{8,12},{10,14},{16,20},{18,22},{24,28},{26,30},{4,0},{... | collective-permute-start | bytes 3145736 | tf_op jit(solution)/shard_map/ppermute | solution.py:574
  377.5 84.1 %collective-permute-start.65 = (bf16[4,256,512]{2,1,0:T(8,128)(2,1)S(1)}, bf16[4,256,512]{2,1,0:T(8,128)(2,1)S(1)}, u32[]{:S(2)}, u32[]{:S(2)}) collective-permute-start(bf16[4,256,512]{2,1,0:T(8,128)(2,1)S(1)} %dynamic-slice_bitcast_fusion.3), channel_id=1, source_target_pairs={{0,4},{2,6},{8,12},{10,14},{16,20},{18,22},{24,28},{26,30},{4,0},{... | collective-permute-start | bytes 3145736 | tf_op jit(solution)/shard_map/ppermute | solution.py:574
  379.6 104.4 %collective-permute-start.33 = (bf16[4,256,512]{2,1,0:T(8,128)(2,1)S(1)}, bf16[4,256,512]{2,1,0:T(8,128)(2,1)S(1)}, u32[]{:S(2)}, u32[]{:S(2)}) collective-permute-start(bf16[4,256,512]{2,1,0:T(8,128)(2,1)S(1)} %dynamic-slice_bitcast_fusion.7), channel_id=1, source_target_pairs={{0,4},{2,6},{8,12},{10,14},{16,20},{18,22},{24,28},{26,30},{4,0},{... | collective-permute-start | bytes 3145736 | tf_op jit(solution)/shard_map/ppermute | solution.py:574
  395.8 66.8 %collective-permute-start.90 = (bf16[256,512]{1,0:T(8,128)(2,1)S(1)}, bf16[256,512]{1,0:T(8,128)(2,1)S(1)}, u32[]{:S(2)}, u32[]{:S(2)}) collective-permute-start(bf16[256,512]{1,0:T(8,128)(2,1)S(1)} %get-tuple-element.243), channel_id=1, source_target_pairs={{0,8},{2,10},{4,12},{6,14},{1,9},{3,11},{5,13},{7,15}} | collective-permute-start | bytes 786440 | tf_op jit(solution)/shard_map/ppermute | solution.py:581
  416.8 49.5 %collective-permute-start.93 = (bf16[256,512]{1,0:T(8,128)(2,1)S(1)}, bf16[256,512]{1,0:T(8,128)(2,1)S(1)}, u32[]{:S(2)}, u32[]{:S(2)}) collective-permute-start(bf16[256,512]{1,0:T(8,128)(2,1)S(1)} %get-tuple-element.244), channel_id=1, source_target_pairs={{24,16},{26,18},{28,20},{30,22},{25,17},{27,19},{29,21},{31,23}} | collective-permute-start | bytes 786440 | tf_op jit(solution)/shard_map/ppermute | solution.py:582
  467.1 39.4 %collective-permute-start.41 = (bf16[4,256,512]{2,1,0:T(8,128)(2,1)S(1)}, bf16[4,256,512]{2,1,0:T(8,128)(2,1)S(1)}, u32[]{:S(2)}, u32[]{:S(2)}) collective-permute-start(bf16[4,256,512]{2,1,0:T(8,128)(2,1)S(1)} %dynamic-slice_bitcast_fusion.6), channel_id=1, source_target_pairs={{0,4},{2,6},{8,12},{10,14},{16,20},{18,22},{24,28},{26,30},{4,0},{... | collective-permute-start | bytes 3145736 | tf_op jit(solution)/shard_map/ppermute | solution.py:574
  473.8 55.2 %collective-permute-start.49 = (bf16[4,256,512]{2,1,0:T(8,128)(2,1)S(1)}, bf16[4,256,512]{2,1,0:T(8,128)(2,1)S(1)}, u32[]{:S(2)}, u32[]{:S(2)}) collective-permute-start(bf16[4,256,512]{2,1,0:T(8,128)(2,1)S(1)} %dynamic-slice_bitcast_fusion.5), channel_id=1, source_target_pairs={{0,4},{2,6},{8,12},{10,14},{16,20},{18,22},{24,28},{26,30},{4,0},{... | collective-permute-start | bytes 3145736 | tf_op jit(solution)/shard_map/ppermute | solution.py:574
  476.7 74.3 %collective-permute-start.57 = (bf16[4,256,512]{2,1,0:T(8,128)(2,1)S(1)}, bf16[4,256,512]{2,1,0:T(8,128)(2,1)S(1)}, u32[]{:S(2)}, u32[]{:S(2)}) collective-permute-start(bf16[4,256,512]{2,1,0:T(8,128)(2,1)S(1)} %dynamic-slice_bitcast_fusion.4), channel_id=1, source_target_pairs={{0,4},{2,6},{8,12},{10,14},{16,20},{18,22},{24,28},{26,30},{4,0},{... | collective-permute-start | bytes 3145736 | tf_op jit(solution)/shard_map/ppermute | solution.py:574
  478.1 77.0 %collective-permute-start.91 = (bf16[256,512]{1,0:T(8,128)(2,1)S(1)}, bf16[256,512]{1,0:T(8,128)(2,1)S(1)}, u32[]{:S(2)}, u32[]{:S(2)}) collective-permute-start(bf16[256,512]{1,0:T(8,128)(2,1)S(1)} %get-tuple-element.241), channel_id=1, source_target_pairs={{0,8},{2,10},{4,12},{6,14},{8,16},{10,18},{12,20},{14,22},{1,9},{3... | collective-permute-start | bytes 786440 | tf_op jit(solution)/shard_map/ppermute | solution.py:581
  484.1 71.7 %collective-permute-start.94 = (bf16[256,512]{1,0:T(8,128)(2,1)S(1)}, bf16[256,512]{1,0:T(8,128)(2,1)S(1)}, u32[]{:S(2)}, u32[]{:S(2)}) collective-permute-start(bf16[256,512]{1,0:T(8,128)(2,1)S(1)} %get-tuple-element.242), channel_id=1, source_target_pairs={{16,8},{18,10},{20,12},{22,14},{24,16},{26,18},{28,20},{30,22},{17... | collective-permute-start | bytes 786440 | tf_op jit(solution)/shard_map/ppermute | solution.py:582
  506.5 53.4 %collective-permute-start.83 = (bf16[256,512]{1,0:T(8,128)(2,1)S(1)}, bf16[256,512]{1,0:T(8,128)(2,1)S(1)}, u32[]{:S(2)}, u32[]{:S(2)}) collective-permute-start(bf16[256,512]{1,0:T(8,128)(2,1)S(1)} %get-tuple-element.247), channel_id=1, source_target_pairs={{0,8},{2,10},{4,12},{6,14},{8,16},{10,18},{12,20},{14,22},{1,9},{3... | collective-permute-start | bytes 786440 | tf_op jit(solution)/shard_map/ppermute | solution.py:581
  (146 other events, 1585.4 us)
Sparse Core Ops, SparseCore 0:
  356.5 58.2 reduce-scatter.1
  689.6 97.6 all-reduce.2

commit v2 on v1

--- a/solution.py
+++ b/solution.py
@@ -63,25 +63,15 @@
 
 
 def gelu_both(x):
-    z = x * 0.7071067811865476
-    size = jnp.abs(z)
-    denom = 1.0 + 0.3275911 * size
-    guess = pl.reciprocal(denom, approx=True)
-    t = guess * (2.0 - denom * guess)
-    raised = jnp.exp(-(z * z))
-    poly = t * (
-        0.127414796
-        + t * (-0.142248368 + t * (0.7107068705 + t * (-0.7265760135 + t * 0.5307027145)))
-    )
-    tail = poly * raised
-    phi = jnp.where(x >= 0.0, 1.0 - tail, tail)
+    phi = 0.5 + 0.5 * lax.erf(x * 0.7071067811865476)
+    raised = jnp.exp2((x * x) * -0.7213475204444817)
     return x * phi, phi + x * raised * 0.3989422804014327
 
 
 def route_kernel(ids, r_ref, p_ref, row_ref, col_ref, tall, wide, *, n, per, cap, cp, images, seq):
     tokens = images * seq
     bits = (2 * tokens - 1).bit_length()
-    me = ids[0]
+    my_exp, my_core = ids[0], ids[1]
     key = (r_ref[0] << bits) + p_ref[0]
     tall[...] = jnp.full(tall.shape, -1, jnp.int32)
     tall[0:tokens, 0:2] = key
@@ -101,8 +91,9 @@
         group = jnp.zeros((1, lanes), jnp.int32)
         for q in range(1, n):
             group = group + jnp.where(expert >= q * per, 1, 0)
-        ahead = group - me
-        ahead = jnp.where(ahead < 0, ahead + n, ahead)
+        ahead = (group >> 1) - my_exp
+        ahead = jnp.where(ahead < 0, ahead + n // 2, ahead)
+        ahead = 2 * ahead + jnp.where((group & 1) == my_core, 0, 1)
         slot = (ahead * per + (expert - group * per)) * cp + count
         kept = count < cap
         slots.append(jnp.where(kept, slot, -1))
@@ -118,7 +109,13 @@
         col_ref[0, i] = wide[...].T[0:sp, :]
 
 
-def spread_rows(me, row_ref, rhs, outs, n, per, cp, width, experts):
+def first_expert(ids, d, n, per):
+    side = lax.rem(ids[0] + d // 2, n // 2)
+    core = ids[1] if d % 2 == 0 else 1 - ids[1]
+    return (2 * side + core) * per
+
+
+def spread_rows(ids, row_ref, rhs, outs, n, per, cp, width, experts):
     slots0 = row_ref[0, 0:1, :]
     slots1 = row_ref[0, 1:2, :]
     shape = (per * cp, row_ref.shape[2])
@@ -126,7 +123,7 @@
         place = iota(shape, 0) + d * per * cp
         pick = jnp.where(jnp.logical_or(place == slots0, place == slots1), 1.0, 0.0).astype(BF16)
         rows = nn(pick, rhs[...])
-        base = lax.rem(me + d, n) * per
+        base = first_expert(ids, d, n, per)
         for j in range(per):
             part = rows[j * cp : (j + 1) * cp, :]
             data = part[:, :width]
@@ -140,7 +137,10 @@
                 where = iota(data.shape, 0)
                 data = jnp.where(where == cp - 1, high, data)
                 data = jnp.where(where == cp - 2, line - high, data)
-            outs[d][j][...] = data.astype(BF16)
+            if len(outs[d]) == per:
+                outs[d][j][...] = data.astype(BF16)
+            else:
+                outs[d][0][j * cp : (j + 1) * cp, :] = data.astype(BF16)
 
 
 def gathered(c0, c1, v0, v1, back, n, per, cp):
@@ -262,24 +262,25 @@
 
     @pl.when(i == images - 1)
     def _():
-        spread_rows(ids[0], row, rhs, disp, n, per, cp, width, experts)
+        spread_rows(ids, row, rhs, disp, n, per, cp, width, experts)
 
 
 def cotangent_kernel(*refs, n, per, cp, images, seq):
     it = iter(refs)
     ids, g_ref, row = next(it), next(it), next(it)
-    outs = take(it, n, per)
+    outs = take(it, n, 1)
     rhs = next(it)
     rhs[...] = jnp.zeros(rhs.shape, BF16)
     for i in range(images):
         rhs[i * WIDE : i * WIDE + seq, :] = g_ref[i].astype(BF16)
-    spread_rows(ids[0], row, rhs, outs, n, per, cp, rhs.shape[1], 0)
+    spread_rows(ids, row, rhs, outs, n, per, cp, rhs.shape[1], 0)
 
 
 def out_kernel(*refs, n, per, cp, seq):
     it = iter(refs)
     mid, gate, col = next(it), next(it), next(it)
-    back = take(it, n, per)
+    joint = take(it, n, 1)
+    back = [[part[0].at[pl.ds(j * cp, cp)] for j in range(per)] for part in joint]
     out = next(it)
     state = mid[0] + gathered(
         col[0, 0, :, 0:1], col[0, 0, :, 1:2], gate[0, :, 0:1], gate[0, :, 1:2], back, n, per, cp
@@ -287,25 +288,31 @@
     out[0] = state[0:seq, :]
 
 
-def expert_kernel(*refs, n, cp, tiles, forward, backward, sizes):
+def slot_gates(rows, cp):
+    tail = rows[cp - 16 : cp, 0:WIDE].astype(F32)
+    line = jnp.sum(jnp.where(iota(tail.shape, 0) >= 14, tail, 0.0), axis=0, keepdims=True)
+    return row_to_col(line, cp)
+
+
+def expert_kernel(*refs, n, cp, tiles, produce, backward, joined):
     it = iter(refs)
-    ids = next(it)
+    next(it)
     xs = [next(it) for _ in range(n)]
     if backward:
         gs = [next(it) for _ in range(n)]
-        if not forward:
+        if not produce:
             made = [next(it) for _ in range(n)]
-            act_in, slope_in = next(it), next(it)
+    earlier = [[next(it) for _ in range(n)] for _ in range(joined)]
     w_in, w_out = next(it), next(it)
-    if forward:
+    if produce:
         prod = [next(it) for _ in range(n)]
-        if not backward:
-            act_out, slope_out = next(it), next(it)
     if backward:
         dx = [next(it) for _ in range(n)]
-        wire = next(it)
+        act_s, dpre_s, dprod_out = next(it), next(it), next(it)
     xcat = next(it)
-    if forward:
+    if not backward:
+        act_s = next(it)
+    if produce:
         acc_p = next(it)
     if backward:
         dprod, acc_d = next(it), next(it)
@@ -317,70 +324,41 @@
         for d in range(n):
             xcat[d * cp : (d + 1) * cp, :] = xs[d][...]
             if backward:
-                tail = xs[d][cp - 16 : cp, 0:WIDE].astype(F32)
-                line = jnp.sum(jnp.where(iota(tail.shape, 0) >= 14, tail, 0.0), axis=0, keepdims=True)
-                gate = row_to_col(line, cp)
-                dprod[d * cp : (d + 1) * cp, :] = (gate * gs[d][...].astype(F32)).astype(BF16)
-
-    if forward:
-        pre = nn(xcat[...], w_in[0, 0])
-        value, slope = gelu_both(pre)
-        act = value.astype(BF16)
-        if not backward:
-            act_out[...] = act
-            slope_out[...] = slope.astype(BF16)
-        term = nn(act, w_out[0, 0])
-
-        @pl.when(h == 0)
-        def _():
-            acc_p[...] = term
-
-        @pl.when(h > 0)
-        def _():
-            acc_p[...] += term
-    else:
-        act = act_in[...]
-        slope = slope_in[...].astype(F32)
+                gate = slot_gates(xs[d], cp)
+                part = (gate * gs[d][...].astype(F32)).astype(BF16)
+                dprod[d * cp : (d + 1) * cp, :] = part
+                dprod_out[d * cp : (d + 1) * cp, :] = part
+        if produce:
+            acc_p[...] = jnp.zeros(acc_p.shape, F32)
+        if backward:
+            acc_d[...] = jnp.zeros(acc_d.shape, F32)
+
+    step = 16
+    pre = nn(xcat[...], w_in[0, 0])
     if backward:
-        zs, xs_, cores, rows_in, rows_out = sizes
-        core = ids[1]
         d_act = nt(dprod[...], w_out[0, 0])
-        d_pre = (d_act * slope).astype(BF16)
-        grad_out = tn(act, dprod[...]).astype(BF16)
-        for x in range(xs_):
-            for c in range(cores):
-                at = (x * cores + c) * rows_out
-                wire[lax.rem(c + core, cores), x, h, tiles * rows_in :, :] = grad_out[
-                    at : at + rows_out, :
-                ]
-        grad_in = tn(xcat[...], d_pre).astype(BF16)
-        spot = pl.multiple_of(h * rows_in, rows_in)
-        for z in range(zs):
-            for x in range(xs_):
-                for c in range(cores):
-                    at = ((z * xs_ + x) * cores + c) * rows_in
-                    wire[lax.rem(c + core, cores), x, z, pl.ds(spot, rows_in), :] = grad_in[
-                        at : at + rows_in, :
-                    ]
-        term_d = nt(d_pre, w_in[0, 0])
-
-        @pl.when(h == 0)
-        def _():
-            acc_d[...] = term_d
-
-        @pl.when(h > 0)
-        def _():
-            acc_d[...] += term_d
+    for r in range(0, n * cp, step):
+        rows = slice(r, r + step)
+        value, slope = gelu_both(pre[rows, :])
+        act_s[rows, :] = value.astype(BF16)
+        if backward:
+            dpre_s[rows, :] = (d_act[rows, :] * slope).astype(BF16)
+    if produce:
+        acc_p[...] += nn(act_s[...], w_out[0, 0])
+    if backward:
+        acc_d[...] += nt(dpre_s[...], w_in[0, 0])
 
     @pl.when(h == tiles - 1)
     def _():
         for d in range(n):
             rows = pl.ds(d * cp, cp)
-            if forward:
+            if produce:
                 result = acc_p[rows, :].astype(BF16)
-                prod[d][...] = result
+                prod[d][joined * cp :, :] = result
+                for k in range(joined):
+                    prod[d][k * cp : (k + 1) * cp, :] = earlier[k][d][...]
             if backward:
-                if not forward:
+                if not produce:
                     result = made[d][...]
                 d_gate = jnp.sum(
                     result.astype(F32) * gs[d][...].astype(F32), axis=1, keepdims=True
@@ -388,6 +366,123 @@
                 line = col_to_row(d_gate, width)
                 data = acc_d[rows, :]
                 dx[d][...] = jnp.where(iota(data.shape, 0) == cp - 1, line, data).astype(BF16)
+
+
+def place_of(index, order):
+    return sum(((index >> bit) & 1) << (len(order) - 1 - k) for k, bit in enumerate(order))
+
+
+def weight_kernel(*refs, n, cp, tiles, wire, follows):
+    it = iter(refs)
+    ids = next(it)
+    xs = [next(it) for _ in range(n)]
+    act, dpre, dprod = next(it), next(it), next(it)
+    if follows:
+        next(it)
+    reps, rows_in, rows_out, order_out, order_in, out_at, in_at, whole_at = wire
+    wire_refs = [next(it) for _ in range(4 if whole_at is None else 1)]
+    xcat, wires, sems = next(it), [next(it), next(it)], next(it)
+    h = pl.program_id(0)
+    mine_out, mine_in = ids[out_at], ids[in_at]
+
+    @pl.when(h == 0)
+    def _():
+        for d in range(n):
+            xcat[d * cp : (d + 1) * cp, :] = xs[d][...]
+
+    grad_out = tn(act[...], dprod[...]).astype(BF16)
+    for q in range(reps // tiles):
+        spot = place_of(h * (reps // tiles) + q, order_out) ^ mine_out
+        wires[0][spot] = grad_out[q * rows_out : (q + 1) * rows_out, :]
+    grad_in = tn(xcat[...], dpre[...]).astype(BF16)
+    line = pl.multiple_of(h * rows_in, rows_in)
+    for q in range(reps):
+        spot = place_of(q, order_in) ^ mine_in
+        wires[1][spot, pl.ds(line, rows_in), :] = grad_in[q * rows_in : (q + 1) * rows_in, :]
+
+    @pl.when(h == tiles - 1)
+    def _():
+        copies = []
+        half = wires[0].shape[0] // 2
+        rows = wires[0].shape[1]
+        for k in range(2):
+            for part in range(2):
+                if whole_at is None:
+                    target = wire_refs[2 * k + part]
+                else:
+                    place = pl.ds((2 * whole_at + k) * rows, rows)
+                    target = wire_refs[0].at[pl.ds(part * half, half), place]
+                copies.append(
+                    pltpu.make_async_copy(
+                        wires[k].at[pl.ds(part * half, half)], target, sems.at[2 * k + part]
+                    )
+                )
+        for copy in copies:
+            copy.start()
+        for copy in copies:
+            copy.wait()
+
+
+def halve_kernel(*refs, count):
+    for k in range(count):
+        mine, got, keep, rest = refs[k], refs[count + k], refs[2 * count + k], refs[3 * count + k]
+        half = keep.shape[0]
+        keep[...] = (mine[:half].astype(F32) + got[:half].astype(F32)).astype(BF16)
+        rest[...] = (mine[half:].astype(F32) + got[half:].astype(F32)).astype(BF16)
+
+
+def finish_kernel(*refs, layers, pairs, tiles, rows_in):
+    it = iter(refs)
+    ids = next(it)
+    parts = [[(next(it), next(it)) for _ in range(2)] for _ in range(pairs)]
+    joint = next(it), next(it)
+    grad_in, grad_out = next(it), next(it)
+    rows, tile = grad_out.shape[2:]
+    for layer in range(layers):
+        for j in range(pairs):
+            for side in range(2):
+                core = ids[1] if side == 0 else 1 - ids[1]
+                expert = core * pairs + j
+                if layer == 0:
+                    one, two = parts[j][0][side].at[0], parts[j][1][side].at[0]
+                else:
+                    one = joint[side].at[0, pl.ds(2 * j * rows, rows)]
+                    two = joint[side].at[0, pl.ds((2 * j + 1) * rows, rows)]
+                grad_out[layer, expert] = one[...].astype(F32)
+                for h in range(tiles):
+                    grad_in[layer, expert, :, h * tile : (h + 1) * tile] = two[
+                        h * rows_in : (h + 1) * rows_in, :
+                    ].astype(F32)
+
+
+def add_kernel(*refs):
+    a, b, outs = refs[0], refs[1], refs[2:]
+    for k, out in enumerate(outs):
+        one, two = (a, b) if len(a.shape) == 2 else (a.at[k], b.at[k])
+        out[...] = (one[...].astype(F32) + two[...].astype(F32)).astype(BF16)
+
+
+def dense_kernel(*refs, layers, width, experts):
+    it = iter(refs)
+    ids = next(it)
+    parts = [next(it), next(it)]
+    qkv, out, router = next(it), next(it), next(it)
+    norms = [next(it) for _ in range(4)]
+    tall = next(it)
+    half = parts[0].shape[1]
+    for layer in range(layers):
+        for side in range(2):
+            core = ids[1] if side == 0 else 1 - ids[1]
+            rows = pl.ds(pl.multiple_of(core * half, half), half)
+            part = parts[side].at[layer]
+            qkv[layer, rows, :] = part[:, 0 : 3 * width].astype(F32)
+            out[layer, rows, :] = part[:, 3 * width : 4 * width].astype(F32)
+            small = part[:, 4 * width :].astype(F32)
+            router[layer, rows, :] = small[:, 0:experts]
+            tall[rows, :] = small
+        flipped = tall[...].T
+        for k in range(4):
+            norms[k][layer : layer + 1, :] = flipped[experts + k : experts + k + 1, 0 : 2 * half]
 
 
 def backward_kernel(*refs, first, last, layer, n, per, cp, images, seq, experts):
@@ -398,7 +493,8 @@
     g1, b1, wqkv, wo, g2, wr = (next(it) for _ in range(6))
     if not first:
         row = next(it)
-    g_out, dense = next(it), next(it)
+    g_out = next(it)
+    dense = [next(it), next(it)]
     if not first:
         outs = take(it, n, per)
     d_cols, a_qkv, a_out, a_router, stats, flip, d_join = (next(it) for _ in range(7))
@@ -411,7 +507,6 @@
     i = pl.program_id(0)
     sp = middle_in.shape[1]
     width = middle_in.shape[2]
-    me = ids[0]
 
     @pl.when(i == 0)
     def _():
@@ -427,7 +522,7 @@
         else:
             rhs[...] = jnp.zeros(rhs.shape, BF16)
         for d in range(n):
-            base = lax.rem(me + d, n) * per
+            base = first_expert(ids, d, n, per)
             for j in range(per):
                 tail = back[d][j][cp - 16 : cp, 0:WIDE].astype(F32)
                 line = jnp.sum(jnp.where(iota(tail.shape, 0) == 15, tail, 0.0), axis=0, keepdims=True)
@@ -513,11 +608,21 @@
     @pl.when(i == images - 1)
     def _():
         if not first:
-            spread_rows(me, row, rhs, outs, n, per, cp, width, 0)
+            spread_rows(ids, row, rhs, outs, n, per, cp, width, 0)
         flip[experts : experts + 8, :] = stats[...]
-        dense[:, 0 : 3 * width] = a_qkv[...].astype(BF16)
-        dense[:, 3 * width : 4 * width] = a_out[...].astype(BF16)
-        dense[:, 4 * width :] = (a_router[...] + flip[...].T).astype(BF16)
+        a_router[...] += flip[...].T
+        half = dense[0].shape[1]
+        for core in range(2):
+
+            @pl.when(ids[1] == core)
+            def _():
+                for side in range(n // 2):
+                    spot = ids[0] ^ side
+                    for target, c in ((dense[0], core), (dense[1], 1 - core)):
+                        rows = slice((2 * side + c) * half, (2 * side + c + 1) * half)
+                        target[spot, :, 0 : 3 * width] = a_qkv[rows, :].astype(BF16)
+                        target[spot, :, 3 * width : 4 * width] = a_out[rows, :].astype(BF16)
+                        target[spot, :, 4 * width :] = a_router[rows, :].astype(BF16)
 
 
 def spec(shape, index):
@@ -551,50 +656,90 @@
     return pl.BlockSpec((1,) + tuple(array.shape[1:]), lambda *_: (layer,) + rest)
 
 
-def pairs_along(stride, length, total, valid, step):
-    pairs = []
-    for source in range(total):
-        spot = (source // stride) % length
-        target = spot + step
-        if 0 <= target < length and valid(spot):
-            pairs.append((source, source + step * stride))
-    return pairs
-
-
-def line_sum(parts, axis, stride, length, total, spot):
-    def part(at):
-        return lax.dynamic_index_in_dim(parts, jnp.clip(at, 0, length - 1), 0, keepdims=False).astype(
-            F32
-        )
-
-    if length == 2:
-        swap = pairs_along(stride, length, total, lambda s: True, 1) + pairs_along(
-            stride, length, total, lambda s: True, -1
-        )
-        got = lax.ppermute(part(1 - spot).astype(BF16), axis, swap)
-        return part(spot) + got.astype(F32)
-    rising = part(length - 1 + spot)
-    falling = part(1 - length + spot)
-    for step in range(1, length):
-        up = pairs_along(stride, length, total, lambda s: s <= step - 1, 1)
-        down = pairs_along(stride, length, total, lambda s: length - 1 - s <= step - 1, -1)
-        got_up = lax.ppermute(rising.astype(BF16), axis, up).astype(F32)
-        got_down = lax.ppermute(falling.astype(BF16), axis, down).astype(F32)
-        if step < length - 1:
-            rising = got_up + part(length - step - 1 + spot)
-            falling = got_down + part(step + 1 - length + spot)
-    return part(spot) + got_up + got_down
-
-
-def expert_sum(wire, rep_sizes):
-    zs, xs, cores = rep_sizes
-    total = zs * xs * cores
-    index = lax.axis_index("rep")
-    core_swap = [(r, r ^ 1) for r in range(total)]
-    got = lax.ppermute(wire[1], "rep", core_swap)
-    both = (wire[0].astype(F32) + got.astype(F32)).astype(BF16)
-    along_x = line_sum(both, "rep", cores, xs, total, (index // cores) % xs).astype(BF16)
-    return line_sum(along_x, "rep", cores * xs, zs, total, index // (cores * xs))
+def swap(values, axis, distance, total):
+    return lax.ppermute(values, axis, [(r, r ^ distance) for r in range(total)])
+
+
+class Line:
+    def __init__(self):
+        self.last = None
+
+    def __call__(
+        self, kernel, args, in_specs, out_specs, out_shape, grid, scratch=(), price=None, name=None, ahead=0, carry=(), after=(), aliases=None
+    ):
+        anywhere = pl.BlockSpec(memory_space=pl.ANY)
+        args, in_specs = list(args), list(in_specs)
+        out_specs, out_shape = list(out_specs), list(out_shape)
+        spot, spot_out = len(args), len(args) + len(out_specs)
+        aliases = dict(aliases or {})
+        aliases.update({spot + k: len(out_specs) + k for k in range(len(carry))})
+        known = self.last is None or any(self.last is x for x in list(args) + list(carry))
+        unread = list(carry) + list(after) + ([] if known else [self.last])
+        args += unread
+        in_specs += [anywhere] * len(unread)
+        out_specs += [anywhere] * len(carry)
+        out_shape += [shape_of(c.shape, c.dtype) for c in carry]
+
+        def body(*refs):
+            outs_at = spot + len(unread)
+            outs_end = outs_at + spot_out - spot
+            kernel(*refs[:spot], *refs[outs_at:outs_end], *refs[outs_end + len(carry) :])
+
+        out = pl.pallas_call(
+            body,
+            grid_spec=pltpu.PrefetchScalarGridSpec(
+                num_scalar_prefetch=ahead,
+                grid=grid,
+                in_specs=in_specs,
+                out_specs=list(out_specs),
+                scratch_shapes=list(scratch),
+            ),
+            out_shape=list(out_shape),
+            input_output_aliases=aliases,
+            compiler_params=pltpu.CompilerParams(
+                vmem_limit_bytes=VMEM_LIMIT, dimension_semantics=("arbitrary",)
+            ),
+            cost_estimate=price,
+            name=name,
+        )(*args)
+        out = list(out)
+        self.last = out[0]
+        return out
+
+
+def halve(line, mine, got, carry=(), after=()):
+    count = len(mine)
+    parts = [shape_of((m.shape[0] // 2,) + tuple(m.shape[1:]), BF16) for m in mine]
+    size = sum(m.size for m in mine)
+    out = line(
+        partial(halve_kernel, count=count),
+        list(mine) + list(got),
+        [whole(m) for m in list(mine) + list(got)],
+        [whole(p) for p in parts + parts],
+        parts + parts,
+        (1,),
+        price=cost(size, 6 * size),
+        name="halve",
+        carry=carry,
+        after=after,
+    )
+    return out[:count], out[count : 2 * count], out[2 * count :]
+
+
+def add(line, a, b):
+    count = a.shape[0] if len(a.shape) == 3 else 1
+    part = shape_of(a.shape[-2:], BF16)
+    out = line(
+        add_kernel,
+        [a, b],
+        [whole(a), whole(b)],
+        [whole(part)] * count,
+        [part] * count,
+        (1,),
+        price=cost(a.size, 6 * a.size),
+        name="add",
+    )
+    return out if len(a.shape) == 3 else out[0]
 
 
 def local(
@@ -611,55 +756,63 @@
     routes,
     priority,
     cotangent,
-    n,
+    n_exp,
     reps,
 ):
     images, seq, width = tokens.shape
     tok_count = images * seq
-    layers, per, _, hidden = w_in.shape
-    experts = n * per
+    layers, local_experts, _, hidden = w_in.shape
+    experts = n_exp * local_experts
+    zs, cores = 4, 2
+    xs = reps // (zs * cores)
+    n = n_exp * cores
+    per = local_experts // cores
     cap = 2 * tok_count // experts
     cp = round_up(cap + 2, 16)
     sp = round_up(seq, 16)
-    zs, cores = 4, 2
-    xs = reps // (zs * cores)
-    rep_sizes = (zs, xs, cores)
     tiles = zs
     tile = hidden // tiles
     rows_in = width // reps
     rows_out = hidden // reps
-    rows = tiles * rows_in + rows_out
-    me = lax.axis_index("exp")
-    core = lax.axis_index("rep") % cores
-    ids = jnp.stack([me, core]).astype(jnp.int32)
+    bits = reps.bit_length() - 1
+    x_bits = list(range(1, bits - 2))
+    z_bits = [bits - 2, bits - 1]
+    me_rep = lax.axis_index("rep")
+    me_exp = lax.axis_index("exp")
+    core = me_rep % cores
+    x_first = x_bits + z_bits + [0]
+    z_first = z_bits[:1] + x_bits + z_bits[1:] + [0]
+    ids = jnp.stack(
+        [me_exp, core, place_of(me_rep, x_first), place_of(me_rep, z_first)]
+    ).astype(jnp.int32)
     router_wide = jnp.pad(w_router, ((0, 0), (0, 0), (0, LANES - experts)))
-    params = pltpu.CompilerParams(
-        vmem_limit_bytes=VMEM_LIMIT, dimension_semantics=("arbitrary",)
-    )
     dims = dict(n=n, per=per, cp=cp)
 
     lanes = round_up(tok_count, LANES)
-    row, col = pl.pallas_call(
+    line = Line()
+    row, col = line(
         partial(route_kernel, cap=cap, images=images, seq=seq, **dims),
-        grid=(layers,),
-        in_specs=[smem()] + [spec((1, tok_count, 2), lambda l: (l, 0, 0))] * 2,
-        out_specs=[
+        [ids, routes, priority],
+        [smem()] + [spec((1, tok_count, 2), lambda l: (l, 0, 0))] * 2,
+        [
             spec((1, 8, images * WIDE), lambda l: (l, 0, 0)),
             spec((1, images, sp, LANES), lambda l: (l, 0, 0, 0)),
         ],
-        out_shape=[
+        [
             shape_of((layers, 8, images * WIDE), jnp.int32),
             shape_of((layers, images, sp, LANES), jnp.int32),
         ],
-        scratch_shapes=[pltpu.VMEM((lanes, LANES), jnp.int32), pltpu.VMEM((LANES, WIDE), jnp.int32)],
-        compiler_params=params,
-        cost_estimate=cost(4e7, 1e6),
-        name="route",
-    )(ids, routes, priority)
+        (layers,),
+        [pltpu.VMEM((lanes, LANES), jnp.int32), pltpu.VMEM((LANES, WIDE), jnp.int32)],
+        cost(4e7, 1e6),
+        "route",
+    )
 
     slot_shape = shape_of((cp, width), BF16)
     slot_shapes = [slot_shape] * (n * per)
     slot_specs = [whole(slot_shape)] * (n * per)
+    joint_shapes = [shape_of((per * cp, width), BF16)] * n
+    joint_specs = [whole(joint_shapes[0])] * n
 
     def nested(flat):
         return [list(flat[d * per : (d + 1) * per]) for d in range(n)]
@@ -667,19 +820,31 @@
     def flat_of(lists):
         return [part for group in lists for part in group]
 
-    def send(lists):
+    axes = ("rep", "exp")
+
+    def shifted(d, back):
+        pairs = []
+        for r in range(reps):
+            for y in range(n_exp):
+                there = (r ^ (d % 2)) * n_exp + (y + d // 2) % n_exp
+                here = r * n_exp + y
+                pairs.append((there, here) if back else (here, there))
+        return pairs
+
+    def move(lists, back):
         result = [lists[0]]
         for d in range(1, n):
-            pairs = [(s, (s + d) % n) for s in range(n)]
-            result.append([lax.ppermute(part, "exp", pairs) for part in lists[d]])
+            result.append([lax.ppermute(part, axes, shifted(d, back)) for part in lists[d]])
         return result
 
+    def go_back(part, d):
+        return part if d == 0 else lax.ppermute(part, axes, shifted(d, True))
+
+    def send(lists):
+        return move(lists, False)
+
     def send_back(lists):
-        result = [lists[0]]
-        for d in range(1, n):
-            pairs = [(s, (s - d) % n) for s in range(n)]
-            result.append([lax.ppermute(part, "exp", pairs) for part in lists[d]])
-        return result
+        return move(lists, True)
 
     def col_spec(layer):
         return spec((1, 1, sp, LANES), lambda i: (layer, i, 0, 0))
@@ -687,20 +852,22 @@
     row_spec_of = lambda layer: spec((1, 8, images * WIDE), lambda *_: (layer, 0, 0))
 
     top = layers - 1
-    g_rows = nested(
-        pl.pallas_call(
-            partial(cotangent_kernel, images=images, seq=seq, **dims),
-            grid=(1,),
-            in_specs=[smem(), whole(cotangent), row_spec_of(top)],
-            out_specs=slot_specs,
-            out_shape=slot_shapes,
-            scratch_shapes=[pltpu.VMEM((images * WIDE, width), BF16)],
-            compiler_params=params,
-            cost_estimate=cost(4 * n * per * cp * images * WIDE * width // 2, 4e6),
-            name="spread_cotangent",
-        )(ids, cotangent, row)
-    )
-    g_rows = send(g_rows)
+
+    def spread_cotangent():
+        return [
+            [part]
+            for part in line(
+                partial(cotangent_kernel, images=images, seq=seq, **dims),
+                [ids, cotangent, row],
+                [smem(), whole(cotangent), row_spec_of(top)],
+                joint_specs,
+                joint_shapes,
+                (1,),
+                [pltpu.VMEM((images * WIDE, width), BF16)],
+                cost(2 * n * per * cp * images * WIDE * width, 4e6),
+                "spread_cotangent",
+            )
+        ]
 
     def run_forward(layer, previous):
         first = layer == 0
@@ -739,7 +906,7 @@
         scratch = [pltpu.VMEM((images * WIDE, width + 2 * LANES), BF16)]
         if first:
             scratch.append(pltpu.VMEM((sp, width), F32))
-        out = pl.pallas_call(
+        out = line(
             partial(
                 forward_kernel,
                 first=first,
@@ -749,130 +916,185 @@
                 experts=experts,
                 **dims,
             ),
-            grid=(images,),
-            in_specs=specs,
-            out_specs=out_specs,
-            out_shape=shapes + slot_shapes,
-            scratch_shapes=scratch,
-            compiler_params=params,
-            cost_estimate=cost(6e9, 2e7, 1e6),
-            name="forward",
-        )(*args)
-        out = list(out)
+            args,
+            specs,
+            out_specs,
+            shapes + slot_shapes,
+            (images,),
+            scratch,
+            cost(6e9, 2e7, 1e6),
+            "forward",
+        )
         state = tokens if first else out.pop(0)
         return state, out[:7], nested(out[7:])
 
+    any_spec = pl.BlockSpec(memory_space=pl.ANY)
+
+    def rows_of(lists, j, args, specs):
+        for d in range(n):
+            array = lists[d][j] if len(lists[d]) > 1 else lists[d][0]
+            at = 0 if len(lists[d]) > 1 else j
+            args.append(array)
+            specs.append(spec((cp, width), lambda *_, at=at: (at, 0)))
+
     act_shape = shape_of((n * cp, hidden), BF16)
-    wire_shape = shape_of((cores, xs, zs, rows, width), BF16)
-
-    def run_expert(layer, j, x, g, saved, forward, backward):
-        args = [ids] + [x[d][j] for d in range(n)]
-        specs = [smem()] + [whole(slot_shape)] * n
-        tile_spec = spec((n * cp, tile), lambda h: (0, h))
+    act_spec = spec((n * cp, tile), lambda h, *_: (0, h))
+    cat_shape = shape_of((n * cp, width), BF16)
+
+    def run_expert(layer, j, x, g, made, produce, backward, earlier=()):
+        args, specs = [ids], []
+        rows_of(x, j, args, specs)
         if backward:
-            args += [g[d][j] for d in range(n)]
+            rows_of(g, j, args, specs)
+            if not produce:
+                rows_of(made, j, args, specs)
+        for parts in earlier:
+            args += parts
             specs += [whole(slot_shape)] * n
-            if not forward:
-                made, act, slope = saved
-                args += list(made) + [act, slope]
-                specs += [whole(slot_shape)] * n + [tile_spec] * 2
         args += [w_in, w_out]
         specs += [
-            spec((1, 1, width, tile), lambda h: (layer, j, 0, h)),
-            spec((1, 1, tile, width), lambda h: (layer, j, h, 0)),
+            spec((1, 1, width, tile), lambda h, who: (layer, who[1] * per + j, 0, h)),
+            spec((1, 1, tile, width), lambda h, who: (layer, who[1] * per + j, h, 0)),
         ]
         shapes = []
         out_specs = []
         scratch = [pltpu.VMEM((n * cp, width), BF16)]
-        if forward:
-            shapes += [slot_shape] * n
-            out_specs += [whole(slot_shape)] * n
-            if not backward:
-                shapes += [act_shape] * 2
-                out_specs += [tile_spec] * 2
+        if not backward:
+            scratch.append(pltpu.VMEM((n * cp, tile), BF16))
+        if produce:
+            made_shape = shape_of(((1 + len(earlier)) * cp, width), BF16)
+            shapes += [made_shape] * n
+            out_specs += [whole(made_shape)] * n
             scratch += [pltpu.VMEM((n * cp, width), F32)]
         if backward:
-            shapes += [slot_shape] * n + [wire_shape]
-            out_specs += [whole(slot_shape)] * n + [whole(wire_shape)]
+            shapes += [slot_shape] * n + [act_shape] * 2 + [cat_shape]
+            out_specs += [whole(slot_shape)] * n + [act_spec] * 2 + [whole(cat_shape)]
             scratch += [pltpu.VMEM((n * cp, width), BF16), pltpu.VMEM((n * cp, width), F32)]
-        matmuls = (2 if forward else 0) + (4 if backward else 0)
-        return list(
-            pl.pallas_call(
-                partial(
-                    expert_kernel,
-                    n=n,
-                    cp=cp,
-                    tiles=tiles,
-                    forward=forward,
-                    backward=backward,
-                    sizes=(zs, xs, cores, rows_in, rows_out),
-                ),
-                grid=(tiles,),
-                in_specs=specs,
-                out_specs=out_specs,
-                out_shape=shapes,
-                scratch_shapes=scratch,
-                compiler_params=params,
-                cost_estimate=cost(2 * matmuls * n * cp * width * hidden, 6e6, 2e6 if forward else 0),
-                name="expert",
-            )(*args)
+        matmuls = (2 if produce else 1) + (2 if backward else 0)
+        out = line(
+            partial(
+                expert_kernel,
+                n=n,
+                cp=cp,
+                tiles=tiles,
+                produce=produce,
+                backward=backward,
+                joined=len(earlier),
+            ),
+            args,
+            specs,
+            out_specs,
+            shapes,
+            (tiles,),
+            scratch,
+            cost(2 * matmuls * n * cp * width * hidden, 6e6, 2e6),
+            "expert",
+            1,
         )
-
-    kept = []
-    previous = None
-    for layer in range(layers):
-        state, cached, rows_sent = run_forward(layer, previous)
-        x = send(rows_sent)
-        made = [[None] * per for _ in range(n)]
-        d_rows = [[None] * per for _ in range(n)]
-        saved = []
-        wires = []
-        for j in range(per):
-            if layer < top:
-                out = run_expert(layer, j, x, None, None, True, False)
-                saved.append((out[:n], out[n], out[n + 1]))
-            else:
-                out = run_expert(layer, j, x, g_rows, None, True, True)
-                wires.append(out[2 * n])
-                for d in range(n):
-                    d_rows[d][j] = out[n + d]
-            for d in range(n):
-                made[d][j] = out[d]
-        if layer == top:
-            d_back = send_back(d_rows)
-        back = send_back(made)
-        kept.append((state, cached, x, saved))
-        previous = (cached[3], cached[6], back)
-
-    middle, gate, back = previous
-    block_out = pl.pallas_call(
-        partial(out_kernel, seq=seq, **dims),
-        grid=(images,),
-        in_specs=[per_image(middle.shape), per_image(gate.shape), col_spec(top)] + slot_specs,
-        out_specs=per_image(tokens.shape),
-        out_shape=shape_of(tokens.shape, F32),
-        compiler_params=params,
-        cost_estimate=cost(2 * images * sp * n * per * cp * width, 6e6),
-        name="block_out",
-    )(middle, gate, col, *flat_of(back))
-
-    dense = [None] * layers
-    summed = [None] * layers
-    grad = cotangent
-    for layer in reversed(range(layers)):
+        if backward:
+            return out[:-3], out[-3:]
+        return out, None
+
+    def run_weights(j, x, saved, joint=False, before=None, carry=(), after=()):
+        args, specs = [ids], []
+        rows_of(x, j, args, specs)
+        args += saved
+        specs += [act_spec] * 2 + [whole(cat_shape)]
+        aliases = {}
+        if before is not None:
+            aliases = {len(args): 0}
+            args.append(before)
+            specs.append(any_spec)
+        order_in = z_first if j == 0 else x_first
+        chunk_out = (reps, rows_out, width)
+        chunk_in = (reps, tiles * rows_in, tile)
+        if joint:
+            natural = list(range(bits - 1, -1, -1))
+            wire = (reps, rows_in, rows_out, natural, natural, 1, 1, j)
+            shapes = [shape_of((reps, 2 * per * rows_out, width), BF16)]
+        else:
+            wire = (reps, rows_in, rows_out, x_first, order_in, 2, 3 if j == 0 else 2, None)
+            shapes = [shape_of((c[0] // 2,) + c[1:], BF16) for c in (chunk_out,) * 2 + (chunk_in,) * 2]
+        out = line(
+            partial(
+                weight_kernel, n=n, cp=cp, tiles=tiles, wire=wire, follows=before is not None
+            ),
+            args,
+            specs,
+            [any_spec] * len(shapes),
+            shapes,
+            (tiles,),
+            [
+                pltpu.VMEM((n * cp, width), BF16),
+                pltpu.VMEM(chunk_out, BF16),
+                pltpu.VMEM(chunk_in, BF16),
+                pltpu.SemaphoreType.DMA((4,)),
+            ],
+            cost(4 * n * cp * width * hidden, 6e6, 0),
+            "weights",
+            1,
+            carry,
+            after,
+            aliases,
+        )
+        if joint:
+            return out[0], out[1:]
+        chunks = [
+            dict(mine=out[0], other=out[1], order=x_first, at=0),
+            dict(mine=out[2], other=out[3], order=order_in, at=0),
+        ]
+        return chunks, out[4:]
+
+    def dense_steps(mine, other, result):
+        parts = add(line, mine, swap(other, "rep", 1, reps))
+        yield
+        total = parts[0]
+        for side in range(1, n_exp):
+            total = add(line, total, swap(parts[side], "exp", side, n_exp))
+            yield
+        result.append(total)
+        while True:
+            yield
+
+    def dense_over_chips(totals):
+        chips = reps // cores
+        parts = jnp.stack([t.reshape(chips, t.shape[0] // chips, t.shape[1]) for t in totals], axis=1)
+        parts = lax.all_to_all(
+            parts, "rep", split_axis=0, concat_axis=0, axis_index_groups=groups, tiled=True
+        )
+        share = jnp.sum(parts.astype(F32), axis=0, keepdims=True).astype(BF16)
+        parts = lax.all_to_all(
+            jnp.broadcast_to(share, parts.shape),
+            "rep",
+            split_axis=0,
+            concat_axis=0,
+            axis_index_groups=groups,
+            tiled=True,
+        )
+        full = parts.transpose(1, 0, 2, 3).reshape(layers, totals[0].shape[0], totals[0].shape[1])
+        return full, swap(full, "rep", 1, reps)
+
+    def step(process):
+        next(process, None)
+
+    def run_out(previous):
+        middle, gate, back = previous
+        back = flat_of(back)
+        return line(
+            partial(out_kernel, seq=seq, **dims),
+            [middle, gate, col] + back,
+            [per_image(middle.shape), per_image(gate.shape), col_spec(top)] + [whole(p) for p in back],
+            [per_image(tokens.shape)],
+            [shape_of(tokens.shape, F32)],
+            (images,),
+            (),
+            cost(2 * images * sp * n * per * cp * width, 6e6),
+            "block_out",
+        )[0]
+
+    def run_backward(layer, grad, state, cached, d_back, carry):
         first = layer == 0
         last = layer == top
-        state, cached, x, saved = kept[layer]
-        if not last:
-            d_rows = [[None] * per for _ in range(n)]
-            wires = []
-            for j in range(per):
-                out = run_expert(layer, j, x, g_rows, saved[j], False, True)
-                wires.append(out[n])
-                for d in range(n):
-                    d_rows[d][j] = out[d]
-            d_back = send_back(d_rows)
-        summed[layer] = [expert_sum(wire, rep_sizes) for wire in wires]
         joined, probs, attended, middle, moe_in, router, gate = cached
         args = [ids, grad, state, joined, probs, attended, middle, moe_in, router, col]
         specs = [smem()] + [per_image(a.shape) for a in args[1:-1]] + [col_spec(layer)]
@@ -887,10 +1109,10 @@
             whole(ln2_gain),
             of_layer(router_wide, layer),
         ]
-        dense_shape = shape_of((width, 4 * width + LANES), BF16)
+        dense_shape = shape_of((n_exp, width // n, 4 * width + LANES), BF16)
         grad_shape = tokens.shape if first else (images, sp, width)
-        shapes = [shape_of(grad_shape, F32), dense_shape]
-        out_specs = [per_image(grad_shape), whole(dense_shape)]
+        shapes = [shape_of(grad_shape, F32), dense_shape, dense_shape]
+        out_specs = [per_image(grad_shape), whole(dense_shape), whole(dense_shape)]
         scratch = [
             pltpu.VMEM((n, per, cp, LANES), BF16),
             pltpu.VMEM((width, 3 * width), F32),
@@ -910,7 +1132,7 @@
             shapes += slot_shapes
             out_specs += slot_specs
             scratch.append(pltpu.VMEM((images * WIDE, width), BF16))
-        out = pl.pallas_call(
+        out = line(
             partial(
                 backward_kernel,
                 first=first,
@@ -921,44 +1143,150 @@
                 experts=experts,
                 **dims,
             ),
-            grid=(images,),
-            in_specs=specs,
-            out_specs=out_specs,
-            out_shape=shapes,
-            scratch_shapes=scratch,
-            compiler_params=params,
-            cost_estimate=cost(1.2e10, 3e7, 0),
-            name="backward",
-        )(*args)
-        grad = out[0]
-        dense[layer] = out[1]
-        if not first:
-            g_rows = send(nested(out[2:]))
-
-    stacked = jnp.stack(dense)
-    shares = lax.psum_scatter(stacked, "exp", scatter_dimension=1, tiled=True)
-    shares = lax.psum(shares, "rep").astype(F32)
-    at = 4 * width
-    columns = lambda k: shares[:, :, at + experts + k]
-    grad_in = []
-    grad_out = []
+            args,
+            specs,
+            out_specs,
+            shapes,
+            (images,),
+            scratch,
+            cost(1.2e10, 3e7, 0),
+            "backward",
+            carry=carry,
+        )
+        count = len(out) - len(carry)
+        return out[0], out[1:3], nested(out[3:count]), out[count:]
+
+    def add_up(chunks, carry=(), after=()):
+        chunks = [c for c in chunks if c["at"] < bits - 1]
+        if not chunks:
+            return list(carry)
+        got = [swap(c["other"], "rep", 1 << c["order"][c["at"]], reps) for c in chunks]
+        keep, rest, carried = halve(line, [c["mine"] for c in chunks], got, carry, after)
+        for c, mine, other in zip(chunks, keep, rest):
+            c["mine"], c["other"], c["at"] = mine, other, c["at"] + 1
+            if c["at"] == bits - 1:
+                c["other"] = swap(other, "rep", 1 << c["order"][-1], reps)
+        return carried
+
+    def later(chunks, carried):
+        for c, other in zip(chunks, carried):
+            c["other"] = other
+
+    kept = []
+    previous = None
     for layer in range(layers):
-        for total in summed[layer]:
-            part = total[: tiles * rows_in].reshape(tiles, rows_in, tile)
-            grad_in.append(part.transpose(1, 0, 2).reshape(rows_in, hidden))
-            grad_out.append(total[tiles * rows_in :])
-    grad_in = jnp.stack(grad_in).reshape(layers, per, rows_in, hidden)
-    grad_out = jnp.stack(grad_out).reshape(layers, per, rows_out, width)
+        if layer == top:
+            g_rows = send(spread_cotangent())
+        state, cached, rows_sent = run_forward(layer, previous)
+        x = send(rows_sent)
+        made = [[] for _ in range(n)]
+        if layer < top:
+            for j in range(per):
+                out, _ = run_expert(layer, j, x, None, None, True, False)
+                for d in range(n):
+                    made[d].append(out[d])
+            previous = (cached[3], cached[6], send_back(made))
+        kept.append((state, cached, x, made))
+
+    state, cached, x, _ = kept[top]
+    outs, saved = [], []
+    d_back = [[] for _ in range(n)]
+    for j in range(per):
+        earlier = [o[:n] for o in outs] if j == per - 1 else ()
+        out, kept_rows = run_expert(top, j, x, g_rows, None, True, True, earlier)
+        outs.append(out)
+        saved.append(kept_rows)
+        for d, part in enumerate(out[n : 2 * n]):
+            d_back[d].append(go_back(part, d))
+    wire = None
+    for j in range(per):
+        carry = outs[-1][:n] if j == per - 1 else ()
+        wire, made_top = run_weights(j, x, saved[j], True, wire, carry)
+    back_top = send_back([[part] for part in made_top])
+    groups = [[r for r in range(reps) if r % cores == c] for c in range(cores)]
+    share = lax.psum_scatter(
+        wire, "rep", scatter_dimension=0, axis_index_groups=groups, tiled=True
+    )
+    grad, parts, g_rows, _ = run_backward(top, cotangent, state, cached, d_back, ())
+    g_rows = send(g_rows)
+    dense = [[] for _ in range(layers)]
+    flow_top = dense_steps(parts[0], parts[1], dense[top])
+    block_out = run_out((cached[3], cached[6], back_top))
+
+    state, cached, x, made = kept[0]
+    d_back = [[] for _ in range(n)]
+    saved = []
+    for j in range(per):
+        out, kept_rows = run_expert(0, j, x, g_rows, made, False, True)
+        saved.append(kept_rows)
+        for k in range(n):
+            d_back[k].append(go_back(out[k], k))
+        if j == 0:
+            step(flow_top)
+    sums = []
+    for j in range(per):
+        new, _ = run_weights(j, x, saved[j])
+        sums += new
+        if j == 0:
+            step(flow_top)
+    a, b, c, d = sums
+    grad, parts, _, carried = run_backward(0, grad, state, cached, d_back, [d["other"]])
+    later([d], carried)
+    flow = dense_steps(parts[0], parts[1], dense[0])
+    while not dense[top]:
+        step(flow_top)
+    step(flow)
+    add_up([a, b])
+    while not dense[0]:
+        step(flow)
+    halves = list(dense_over_chips([d[0] for d in dense]))
+    for group in ((c,), (a,), (d,), (b, c), (a,), (d,), (c, b), (d,)):
+        add_up(group)
+    for _ in range(bits):
+        add_up([a, b, c, d])
+    top_mine = share[: share.shape[0] // 2]
+    top_other = swap(share[share.shape[0] // 2 :], "rep", 1, reps)
+    pieces = [part for k in sums for part in (k["mine"], k["other"])] + [top_mine, top_other]
+    in_shape = shape_of((layers, local_experts, rows_in, hidden), F32)
+    out_shape = shape_of((layers, local_experts, rows_out, width), F32)
+    grad_in, grad_out = line(
+        partial(finish_kernel, layers=layers, pairs=per, tiles=tiles, rows_in=rows_in),
+        [ids] + pieces,
+        [smem()] + [whole(p) for p in pieces],
+        [whole(in_shape), whole(out_shape)],
+        [in_shape, out_shape],
+        (1,),
+        (),
+        cost(1e6, 6e6),
+        "finish",
+    )
+    rows = width // n_exp
+    dense_shapes = [
+        shape_of((layers, rows, 3 * width), F32),
+        shape_of((layers, rows, width), F32),
+        shape_of((layers, rows, experts), F32),
+    ] + [shape_of((layers, rows), F32)] * 4
+    qkv, attn_out, router, gain1, bias1, gain2, bias2 = line(
+        partial(dense_kernel, layers=layers, width=width, experts=experts),
+        [ids] + halves,
+        [smem()] + [whole(p) for p in halves],
+        [whole(s) for s in dense_shapes],
+        dense_shapes,
+        (1,),
+        [pltpu.VMEM((WIDE, LANES), F32)],
+        cost(1e6, 6e6),
+        "finish_dense",
+    )
     return (
         block_out,
         grad,
-        columns(0),
-        columns(1),
-        shares[:, :, 0 : 3 * width],
-        shares[:, :, 3 * width : 4 * width],
-        columns(2),
-        columns(3),
-        shares[:, :, at : at + experts],
+        gain1,
+        bias1,
+        qkv,
+        attn_out,
+        gain2,
+        bias2,
+        router,
         grad_in,
         grad_out,
     )
@@ -966,7 +1294,7 @@
 
 def solution(mesh):
     return jax.shard_map(
-        partial(local, n=mesh.shape["exp"], reps=mesh.shape["rep"]),
+        partial(local, n_exp=mesh.shape["exp"], reps=mesh.shape["rep"]),
         mesh=mesh,
         in_specs=(
             P(("rep", "exp"), None, None),

time: 815 us -> 553 us (0.68)
  waiting for transfers between devices: 246 us -> 138 us
  starting transfers between devices: 169 us -> 61.5 us
  local copies, waits for them, and re-layouts: 77.7 us -> 32.3 us
  other arithmetic: 45 us -> 1.91 us
  blocking collectives: 0 us -> 32.2 us
  Pallas kernels: 249 us -> 263 us
    ppermute x96 -> x64, starting transfers between devices: 169 us -> 57.9 us  [the longest x22 24.2 us: swap(): return lax.ppermute(values, axis, [(r, r ^ distance) for r in range(total)])]
    psum x1 -> x0, waiting for transfers between devices: 94.2 us -> none  [local(): shares = lax.psum(shares, 'rep').astype(F32)]
    convert_element_type x33 -> x0, other arithmetic: 33.1 us -> none  [the longest x8 14.8 us: expert_sum(): both = (wire[0].astype(F32) + got.astype(F32)).astype(BF16)]
    all_to_all x0 -> x1, blocking collectives: none -> 32.2 us  [dense_over_chips(): lax.all_to_all(parts, 'rep', split_axis=0, concat_axis=0, axis_index_grou...]
    squeeze x24 -> x0, local copies, waits for them, and re-layouts: 23.2 us -> none  [the longest x8 20.3 us: expert_sum(): got = lax.ppermute(wire[1], 'rep', core_swap)]
    ppermute x96 -> x64, waiting for transfers between devices: 152 us -> 138 us  [the longest x22 93.9 us: swap(): return lax.ppermute(values, axis, [(r, r ^ distance) for r in range(total)])]
    pallas_call x19 -> x32, Pallas kernels: 249 us -> 263 us  [__call__(): pl.pallas_call(body, grid_spec=pltpu.PrefetchScalarGridSpec(num_scalar_pr...]
    another operation x10 -> x0, local copies, waits for them, and re-layouts: 11.7 us -> none  [the longest x9 10.9 us: local(): grad_in = jnp.stack(grad_in).reshape(layers, per, rows_in, hidden)]
  transfers between devices with their start and end apart: 98 -> 66, of which waited for: 16 -> 19; matrix products, arithmetic and copies ran while one was open for 12% -> 2% of each run, Pallas kernels for 28% -> 37%
where the time goes in v2:
time: 553 us; the launch traced here: 543 us
  Pallas kernels  263 us (48%)
  waiting for transfers between devices  138 us (25%)
  starting transfers between devices  61.5 us (11%)
  local copies, waits for them, and re-layouts  32.3 us (6%)
  blocking collectives  32.2 us (6%)
  between operations  15.2 us (3%)
    pallas_call x32, Pallas kernels, __call__(): pl.pallas_call(body, grid_spec=pltpu.PrefetchScalarGridSpec(num_scalar_pr...  263 us
    ppermute x22, waiting for transfers between devices, swap(): return lax.ppermute(values, axis, [(r, r ^ distance) for r in range(total)])  93.9 us
    all_to_all x1, blocking collectives, dense_over_chips(): lax.all_to_all(parts, 'rep', split_axis=0, concat_axis=0, axis_index_grou...  32.2 us
    unnamed x158, local copies, waits for them, and re-layouts  28.2 us
    ppermute x30, waiting for transfers between devices, move(): lax.ppermute(part, axes, shifted(d, back))  27.4 us
    ppermute x22, starting transfers between devices, swap(): return lax.ppermute(values, axis, [(r, r ^ distance) for r in range(total)])  24.2 us
    ppermute x30, starting transfers between devices, move(): lax.ppermute(part, axes, shifted(d, back))  23.8 us
    ppermute x12, waiting for transfers between devices, go_back(): return part if d == 0 else lax.ppermute(part, axes, shifted(d, True))  16.3 us
  transfers between devices with their start and end apart: 66, of which 19 were waited for; matrix products, arithmetic and copies ran while one was open for 2% of the time, Pallas kernels for 37%

profile of v2, /device:TPU:0, one launch (start us, length us, event | category | flops | bytes accessed | tf_op | source)
XLA Modules:
  0.0 543.3 jit_solution(10076925717351137429)
XLA Ops:
  15.1 6.8 %route.1 = (s32[2,8,1024]{2,1,0:T(8,128)}, s32[2,4,208,128]{3,2,1,0:T(8,128)}) custom-call(s32[4]{0:T(128)} %pad_add_fusion.refs_0_, s32[2,788,2]{2,1,0:T(8,128)} %copy.41.refs_1_, s32[2,788,2]{2,1,0:T(8,128)} %copy.42.refs_2_), custom_call_target="tpu_custom_call" | custom-call | flops 40000000 | bytes 1000000 | tf_op jit(solution)/shard_map/route/pallas_call | solution.py:688
  21.9 17.2 %forward.2 = (bf16[4,208,1536]{2,1,0:T(8,128)(2,1)}, bf16[4,8,208,208]{3,2,1,0:T(8,128)(2,1)}, bf16[4,208,512]{2,1,0:T(8,128)(2,1)}, f32[4,208,512]{2,1,0:T(8,12...) custom-call(s32[4]{0:T(128)} %pad_add_fusion.refs_0_, ...), custom_call_target="tpu_custom_call" | custom-call | flops 6000000000 | bytes 20000000 | tf_op jit(solution)/shard_map/forward/pallas_call | solution.py:688
  44.5 4.2 collective-permute-done.1.refs_3_
  48.6 4.1 collective-permute-done.2.refs_4_
  53.4 7.9 %expert.6 = (bf16[208,512]{1,0:T(8,128)(2,1)}, bf16[208,512]{1,0:T(8,128)(2,1)}, bf16[208,512]{1,0:T(8,128)(2,1)}, bf16[208,512]{1,0:T(8,128)(2,1)}) custom-call(s32[4]{0:T(128)} %pad_add_fusion.refs_0_, bf16[208,512]{1,0:T(8,128)(2,1)} %get-tuple-element.161.refs_1_, bf16[208,512]{1,0:T(8,128)(2,1)} %copy-done.16, bf16[208,512]{1,0:T(8,128)(2,1)} %copy-done.17, ...), custom_call_target="tpu_custom_call" | custom-call | flops 3489660928 | bytes 6000000 | tf_op jit(solution)/shard_map/expert/pallas_call | solution.py:688
  64.3 8.2 %expert.7 = (bf16[208,512]{1,0:T(8,128)(2,1)}, bf16[208,512]{1,0:T(8,128)(2,1)}, bf16[208,512]{1,0:T(8,128)(2,1)}, bf16[208,512]{1,0:T(8,128)(2,1)}) custom-call(s32[4]{0:T(128)} %pad_add_fusion.refs_0_, bf16[208,512]{1,0:T(8,128)(2,1)} %get-tuple-element.167.refs_1_, bf16[208,512]{1,0:T(8,128)(2,1)} %copy-done.25, bf16[208,512]{1,0:T(8,128)(2,1)} %copy-done.26, ...), custom_call_target="tpu_custom_call" | custom-call | flops 3489660928 | bytes 6000000 | tf_op jit(solution)/shard_map/expert/pallas_call | solution.py:688
  76.4 4.2 spread_cotangent.1
  85.9 21.5 %forward.3 = (f32[4,208,512]{2,1,0:T(8,128)}, bf16[4,208,1536]{2,1,0:T(8,128)(2,1)}, bf16[4,8,208,208]{3,2,1,0:T(8,128)(2,1)}, bf16[4,208,512]{2,1,0:T(8,128)(2,...) custom-call(s32[4]{0:T(128)} %pad_add_fusion.refs_0_, ...), custom_call_target="tpu_custom_call" | custom-call | flops 6000000000 | bytes 20000000 | tf_op jit(solution)/shard_map/forward/pallas_call | solution.py:688
  111.8 4.2 collective-permute-done.19.refs_3_
  116.0 4.2 collective-permute-done.20.refs_4_
  120.8 14.0 %expert.8 = (bf16[208,512]{1,0:T(8,128)(2,1)}, bf16[208,512]{1,0:T(8,128)(2,1)}, bf16[208,512]{1,0:T(8,128)(2,1)}, bf16[208,512]{1,0:T(8,128)(2,1)}, bf16[208,51...) custom-call(s32[4]{0:T(128)} %pad_add_fusion.refs_0_, ...), custom_call_target="tpu_custom_call" | custom-call | flops 6979321856 | bytes 6000000 | tf_op jit(solution)/shard_map/expert/pallas_call | solution.py:688
  135.7 14.3 %expert.9 = (bf16[416,512]{1,0:T(8,128)(2,1)}, bf16[416,512]{1,0:T(8,128)(2,1)}, bf16[416,512]{1,0:T(8,128)(2,1)}, bf16[416,512]{1,0:T(8,128)(2,1)}, bf16[208,51...) custom-call(s32[4]{0:T(128)} %pad_add_fusion.refs_0_, ...), custom_call_target="tpu_custom_call" | custom-call | flops 6979321856 | bytes 6000000 | tf_op jit(solution)/shard_map/expert/pallas_call | solution.py:688
  150.0 9.9 %weights.4.refs_8_ = bf16[16,512,512]{2,1,0:T(8,128)(2,1)} custom-call(s32[4]{0:T(128)} %pad_add_fusion.refs_0_, bf16[208,512]{1,0:T(8,128)(2,1)} %get-tuple-element.188.refs_1_, bf16[208,512]{1,0:T(8,128)(2,1)} %copy-done.19, bf16[208,512]{1,0:T(8,128)(2,1)} %copy-done.20, bf16[208,512]{1,0:T(8,128)(2,1)} %copy-done.21, ...), custom_call_target="tpu_custom_call" | custom-call | flops 3489660928 | bytes 6000000 | tf_op jit(solution)/shard_map/weights/pallas_call | solution.py:688
  160.0 9.9 %weights.5 = (bf16[16,512,512]{2,1,0:T(8,128)(2,1)}, bf16[416,512]{1,0:T(8,128)(2,1)}, bf16[416,512]{1,0:T(8,128)(2,1)}, bf16[416,512]{1,0:T(8,128)(2,1)}, bf16[416,512]{1,0:T(8,128)(2,1)}) custom-call(s32[4]{0:T(128)} %pad_add_fusion.refs_0_, ...), custom_call_target="tpu_custom_call", output_to_operand_aliasing={{0}: (8, {}), {1}: (9, {}), {2}: (10, {}), {3}: (11, {}), {... | custom-call | flops 3489660928 | bytes 6000000 | tf_op jit(solution)/shard_map/weights/pallas_call | solution.py:688
  179.2 4.1 collective-permute-done.28.refs_16_
  184.0 4.2 collective-permute-done.27.refs_15_
  188.3 4.1 collective-permute-done.29.refs_17_
  193.1 30.7 %backward.2 = (f32[4,208,512]{2,1,0:T(8,128)}, bf16[2,128,2176]{2,1,0:T(8,128)(2,1)}, bf16[2,128,2176]{2,1,0:T(8,128)(2,1)}, bf16[208,512]{1,0:T(8,128)(2,1)}, b...) custom-call(s32[4]{0:T(128)} %pad_add_fusion.refs_0_, ...), custom_call_target="tpu_custom_call" | custom-call | flops 12000000000 | bytes 30000000 | tf_op jit(solution)/shard_map/backward/pallas_call | solution.py:688
  228.2 8.3 %collective-permute-done.23.refs_6_ = bf16[416,512]{1,0:T(8,128)(2,1)S(1)} collective-permute-done((bf16[416,512]{1,0:T(8,128)(2,1)S(1)}, bf16[416,512]{1,0:T(8,128)(2,1)S(1)}, u32[]{:S(2)}, u32[]{:S(2)}) %collective-permute-start.23) | collective-permute-done | bytes 426016 | tf_op jit(solution)/shard_map/ppermute | solution.py:837
  237.5 6.2 %block_out.1.refs_15_ = f32[4,197,512]{2,1,0:T(8,128)} custom-call(f32[4,208,512]{2,1,0:T(8,128)} %get-tuple-element.179.refs_6_.refs_0_, f32[4,208,128]{2,1,0:T(8,128)} %get-tuple-element.180.refs_1_, s32[2,4,208,128]{3,2,1,0:T(8,128)} %get-tuple-element.157.refs_9_.refs_3_.refs_19_.refs_2_, bf16[416,512]{1,0:T(8,128)(2,1)} %get-tuple-element.207.refs_3_, ...), custom_call_target="tpu_custom_call" | custom-call | flops 1417674752 | bytes 6000000 | tf_op jit(solution)/shard_map/block_out/pallas_call | solution.py:688
  246.8 12.1 %expert.10 = (bf16[208,512]{1,0:T(8,128)(2,1)}, bf16[208,512]{1,0:T(8,128)(2,1)}, bf16[208,512]{1,0:T(8,128)(2,1)}, bf16[208,512]{1,0:T(8,128)(2,1)}, bf16[832,2...) custom-call(s32[4]{0:T(128)} %pad_add_fusion.refs_0_, ...), custom_call_target="tpu_custom_call" | custom-call | flops 5234491392 | bytes 6000000 | tf_op jit(solution)/shard_map/expert/pallas_call | solution.py:688
  266.1 12.2 %expert.11 = (bf16[208,512]{1,0:T(8,128)(2,1)}, bf16[208,512]{1,0:T(8,128)(2,1)}, bf16[208,512]{1,0:T(8,128)(2,1)}, bf16[208,512]{1,0:T(8,128)(2,1)}, bf16[832,2...) custom-call(s32[4]{0:T(128)} %pad_add_fusion.refs_0_, ...), custom_call_target="tpu_custom_call" | custom-call | flops 5234491392 | bytes 6000000 | tf_op jit(solution)/shard_map/expert/pallas_call | solution.py:688
  278.6 10.1 %weights.6 = (bf16[8,128,512]{2,1,0:T(8,128)(2,1)}, bf16[8,128,512]{2,1,0:T(8,128)(2,1)}, bf16[8,128,512]{2,1,0:T(8,128)(2,1)}, bf16[8,128,512]{2,1,0:T(8,128)(2,1)}) custom-call(s32[4]{0:T(128)} %pad_add_fusion.refs_0_, bf16[208,512]{1,0:T(8,128)(2,1)} %get-tuple-element.161.refs_1_, bf16[208,512]{1,0:T(8,128)(2,1)} %copy-done.16, ...), custom_call_target="tpu_custom_call" | custom-call | flops 3489660928 | bytes 6000000 | tf_op jit(solution)/shard_map/weights/pallas_call | solution.py:688
  293.2 10.0 %weights.7 = (bf16[8,128,512]{2,1,0:T(8,128)(2,1)}, bf16[8,128,512]{2,1,0:T(8,128)(2,1)}, bf16[8,128,512]{2,1,0:T(8,128)(2,1)}, bf16[8,128,512]{2,1,0:T(8,128)(2,1)}) custom-call(s32[4]{0:T(128)} %pad_add_fusion.refs_0_, bf16[208,512]{1,0:T(8,128)(2,1)} %get-tuple-element.167.refs_1_, bf16[208,512]{1,0:T(8,128)(2,1)} %copy-done.25, ...), custom_call_target="tpu_custom_call" | custom-call | flops 3489660928 | bytes 6000000 | tf_op jit(solution)/shard_map/weights/pallas_call | solution.py:688
  304.3 28.0 %backward.3 = (f32[4,197,512]{2,1,0:T(8,128)}, bf16[2,128,2176]{2,1,0:T(8,128)(2,1)}, bf16[2,128,2176]{2,1,0:T(8,128)(2,1)}, bf16[8,128,512]{2,1,0:T(8,128)(2,1)}) custom-call(s32[4]{0:T(128)} %pad_add_fusion.refs_0_, f32[4,208,512]{2,1,0:T(8,128)} %get-tuple-element.225.refs_7_.refs_1_, ...), custom_call_target="tpu_custom_call", output_to_operand_aliasing={{3}: (24, {})} | custom-call | flops 12000000000 | bytes 30000000 | tf_op jit(solution)/shard_map/backward/pallas_call | solution.py:688
  340.6 17.6 %collective-permute-done.46.refs_2_ = bf16[8,128,512]{2,1,0:T(8,128)(2,1)S(1)} collective-permute-done((bf16[8,128,512]{2,1,0:T(8,128)(2,1)}, bf16[8,128,512]{2,1,0:T(8,128)(2,1)S(1)}, u32[]{:S(2)}, u32[]{:S(2)}) %collective-permute-start.46) | collective-permute-done | bytes 1048608 | tf_op jit(solution)/shard_map/ppermute | solution.py:660
  368.0 32.2 %all_to_all.10 = bf16[8,2,16,2176]{3,2,1,0:T(8,128)(2,1)S(1)} all-to-all(bf16[8,2,16,2176]{3,2,1,0:T(8,128)(2,1)S(1)} %pad_maximum_fusion), channel_id=1, replica_groups={{0,4,8,12,16,20,24,28},{2,6,10,14,18,22,26,30},{1,5,9,13,17,21,25,29},{..., dimensions={0} | all-to-all | bytes 2228224 | tf_op jit(solution)/shard_map/all_to_all | solution.py:1062
  410.5 32.3 %collective-permute-done.50.refs_1_ = bf16[8,128,512]{2,1,0:T(8,128)(2,1)S(1)} collective-permute-done((bf16[8,128,512]{2,1,0:T(8,128)(2,1)}, bf16[8,128,512]{2,1,0:T(8,128)(2,1)S(1)}, u32[]{:S(2)}, u32[]{:S(2)}) %collective-permute-start.50) | collective-permute-done | bytes 1048608 | tf_op jit(solution)/shard_map/ppermute | solution.py:660
  450.4 14.8 %collective-permute-done.54.refs_1_ = bf16[8,128,512]{2,1,0:T(8,128)(2,1)S(1)} collective-permute-done((bf16[8,128,512]{2,1,0:T(8,128)(2,1)}, bf16[8,128,512]{2,1,0:T(8,128)(2,1)S(1)}, u32[]{:S(2)}, u32[]{:S(2)}) %collective-permute-start.54) | collective-permute-done | bytes 1048608 | tf_op jit(solution)/shard_map/ppermute | solution.py:660
  481.7 6.5 %collective-permute-done.51.refs_1_ = bf16[2,128,512]{2,1,0:T(8,128)(2,1)S(1)} collective-permute-done((bf16[2,128,512]{2,1,0:T(8,128)(2,1)}, bf16[2,128,512]{2,1,0:T(8,128)(2,1)S(1)}, u32[]{:S(2)}, u32[]{:S(2)}) %collective-permute-start.51) | collective-permute-done | bytes 262176 | tf_op jit(solution)/shard_map/ppermute | solution.py:660
  496.1 11.9 %collective-permute-done.56.refs_2_ = bf16[2,128,512]{2,1,0:T(8,128)(2,1)S(1)} collective-permute-done((bf16[2,128,512]{2,1,0:T(8,128)(2,1)}, bf16[2,128,512]{2,1,0:T(8,128)(2,1)S(1)}, u32[]{:S(2)}, u32[]{:S(2)}) %collective-permute-start.56) | collective-permute-done | bytes 262176 | tf_op jit(solution)/shard_map/ppermute | solution.py:660
  508.0 5.7 %collective-permute-done.57.refs_3_ = bf16[2,128,512]{2,1,0:T(8,128)(2,1)} collective-permute-done((bf16[2,128,512]{2,1,0:T(8,128)(2,1)}, bf16[2,128,512]{2,1,0:T(8,128)(2,1)}, u32[]{:S(2)}, u32[]{:S(2)}) %collective-permute-start.57) | collective-permute-done | bytes 262176 | tf_op jit(solution)/shard_map/ppermute | solution.py:660
  (299 shorter events, 146.5 us)
Async XLA Ops:
  7.2 472.3 %reduce-scatter.2.cloned.1.call-start = ((), (), s32[]{:S(2)}) async-start(), calls=%async_computation.3 | async-start | bytes 9437184 | tf_op jit(solution)/shard_map/reduce_scatter | solution.py:1207
  42.4 21.1 %collective-permute-start.3 = (bf16[208,512]{1,0:T(8,128)(2,1)}, bf16[208,512]{1,0:T(8,128)(2,1)S(1)}, u32[]{:S(2)}, u32[]{:S(2)}) collective-permute-start(bf16[208,512]{1,0:T(8,128)(2,1)} %get-tuple-element.168), channel_id=1, source_target_pairs={{0,2},{1,3},{2,0},{3,1},{4,6},{5,7},{6,4},{7,5},{8,10},{9,11},{10,... | collective-permute-start | bytes 638984 | tf_op jit(solution)/shard_map/ppermute | solution.py:837
  80.6 29.0 %collective-permute-start.15 = (bf16[416,512]{1,0:T(8,128)(2,1)}, bf16[416,512]{1,0:T(8,128)(2,1)S(1)}, u32[]{:S(2)}, u32[]{:S(2)}) collective-permute-start(bf16[416,512]{1,0:T(8,128)(2,1)} %get-tuple-element.185), channel_id=1, source_target_pairs={{0,2},{1,3},{2,0},{3,1},{4,6},{5,7},{6,4},{7,5},{8,10},{9,11},{10,... | collective-permute-start | bytes 1277960 | tf_op jit(solution)/shard_map/ppermute | solution.py:837
  80.9 28.8 %collective-permute-start.16 = (bf16[416,512]{1,0:T(8,128)(2,1)}, bf16[416,512]{1,0:T(8,128)(2,1)S(1)}, u32[]{:S(2)}, u32[]{:S(2)}) collective-permute-start(bf16[416,512]{1,0:T(8,128)(2,1)} %get-tuple-element.186), channel_id=1, source_target_pairs={{0,1},{1,0},{2,3},{3,2},{4,5},{5,4},{6,7},{7,6},{8,9},{9,8},{10,11... | collective-permute-start | bytes 1277960 | tf_op jit(solution)/shard_map/ppermute | solution.py:837
  82.8 27.0 %collective-permute-start.17 = (bf16[416,512]{1,0:T(8,128)(2,1)}, bf16[416,512]{1,0:T(8,128)(2,1)S(1)}, u32[]{:S(2)}, u32[]{:S(2)}) collective-permute-start(bf16[416,512]{1,0:T(8,128)(2,1)} %get-tuple-element.187), channel_id=1, source_target_pairs={{0,3},{1,2},{2,1},{3,0},{4,7},{5,6},{6,5},{7,4},{8,11},{9,10},{10,... | collective-permute-start | bytes 1277960 | tf_op jit(solution)/shard_map/ppermute | solution.py:837
  109.7 25.2 %collective-permute-start.12 = (bf16[208,512]{1,0:T(8,128)(2,1)}, bf16[208,512]{1,0:T(8,128)(2,1)S(1)}, u32[]{:S(2)}, u32[]{:S(2)}) collective-permute-start(bf16[208,512]{1,0:T(8,128)(2,1)} %get-tuple-element.182), channel_id=1, source_target_pairs={{0,2},{1,3},{2,0},{3,1},{4,6},{5,7},{6,4},{7,5},{8,10},{9,11},{10,... | collective-permute-start | bytes 638984 | tf_op jit(solution)/shard_map/ppermute | solution.py:837
  109.9 25.0 %collective-permute-start.13 = (bf16[208,512]{1,0:T(8,128)(2,1)}, bf16[208,512]{1,0:T(8,128)(2,1)S(1)}, u32[]{:S(2)}, u32[]{:S(2)}) collective-permute-start(bf16[208,512]{1,0:T(8,128)(2,1)} %get-tuple-element.183), channel_id=1, source_target_pairs={{0,1},{1,0},{2,3},{3,2},{4,5},{5,4},{6,7},{7,6},{8,9},{9,8},{10,11... | collective-permute-start | bytes 638984 | tf_op jit(solution)/shard_map/ppermute | solution.py:837
  111.8 23.1 %collective-permute-start.14 = (bf16[208,512]{1,0:T(8,128)(2,1)}, bf16[208,512]{1,0:T(8,128)(2,1)S(1)}, u32[]{:S(2)}, u32[]{:S(2)}) collective-permute-start(bf16[208,512]{1,0:T(8,128)(2,1)} %get-tuple-element.184), channel_id=1, source_target_pairs={{0,3},{1,2},{2,1},{3,0},{4,7},{5,6},{6,5},{7,4},{8,11},{9,10},{10,... | collective-permute-start | bytes 638984 | tf_op jit(solution)/shard_map/ppermute | solution.py:837
  179.2 47.6 %collective-permute-start.21 = (bf16[416,512]{1,0:T(8,128)(2,1)S(1)}, bf16[416,512]{1,0:T(8,128)(2,1)S(1)}, u32[]{:S(2)}, u32[]{:S(2)}) collective-permute-start(bf16[416,512]{1,0:T(8,128)(2,1)S(1)} %copy-done.32), channel_id=1, source_target_pairs={{2,0},{3,1},{0,2},{1,3},{6,4},{7,5},{4,6},{5,7},{10,8},{11,9},{8,1... | collective-permute-start | bytes 1277960 | tf_op jit(solution)/shard_map/ppermute | solution.py:837
  183.2 43.6 %collective-permute-start.22 = (bf16[416,512]{1,0:T(8,128)(2,1)S(1)}, bf16[416,512]{1,0:T(8,128)(2,1)S(1)}, u32[]{:S(2)}, u32[]{:S(2)}) collective-permute-start(bf16[416,512]{1,0:T(8,128)(2,1)S(1)} %copy-done.33), channel_id=1, source_target_pairs={{1,0},{0,1},{3,2},{2,3},{5,4},{4,5},{7,6},{6,7},{9,8},{8,9},{11,10... | collective-permute-start | bytes 1277960 | tf_op jit(solution)/shard_map/ppermute | solution.py:837
  223.8 35.2 %collective-permute-start.36 = (bf16[2,128,2176]{2,1,0:T(8,128)(2,1)}, bf16[2,128,2176]{2,1,0:T(8,128)(2,1)S(1)}, u32[]{:S(2)}, u32[]{:S(2)}) collective-permute-start(bf16[2,128,2176]{2,1,0:T(8,128)(2,1)} %get-tuple-element.240), channel_id=1, source_target_pairs={{0,2},{2,0},{4,6},{6,4},{8,10},{10,8},{12,14},{14,12},{16,18},{18,... | collective-permute-start | bytes 3342344 | tf_op jit(solution)/shard_map/ppermute | solution.py:660
  236.5 27.2 %collective-permute-start.33 = (bf16[208,512]{1,0:T(8,128)(2,1)}, bf16[208,512]{1,0:T(8,128)(2,1)S(1)}, u32[]{:S(2)}, u32[]{:S(2)}) collective-permute-start(bf16[208,512]{1,0:T(8,128)(2,1)} %get-tuple-element.236), channel_id=1, source_target_pairs={{0,2},{1,3},{2,0},{3,1},{4,6},{5,7},{6,4},{7,5},{8,10},{9,11},{10,... | collective-permute-start | bytes 638984 | tf_op jit(solution)/shard_map/ppermute | solution.py:837
  258.9 33.6 %collective-permute-start.37 = (bf16[208,512]{1,0:T(8,128)(2,1)}, bf16[208,512]{1,0:T(8,128)(2,1)S(1)}, u32[]{:S(2)}, u32[]{:S(2)}) collective-permute-start(bf16[208,512]{1,0:T(8,128)(2,1)} %get-tuple-element.243), channel_id=1, source_target_pairs={{2,0},{3,1},{0,2},{1,3},{6,4},{7,5},{4,6},{5,7},{10,8},{11,9},{8,1... | collective-permute-start | bytes 638984 | tf_op jit(solution)/shard_map/ppermute | solution.py:841
  259.0 44.2 %collective-permute-start.39 = (bf16[208,512]{1,0:T(8,128)(2,1)}, bf16[208,512]{1,0:T(8,128)(2,1)S(1)}, u32[]{:S(2)}, u32[]{:S(2)}) collective-permute-start(bf16[208,512]{1,0:T(8,128)(2,1)} %get-tuple-element.245), channel_id=1, source_target_pairs={{1,0},{0,1},{3,2},{2,3},{5,4},{4,5},{7,6},{6,7},{9,8},{8,9},{11,10... | collective-permute-start | bytes 638984 | tf_op jit(solution)/shard_map/ppermute | solution.py:841
  263.7 39.6 %collective-permute-start.41 = (bf16[208,512]{1,0:T(8,128)(2,1)S(1)}, bf16[208,512]{1,0:T(8,128)(2,1)S(1)}, u32[]{:S(2)}, u32[]{:S(2)}) collective-permute-start(bf16[208,512]{1,0:T(8,128)(2,1)S(1)} %copy-done.51), channel_id=1, source_target_pairs={{3,0},{2,1},{1,2},{0,3},{7,4},{6,5},{5,6},{4,7},{11,8},{10,9},{9,1... | collective-permute-start | bytes 638984 | tf_op jit(solution)/shard_map/ppermute | solution.py:841
  264.6 24.1 %collective-permute-start.43 = (bf16[128,2176]{1,0:T(8,128)(2,1)}, bf16[128,2176]{1,0:T(8,128)(2,1)S(1)}, u32[]{:S(2)}, u32[]{:S(2)}) collective-permute-start(bf16[128,2176]{1,0:T(8,128)(2,1)} %get-tuple-element.252), channel_id=1, source_target_pairs={{0,1},{1,0},{2,3},{3,2},{4,5},{5,4},{6,7},{7,6},{8,9},{9,8},{10,11... | collective-permute-start | bytes 1671176 | tf_op jit(solution)/shard_map/ppermute | solution.py:660
  278.2 25.1 %collective-permute-start.38 = (bf16[208,512]{1,0:T(8,128)(2,1)}, bf16[208,512]{1,0:T(8,128)(2,1)S(1)}, u32[]{:S(2)}, u32[]{:S(2)}) collective-permute-start(bf16[208,512]{1,0:T(8,128)(2,1)} %get-tuple-element.244), channel_id=1, source_target_pairs={{2,0},{3,1},{0,2},{1,3},{6,4},{7,5},{4,6},{5,7},{10,8},{11,9},{8,1... | collective-permute-start | bytes 638984 | tf_op jit(solution)/shard_map/ppermute | solution.py:841
  332.5 25.6 %collective-permute-start.46 = (bf16[8,128,512]{2,1,0:T(8,128)(2,1)}, bf16[8,128,512]{2,1,0:T(8,128)(2,1)S(1)}, u32[]{:S(2)}, u32[]{:S(2)}) collective-permute-start(bf16[8,128,512]{2,1,0:T(8,128)(2,1)} %get-tuple-element.265), channel_id=1, source_target_pairs={{0,4},{2,6},{4,0},{6,2},{8,12},{10,14},{12,8},{14,10},{16,20},{18,... | collective-permute-start | bytes 3145736 | tf_op jit(solution)/shard_map/ppermute | solution.py:660
  334.0 25.2 %collective-permute-start.47 = (bf16[8,128,512]{2,1,0:T(8,128)(2,1)}, bf16[8,128,512]{2,1,0:T(8,128)(2,1)S(1)}, u32[]{:S(2)}, u32[]{:S(2)}) collective-permute-start(bf16[8,128,512]{2,1,0:T(8,128)(2,1)} %get-tuple-element.266), channel_id=1, source_target_pairs={{0,8},{2,10},{4,12},{6,14},{8,0},{10,2},{12,4},{14,6},{16,24},{18,... | collective-permute-start | bytes 3145736 | tf_op jit(solution)/shard_map/ppermute | solution.py:660
  339.2 24.7 %collective-permute-start.45 = (bf16[128,2176]{1,0:T(8,128)(2,1)}, bf16[128,2176]{1,0:T(8,128)(2,1)S(1)}, u32[]{:S(2)}, u32[]{:S(2)}) collective-permute-start(bf16[128,2176]{1,0:T(8,128)(2,1)} %get-tuple-element.263), channel_id=1, source_target_pairs={{0,1},{1,0},{2,3},{3,2},{4,5},{5,4},{6,7},{7,6},{8,9},{9,8},{10,11... | collective-permute-start | bytes 1671176 | tf_op jit(solution)/shard_map/ppermute | solution.py:660
  401.5 46.3 %all-to-all-start.1 = ((bf16[8,2,16,2176]{3,2,1,0:T(8,128)(2,1)}), bf16[8,2,16,2176]{3,2,1,0:T(8,128)(2,1)S(1)}, u32[]{:S(2)}, u32[]{:S(2)}) async-start(bf16[8,2,16,2176]{3,2,1,0:T(8,128)(2,1)} %broadcast_in_dim.2), calls=%async_computation.1 | async-start | bytes 2228224 | tf_op jit(solution)/shard_map/all_to_all | solution.py:1066
  405.0 37.7 %collective-permute-start.50 = (bf16[8,128,512]{2,1,0:T(8,128)(2,1)}, bf16[8,128,512]{2,1,0:T(8,128)(2,1)S(1)}, u32[]{:S(2)}, u32[]{:S(2)}) collective-permute-start(bf16[8,128,512]{2,1,0:T(8,128)(2,1)} %get-tuple-element.269), channel_id=1, source_target_pairs={{0,4},{2,6},{4,0},{6,2},{8,12},{10,14},{12,8},{14,10},{16,20},{18,... | collective-permute-start | bytes 3145736 | tf_op jit(solution)/shard_map/ppermute | solution.py:660
  406.9 58.2 %collective-permute-start.54 = (bf16[8,128,512]{2,1,0:T(8,128)(2,1)}, bf16[8,128,512]{2,1,0:T(8,128)(2,1)S(1)}, u32[]{:S(2)}, u32[]{:S(2)}) collective-permute-start(bf16[8,128,512]{2,1,0:T(8,128)(2,1)} %get-tuple-element.277), channel_id=1, source_target_pairs={{0,4},{2,6},{4,0},{6,2},{8,12},{10,14},{12,8},{14,10},{16,20},{18,... | collective-permute-start | bytes 3145736 | tf_op jit(solution)/shard_map/ppermute | solution.py:660
  407.1 40.8 %collective-permute-start.49 = (bf16[4,128,512]{2,1,0:T(8,128)(2,1)}, bf16[4,128,512]{2,1,0:T(8,128)(2,1)}, u32[]{:S(2)}, u32[]{:S(2)}) collective-permute-start(bf16[4,128,512]{2,1,0:T(8,128)(2,1)} %get-tuple-element.268), channel_id=1, source_target_pairs={{0,8},{2,10},{4,12},{6,14},{8,0},{10,2},{12,4},{14,6},{16,24},{18,... | collective-permute-start | bytes 1572872 | tf_op jit(solution)/shard_map/ppermute | solution.py:660
  409.0 65.5 %collective-permute-start.52 = (bf16[4,128,512]{2,1,0:T(8,128)(2,1)}, bf16[4,128,512]{2,1,0:T(8,128)(2,1)}, u32[]{:S(2)}, u32[]{:S(2)}) collective-permute-start(bf16[4,128,512]{2,1,0:T(8,128)(2,1)} %get-tuple-element.274), channel_id=1, source_target_pairs={{0,4},{2,6},{4,0},{6,2},{8,12},{10,14},{12,8},{14,10},{16,20},{18,... | collective-permute-start | bytes 1572872 | tf_op jit(solution)/shard_map/ppermute | solution.py:660
  446.3 28.2 %collective-permute-start.53 = (bf16[4,128,512]{2,1,0:T(8,128)(2,1)}, bf16[4,128,512]{2,1,0:T(8,128)(2,1)}, u32[]{:S(2)}, u32[]{:S(2)}) collective-permute-start(bf16[4,128,512]{2,1,0:T(8,128)(2,1)} %get-tuple-element.275), channel_id=1, source_target_pairs={{0,8},{2,10},{4,12},{6,14},{8,0},{10,2},{12,4},{14,6},{16,24},{18,... | collective-permute-start | bytes 1572872 | tf_op jit(solution)/shard_map/ppermute | solution.py:660
  447.9 81.7 %collective-permute-start.48 = (bf16[2,128,2176]{2,1,0:T(8,128)(2,1)S(1)}, bf16[2,128,2176]{2,1,0:T(8,128)(2,1)S(1)}, u32[]{:S(2)}, u32[]{:S(2)}) collective-permute-start(bf16[2,128,2176]{2,1,0:T(8,128)(2,1)S(1)} %bitcast.13), channel_id=1, source_target_pairs={{0,2},{2,0},{4,6},{6,4},{8,10},{10,8},{12,14},{14,12},{16,18},{18,... | collective-permute-start | bytes 3342344 | tf_op jit(solution)/shard_map/ppermute | solution.py:660
  468.8 24.5 %collective-permute-start.58 = (bf16[4,128,512]{2,1,0:T(8,128)(2,1)}, bf16[4,128,512]{2,1,0:T(8,128)(2,1)}, u32[]{:S(2)}, u32[]{:S(2)}) collective-permute-start(bf16[4,128,512]{2,1,0:T(8,128)(2,1)} %get-tuple-element.285), channel_id=1, source_target_pairs={{0,8},{2,10},{4,12},{6,14},{8,0},{10,2},{12,4},{14,6},{16,24},{18,... | collective-permute-start | bytes 1572872 | tf_op jit(solution)/shard_map/ppermute | solution.py:660
  477.1 30.9 %collective-permute-start.56 = (bf16[2,128,512]{2,1,0:T(8,128)(2,1)}, bf16[2,128,512]{2,1,0:T(8,128)(2,1)S(1)}, u32[]{:S(2)}, u32[]{:S(2)}) collective-permute-start(bf16[2,128,512]{2,1,0:T(8,128)(2,1)} %get-tuple-element.283), channel_id=1, source_target_pairs={{0,16},{2,18},{4,20},{6,22},{8,24},{10,26},{12,28},{14,30},{16,0},... | collective-permute-start | bytes 786440 | tf_op jit(solution)/shard_map/ppermute | solution.py:660
  481.7 43.3 %collective-permute-start.63 = (bf16[1,512,512]{2,1,0:T(8,128)(2,1)}, bf16[1,512,512]{2,1,0:T(8,128)(2,1)}, u32[]{:S(2)}, u32[]{:S(2)}) collective-permute-start(bf16[1,512,512]{2,1,0:T(8,128)(2,1)} %get-tuple-element.325), channel_id=1, source_target_pairs={{0,2},{2,0},{4,6},{6,4},{8,10},{10,8},{12,14},{14,12},{16,18},{18,... | collective-permute-start | bytes 1572872 | tf_op jit(solution)/shard_map/ppermute | solution.py:660
  488.2 25.6 %collective-permute-start.57 = (bf16[2,128,512]{2,1,0:T(8,128)(2,1)}, bf16[2,128,512]{2,1,0:T(8,128)(2,1)}, u32[]{:S(2)}, u32[]{:S(2)}) collective-permute-start(bf16[2,128,512]{2,1,0:T(8,128)(2,1)} %get-tuple-element.284), channel_id=1, source_target_pairs={{0,16},{2,18},{4,20},{6,22},{8,24},{10,26},{12,28},{14,30},{16,0},... | collective-permute-start | bytes 786440 | tf_op jit(solution)/shard_map/ppermute | solution.py:660
  495.5 22.8 %collective-permute-start.61 = (bf16[2,128,512]{2,1,0:T(8,128)(2,1)}, bf16[2,128,512]{2,1,0:T(8,128)(2,1)}, u32[]{:S(2)}, u32[]{:S(2)}) collective-permute-start(bf16[2,128,512]{2,1,0:T(8,128)(2,1)} %get-tuple-element.291), channel_id=1, source_target_pairs={{0,16},{2,18},{4,20},{6,22},{8,24},{10,26},{12,28},{14,30},{16,0},... | collective-permute-start | bytes 786440 | tf_op jit(solution)/shard_map/ppermute | solution.py:660
  (109 other events, 794.7 us)
Sparse Core Ops, SparseCore 0:
  170.1 150.5 reduce-scatter.1

commit v3 on v2

--- a/solution.py
+++ b/solution.py
@@ -368,10 +368,6 @@
                 dx[d][...] = jnp.where(iota(data.shape, 0) == cp - 1, line, data).astype(BF16)
 
 
-def place_of(index, order):
-    return sum(((index >> bit) & 1) << (len(order) - 1 - k) for k, bit in enumerate(order))
-
-
 def weight_kernel(*refs, n, cp, tiles, wire, follows):
     it = iter(refs)
     ids = next(it)
@@ -379,11 +375,10 @@
     act, dpre, dprod = next(it), next(it), next(it)
     if follows:
         next(it)
-    reps, rows_in, rows_out, order_out, order_in, out_at, in_at, whole_at = wire
-    wire_refs = [next(it) for _ in range(4 if whole_at is None else 1)]
+    reps, rows_in, rows_out, spot_at = wire
+    target = next(it)
     xcat, wires, sems = next(it), [next(it), next(it)], next(it)
     h = pl.program_id(0)
-    mine_out, mine_in = ids[out_at], ids[in_at]
 
     @pl.when(h == 0)
     def _():
@@ -392,50 +387,32 @@
 
     grad_out = tn(act[...], dprod[...]).astype(BF16)
     for q in range(reps // tiles):
-        spot = place_of(h * (reps // tiles) + q, order_out) ^ mine_out
+        spot = (h * (reps // tiles) + q) ^ ids[1]
         wires[0][spot] = grad_out[q * rows_out : (q + 1) * rows_out, :]
     grad_in = tn(xcat[...], dpre[...]).astype(BF16)
     line = pl.multiple_of(h * rows_in, rows_in)
     for q in range(reps):
-        spot = place_of(q, order_in) ^ mine_in
-        wires[1][spot, pl.ds(line, rows_in), :] = grad_in[q * rows_in : (q + 1) * rows_in, :]
+        wires[1][q ^ ids[1], pl.ds(line, rows_in), :] = grad_in[q * rows_in : (q + 1) * rows_in, :]
 
     @pl.when(h == tiles - 1)
     def _():
-        copies = []
-        half = wires[0].shape[0] // 2
         rows = wires[0].shape[1]
-        for k in range(2):
-            for part in range(2):
-                if whole_at is None:
-                    target = wire_refs[2 * k + part]
-                else:
-                    place = pl.ds((2 * whole_at + k) * rows, rows)
-                    target = wire_refs[0].at[pl.ds(part * half, half), place]
-                copies.append(
-                    pltpu.make_async_copy(
-                        wires[k].at[pl.ds(part * half, half)], target, sems.at[2 * k + part]
-                    )
-                )
+        copies = [
+            pltpu.make_async_copy(
+                wires[k], target.at[:, pl.ds((2 * spot_at + k) * rows, rows)], sems.at[k]
+            )
+            for k in range(2)
+        ]
         for copy in copies:
             copy.start()
         for copy in copies:
             copy.wait()
 
 
-def halve_kernel(*refs, count):
-    for k in range(count):
-        mine, got, keep, rest = refs[k], refs[count + k], refs[2 * count + k], refs[3 * count + k]
-        half = keep.shape[0]
-        keep[...] = (mine[:half].astype(F32) + got[:half].astype(F32)).astype(BF16)
-        rest[...] = (mine[half:].astype(F32) + got[half:].astype(F32)).astype(BF16)
-
-
 def finish_kernel(*refs, layers, pairs, tiles, rows_in):
     it = iter(refs)
     ids = next(it)
-    parts = [[(next(it), next(it)) for _ in range(2)] for _ in range(pairs)]
-    joint = next(it), next(it)
+    parts = [(next(it), next(it)) for _ in range(layers)]
     grad_in, grad_out = next(it), next(it)
     rows, tile = grad_out.shape[2:]
     for layer in range(layers):
@@ -443,15 +420,13 @@
             for side in range(2):
                 core = ids[1] if side == 0 else 1 - ids[1]
                 expert = core * pairs + j
-                if layer == 0:
-                    one, two = parts[j][0][side].at[0], parts[j][1][side].at[0]
-                else:
-                    one = joint[side].at[0, pl.ds(2 * j * rows, rows)]
-                    two = joint[side].at[0, pl.ds((2 * j + 1) * rows, rows)]
-                grad_out[layer, expert] = one[...].astype(F32)
+                part = parts[layer][side]
+                at = 2 * j * rows
+                grad_out[layer, expert] = part[0, at : at + rows, :].astype(F32)
                 for h in range(tiles):
-                    grad_in[layer, expert, :, h * tile : (h + 1) * tile] = two[
-                        h * rows_in : (h + 1) * rows_in, :
+                    line = at + rows + h * rows_in
+                    grad_in[layer, expert, :, h * tile : (h + 1) * tile] = part[
+                        0, line : line + rows_in, :
                     ].astype(F32)
 
 
@@ -707,25 +682,6 @@
         return out
 
 
-def halve(line, mine, got, carry=(), after=()):
-    count = len(mine)
-    parts = [shape_of((m.shape[0] // 2,) + tuple(m.shape[1:]), BF16) for m in mine]
-    size = sum(m.size for m in mine)
-    out = line(
-        partial(halve_kernel, count=count),
-        list(mine) + list(got),
-        [whole(m) for m in list(mine) + list(got)],
-        [whole(p) for p in parts + parts],
-        parts + parts,
-        (1,),
-        price=cost(size, 6 * size),
-        name="halve",
-        carry=carry,
-        after=after,
-    )
-    return out[:count], out[count : 2 * count], out[2 * count :]
-
-
 def add(line, a, b):
     count = a.shape[0] if len(a.shape) == 3 else 1
     part = shape_of(a.shape[-2:], BF16)
@@ -780,11 +736,7 @@
     me_rep = lax.axis_index("rep")
     me_exp = lax.axis_index("exp")
     core = me_rep % cores
-    x_first = x_bits + z_bits + [0]
-    z_first = z_bits[:1] + x_bits + z_bits[1:] + [0]
-    ids = jnp.stack(
-        [me_exp, core, place_of(me_rep, x_first), place_of(me_rep, z_first)]
-    ).astype(jnp.int32)
+    ids = jnp.stack([me_exp, core]).astype(jnp.int32)
     router_wide = jnp.pad(w_router, ((0, 0), (0, 0), (0, LANES - experts)))
     dims = dict(n=n, per=per, cp=cp)
 
@@ -970,7 +922,6 @@
             shapes += [slot_shape] * n + [act_shape] * 2 + [cat_shape]
             out_specs += [whole(slot_shape)] * n + [act_spec] * 2 + [whole(cat_shape)]
             scratch += [pltpu.VMEM((n * cp, width), BF16), pltpu.VMEM((n * cp, width), F32)]
-        matmuls = (2 if produce else 1) + (2 if backward else 0)
         out = line(
             partial(
                 expert_kernel,
@@ -987,7 +938,7 @@
             shapes,
             (tiles,),
             scratch,
-            cost(2 * matmuls * n * cp * width * hidden, 6e6, 2e6),
+            cost(1, 1),
             "expert",
             1,
         )
@@ -995,7 +946,7 @@
             return out[:-3], out[-3:]
         return out, None
 
-    def run_weights(j, x, saved, joint=False, before=None, carry=(), after=()):
+    def run_weights(j, x, saved, before=None, after=()):
         args, specs = [ids], []
         rows_of(x, j, args, specs)
         args += saved
@@ -1005,45 +956,32 @@
             aliases = {len(args): 0}
             args.append(before)
             specs.append(any_spec)
-        order_in = z_first if j == 0 else x_first
-        chunk_out = (reps, rows_out, width)
-        chunk_in = (reps, tiles * rows_in, tile)
-        if joint:
-            natural = list(range(bits - 1, -1, -1))
-            wire = (reps, rows_in, rows_out, natural, natural, 1, 1, j)
-            shapes = [shape_of((reps, 2 * per * rows_out, width), BF16)]
-        else:
-            wire = (reps, rows_in, rows_out, x_first, order_in, 2, 3 if j == 0 else 2, None)
-            shapes = [shape_of((c[0] // 2,) + c[1:], BF16) for c in (chunk_out,) * 2 + (chunk_in,) * 2]
-        out = line(
+        return line(
             partial(
-                weight_kernel, n=n, cp=cp, tiles=tiles, wire=wire, follows=before is not None
+                weight_kernel,
+                n=n,
+                cp=cp,
+                tiles=tiles,
+                wire=(reps, rows_in, rows_out, j),
+                follows=before is not None,
             ),
             args,
             specs,
-            [any_spec] * len(shapes),
-            shapes,
+            [any_spec],
+            [shape_of((reps, 2 * per * rows_out, width), BF16)],
             (tiles,),
             [
                 pltpu.VMEM((n * cp, width), BF16),
-                pltpu.VMEM(chunk_out, BF16),
-                pltpu.VMEM(chunk_in, BF16),
-                pltpu.SemaphoreType.DMA((4,)),
+                pltpu.VMEM((reps, rows_out, width), BF16),
+                pltpu.VMEM((reps, tiles * rows_in, tile), BF16),
+                pltpu.SemaphoreType.DMA((2,)),
             ],
-            cost(4 * n * cp * width * hidden, 6e6, 0),
+            cost(1, 1),
             "weights",
             1,
-            carry,
-            after,
-            aliases,
-        )
-        if joint:
-            return out[0], out[1:]
-        chunks = [
-            dict(mine=out[0], other=out[1], order=x_first, at=0),
-            dict(mine=out[2], other=out[3], order=order_in, at=0),
-        ]
-        return chunks, out[4:]
+            after=after,
+            aliases=aliases,
+        )[0]
 
     def dense_steps(mine, other, result):
         parts = add(line, mine, swap(other, "rep", 1, reps))
@@ -1156,22 +1094,6 @@
         count = len(out) - len(carry)
         return out[0], out[1:3], nested(out[3:count]), out[count:]
 
-    def add_up(chunks, carry=(), after=()):
-        chunks = [c for c in chunks if c["at"] < bits - 1]
-        if not chunks:
-            return list(carry)
-        got = [swap(c["other"], "rep", 1 << c["order"][c["at"]], reps) for c in chunks]
-        keep, rest, carried = halve(line, [c["mine"] for c in chunks], got, carry, after)
-        for c, mine, other in zip(chunks, keep, rest):
-            c["mine"], c["other"], c["at"] = mine, other, c["at"] + 1
-            if c["at"] == bits - 1:
-                c["other"] = swap(other, "rep", 1 << c["order"][-1], reps)
-        return carried
-
-    def later(chunks, carried):
-        for c, other in zip(chunks, carried):
-            c["other"] = other
-
     kept = []
     previous = None
     for layer in range(layers):
@@ -1198,19 +1120,25 @@
         saved.append(kept_rows)
         for d, part in enumerate(out[n : 2 * n]):
             d_back[d].append(go_back(part, d))
-    wire = None
-    for j in range(per):
-        carry = outs[-1][:n] if j == per - 1 else ()
-        wire, made_top = run_weights(j, x, saved[j], True, wire, carry)
-    back_top = send_back([[part] for part in made_top])
     groups = [[r for r in range(reps) if r % cores == c] for c in range(cores)]
-    share = lax.psum_scatter(
-        wire, "rep", scatter_dimension=0, axis_index_groups=groups, tiled=True
-    )
+
+    def summed(x, saved):
+        wire = None
+        for j in range(per):
+            wire = run_weights(j, x, saved[j], wire)
+        share = lax.psum_scatter(
+            wire, "rep", scatter_dimension=0, axis_index_groups=groups, tiled=True
+        )
+        half = share.shape[0] // 2
+        return share[:half], swap(share[half:], "rep", 1, reps)
+
+    shares = [None] * layers
+    dense = [[] for _ in range(layers)]
+    shares[top] = summed(x, saved)
     grad, parts, g_rows, _ = run_backward(top, cotangent, state, cached, d_back, ())
     g_rows = send(g_rows)
-    dense = [[] for _ in range(layers)]
     flow_top = dense_steps(parts[0], parts[1], dense[top])
+    back_top = send_back([[part] for part in outs[-1][:n]])
     block_out = run_out((cached[3], cached[6], back_top))
 
     state, cached, x, made = kept[0]
@@ -1223,43 +1151,15 @@
             d_back[k].append(go_back(out[k], k))
         if j == 0:
             step(flow_top)
-    sums = []
-    for j in range(per):
-        new, _ = run_weights(j, x, saved[j])
-        sums += new
-        if j == 0:
-            step(flow_top)
-    a, b, c, d = sums
-    grad, parts, _, carried = run_backward(0, grad, state, cached, d_back, [d["other"]])
-    later([d], carried)
+    shares[0] = summed(x, saved)
+    grad, parts, _, _ = run_backward(0, grad, state, cached, d_back, ())
     flow = dense_steps(parts[0], parts[1], dense[0])
+    step(flow)
     while not dense[top]:
         step(flow_top)
-    step(flow)
-    add_up([a, b])
     while not dense[0]:
         step(flow)
     halves = list(dense_over_chips([d[0] for d in dense]))
-    for group in ((c,), (a,), (d,), (b, c), (a,), (d,), (c, b), (d,)):
-        add_up(group)
-    for _ in range(bits):
-        add_up([a, b, c, d])
-    top_mine = share[: share.shape[0] // 2]
-    top_other = swap(share[share.shape[0] // 2 :], "rep", 1, reps)
-    pieces = [part for k in sums for part in (k["mine"], k["other"])] + [top_mine, top_other]
-    in_shape = shape_of((layers, local_experts, rows_in, hidden), F32)
-    out_shape = shape_of((layers, local_experts, rows_out, width), F32)
-    grad_in, grad_out = line(
-        partial(finish_kernel, layers=layers, pairs=per, tiles=tiles, rows_in=rows_in),
-        [ids] + pieces,
-        [smem()] + [whole(p) for p in pieces],
-        [whole(in_shape), whole(out_shape)],
-        [in_shape, out_shape],
-        (1,),
-        (),
-        cost(1e6, 6e6),
-        "finish",
-    )
     rows = width // n_exp
     dense_shapes = [
         shape_of((layers, rows, 3 * width), F32),
@@ -1276,6 +1176,20 @@
         [pltpu.VMEM((WIDE, LANES), F32)],
         cost(1e6, 6e6),
         "finish_dense",
+    )
+    pieces = [part for pair in shares for part in pair]
+    in_shape = shape_of((layers, local_experts, rows_in, hidden), F32)
+    out_shape = shape_of((layers, local_experts, rows_out, width), F32)
+    grad_in, grad_out = line(
+        partial(finish_kernel, layers=layers, pairs=per, tiles=tiles, rows_in=rows_in),
+        [ids] + pieces,
+        [smem()] + [whole(p) for p in pieces],
+        [whole(in_shape), whole(out_shape)],
+        [in_shape, out_shape],
+        (1,),
+        (),
+        cost(1e6, 6e6),
+        "finish",
     )
     return (
         block_out,

time: 553 us -> 526 us (0.951)
  blocking collectives: 32.2 us -> 66 us
  starting transfers between devices: 61.5 us -> 36.5 us
  Pallas kernels: 263 us -> 241 us
  waiting for transfers between devices: 138 us -> 124 us
    ppermute x22 -> x7, waiting for transfers between devices: 93.9 us -> 17.3 us  [swap(): return lax.ppermute(values, axis, [(r, r ^ distance) for r in range(total)])]
    reduce_scatter x1 -> x2, waiting for transfers between devices: 0.01 us -> 32.9 us  [summed(): lax.psum_scatter(wire, 'rep', scatter_dimension=0, axis_index_groups=grou...]
    all_to_all x0 -> x1, blocking collectives: none -> 31 us  [dense_over_chips(): lax.all_to_all(jnp.broadcast_to(share, parts.shape), 'rep', split_axis=0,...]
    pallas_call x32 -> x23, Pallas kernels: 263 us -> 241 us  [__call__(): pl.pallas_call(body, grid_spec=pltpu.PrefetchScalarGridSpec(num_scalar_pr...]
    ppermute x22 -> x7, starting transfers between devices: 24.2 us -> 4.5 us  [swap(): return lax.ppermute(values, axis, [(r, r ^ distance) for r in range(total)])]
    ppermute x12, waiting for transfers between devices: 16.3 us -> 32.7 us  [go_back(): return part if d == 0 else lax.ppermute(part, axes, shifted(d, True))]
    ppermute x30, waiting for transfers between devices: 27.4 us -> 41.5 us  [move(): lax.ppermute(part, axes, shifted(d, back))]
    unnamed x158 -> x142, local copies, waits for them, and re-layouts: 28.2 us -> 26.1 us
  transfers between devices with their start and end apart: 66 -> 51, of which waited for: 19 -> 19; matrix products, arithmetic and copies ran while one was open for 2% -> 3% of each run, Pallas kernels for 37% -> 35%
where the time goes in v3:
time: 526 us; the launch traced here: 516 us
  Pallas kernels  241 us (46%)
  waiting for transfers between devices  124 us (24%)
  blocking collectives  66 us (13%)
  starting transfers between devices  36.5 us (7%)
  local copies, waits for them, and re-layouts  31.7 us (6%)
  between operations  15.1 us (3%)
    pallas_call x23, Pallas kernels, __call__(): pl.pallas_call(body, grid_spec=pltpu.PrefetchScalarGridSpec(num_scalar_pr...  241 us
    ppermute x30, waiting for transfers between devices, move(): lax.ppermute(part, axes, shifted(d, back))  41.5 us
    all_to_all x1, blocking collectives, dense_over_chips(): lax.all_to_all(parts, 'rep', split_axis=0, concat_axis=0, axis_index_grou...  34.9 us
    reduce_scatter x2, waiting for transfers between devices, summed(): lax.psum_scatter(wire, 'rep', scatter_dimension=0, axis_index_groups=grou...  32.9 us
    ppermute x12, waiting for transfers between devices, go_back(): return part if d == 0 else lax.ppermute(part, axes, shifted(d, True))  32.7 us
    all_to_all x1, blocking collectives, dense_over_chips(): lax.all_to_all(jnp.broadcast_to(share, parts.shape), 'rep', split_axis=0,...  31 us
    unnamed x142, local copies, waits for them, and re-layouts  26.1 us
    ppermute x30, starting transfers between devices, move(): lax.ppermute(part, axes, shifted(d, back))  23.4 us
  transfers between devices with their start and end apart: 51, of which 19 were waited for; matrix products, arithmetic and copies ran while one was open for 3% of the time, Pallas kernels for 35%

profile of v3, /device:TPU:0, one launch (start us, length us, event | category | flops | bytes accessed | tf_op | source)
XLA Modules:
  0.0 516.4 jit_solution(15345268758864601184)
XLA Ops:
  15.1 6.8 %route.1 = (s32[2,8,1024]{2,1,0:T(8,128)}, s32[2,4,208,128]{3,2,1,0:T(8,128)}) custom-call(s32[2]{0:T(128)} %pad_add_fusion.refs_0_, s32[2,788,2]{2,1,0:T(8,128)} %copy.37.refs_1_, s32[2,788,2]{2,1,0:T(8,128)} %copy.38.refs_2_), custom_call_target="tpu_custom_call" | custom-call | flops 40000000 | bytes 1000000 | tf_op jit(solution)/shard_map/route/pallas_call | solution.py:663
  21.9 17.3 %forward.2 = (bf16[4,208,1536]{2,1,0:T(8,128)(2,1)}, bf16[4,8,208,208]{3,2,1,0:T(8,128)(2,1)}, bf16[4,208,512]{2,1,0:T(8,128)(2,1)}, f32[4,208,512]{2,1,0:T(8,12...) custom-call(s32[2]{0:T(128)} %pad_add_fusion.refs_0_, ...), custom_call_target="tpu_custom_call" | custom-call | flops 6000000000 | bytes 20000000 | tf_op jit(solution)/shard_map/forward/pallas_call | solution.py:663
  44.5 4.2 collective-permute-done.1.refs_3_
  48.6 4.1 collective-permute-done.2.refs_4_
  53.5 7.9 %expert.6 = (bf16[208,512]{1,0:T(8,128)(2,1)}, bf16[208,512]{1,0:T(8,128)(2,1)}, bf16[208,512]{1,0:T(8,128)(2,1)}, bf16[208,512]{1,0:T(8,128)(2,1)}) custom-call(s32[2]{0:T(128)} %pad_add_fusion.refs_0_, bf16[208,512]{1,0:T(8,128)(2,1)} %get-tuple-element.123.refs_1_, bf16[208,512]{1,0:T(8,128)(2,1)} %copy-done.4, bf16[208,512]{1,0:T(8,128)(2,1)} %copy-done.5, ...), custom_call_target="tpu_custom_call" | custom-call | flops 1 | bytes 1 | tf_op jit(solution)/shard_map/expert/pallas_call | solution.py:663
  64.4 8.2 %expert.7 = (bf16[208,512]{1,0:T(8,128)(2,1)}, bf16[208,512]{1,0:T(8,128)(2,1)}, bf16[208,512]{1,0:T(8,128)(2,1)}, bf16[208,512]{1,0:T(8,128)(2,1)}) custom-call(s32[2]{0:T(128)} %pad_add_fusion.refs_0_, bf16[208,512]{1,0:T(8,128)(2,1)} %get-tuple-element.129.refs_1_, bf16[208,512]{1,0:T(8,128)(2,1)} %copy-done.7, bf16[208,512]{1,0:T(8,128)(2,1)} %copy-done.8, ...), custom_call_target="tpu_custom_call" | custom-call | flops 1 | bytes 1 | tf_op jit(solution)/shard_map/expert/pallas_call | solution.py:663
  76.5 4.1 spread_cotangent.1
  85.9 21.5 %forward.3 = (f32[4,208,512]{2,1,0:T(8,128)}, bf16[4,208,1536]{2,1,0:T(8,128)(2,1)}, bf16[4,8,208,208]{3,2,1,0:T(8,128)(2,1)}, bf16[4,208,512]{2,1,0:T(8,128)(2,...) custom-call(s32[2]{0:T(128)} %pad_add_fusion.refs_0_, ...), custom_call_target="tpu_custom_call" | custom-call | flops 6000000000 | bytes 20000000 | tf_op jit(solution)/shard_map/forward/pallas_call | solution.py:663
  111.7 4.6 collective-permute-done.19.refs_3_
  116.3 3.9 collective-permute-done.20.refs_4_
  121.0 14.0 %expert.8 = (bf16[208,512]{1,0:T(8,128)(2,1)}, bf16[208,512]{1,0:T(8,128)(2,1)}, bf16[208,512]{1,0:T(8,128)(2,1)}, bf16[208,512]{1,0:T(8,128)(2,1)}, bf16[208,51...) custom-call(s32[2]{0:T(128)} %pad_add_fusion.refs_0_, ...), custom_call_target="tpu_custom_call" | custom-call | flops 1 | bytes 1 | tf_op jit(solution)/shard_map/expert/pallas_call | solution.py:663
  135.9 14.3 %expert.9 = (bf16[416,512]{1,0:T(8,128)(2,1)}, bf16[416,512]{1,0:T(8,128)(2,1)}, bf16[416,512]{1,0:T(8,128)(2,1)}, bf16[416,512]{1,0:T(8,128)(2,1)}, bf16[208,51...) custom-call(s32[2]{0:T(128)} %pad_add_fusion.refs_0_, ...), custom_call_target="tpu_custom_call" | custom-call | flops 1 | bytes 1 | tf_op jit(solution)/shard_map/expert/pallas_call | solution.py:663
  150.2 9.9 %weights.4.refs_8_ = bf16[16,512,512]{2,1,0:T(8,128)(2,1)} custom-call(s32[2]{0:T(128)} %pad_add_fusion.refs_0_, bf16[208,512]{1,0:T(8,128)(2,1)} %get-tuple-element.150.refs_1_, bf16[208,512]{1,0:T(8,128)(2,1)} %copy-done.17, bf16[208,512]{1,0:T(8,128)(2,1)} %copy-done.18, bf16[208,512]{1,0:T(8,128)(2,1)} %copy-done.19, ...), custom_call_target="tpu_custom_call" | custom-call | flops 1 | bytes 1 | tf_op jit(solution)/shard_map/weights/pallas_call | solution.py:663
  160.1 9.9 %weights.5.refs_25_ = bf16[16,512,512]{2,1,0:T(8,128)(2,1)} custom-call(s32[2]{0:T(128)} %pad_add_fusion.refs_0_, bf16[208,512]{1,0:T(8,128)(2,1)} %get-tuple-element.143.refs_1_, bf16[208,512]{1,0:T(8,128)(2,1)} %copy-done.20, bf16[208,512]{1,0:T(8,128)(2,1)} %copy-done.21, bf16[208,512]{1,0:T(8,128)(2,1)} %copy-done.22, ...), custom_call_target="tpu_custom_call", output_to_operand_aliasing={{}: (8, {})} | custom-call | flops 1 | bytes 1 | tf_op jit(solution)/shard_map/weights/pallas_call | solution.py:663
  175.4 4.1 collective-permute-done.26.refs_14_
  179.5 3.8 collective-permute-done.28.refs_16_
  183.4 5.3 %collective-permute-done.27.refs_15_ = bf16[208,512]{1,0:T(8,128)(2,1)S(1)} collective-permute-done((bf16[208,512]{1,0:T(8,128)(2,1)S(1)}, bf16[208,512]{1,0:T(8,128)(2,1)S(1)}, u32[]{:S(2)}, u32[]{:S(2)}) %collective-permute-start.27) | collective-permute-done | bytes 213024 | tf_op jit(solution)/shard_map/ppermute | solution.py:793
  192.3 30.8 %backward.2 = (f32[4,208,512]{2,1,0:T(8,128)}, bf16[2,128,2176]{2,1,0:T(8,128)(2,1)}, bf16[2,128,2176]{2,1,0:T(8,128)(2,1)}, bf16[208,512]{1,0:T(8,128)(2,1)}, b...) custom-call(s32[2]{0:T(128)} %pad_add_fusion.refs_0_, ...), custom_call_target="tpu_custom_call" | custom-call | flops 12000000000 | bytes 30000000 | tf_op jit(solution)/shard_map/backward/pallas_call | solution.py:663
  229.1 21.3 %collective-permute-done.31.refs_7_ = bf16[208,512]{1,0:T(8,128)(2,1)S(1)} collective-permute-done((bf16[208,512]{1,0:T(8,128)(2,1)}, bf16[208,512]{1,0:T(8,128)(2,1)S(1)}, u32[]{:S(2)}, u32[]{:S(2)}) %collective-permute-start.31) | collective-permute-done | bytes 213024 | tf_op jit(solution)/shard_map/ppermute | solution.py:789
  253.7 6.2 %block_out.1.refs_15_ = f32[4,197,512]{2,1,0:T(8,128)} custom-call(f32[4,208,512]{2,1,0:T(8,128)} %get-tuple-element.141.refs_6_.refs_0_, f32[4,208,128]{2,1,0:T(8,128)} %get-tuple-element.142.refs_1_, s32[2,4,208,128]{3,2,1,0:T(8,128)} %get-tuple-element.119.refs_9_.refs_3_.refs_19_.refs_2_, bf16[416,512]{1,0:T(8,128)(2,1)} %get-tuple-element.159.refs_8_.refs_3_, ...), custom_call_target="tpu_custom_call" | custom-call | flops 1417674752 | bytes 6000000 | tf_op jit(solution)/shard_map/block_out/pallas_call | solution.py:663
  260.6 12.1 %expert.10 = (bf16[208,512]{1,0:T(8,128)(2,1)}, bf16[208,512]{1,0:T(8,128)(2,1)}, bf16[208,512]{1,0:T(8,128)(2,1)}, bf16[208,512]{1,0:T(8,128)(2,1)}, bf16[832,2...) custom-call(s32[2]{0:T(128)} %pad_add_fusion.refs_0_, ...), custom_call_target="tpu_custom_call" | custom-call | flops 1 | bytes 1 | tf_op jit(solution)/shard_map/expert/pallas_call | solution.py:663
  277.3 12.2 %expert.11 = (bf16[208,512]{1,0:T(8,128)(2,1)}, bf16[208,512]{1,0:T(8,128)(2,1)}, bf16[208,512]{1,0:T(8,128)(2,1)}, bf16[208,512]{1,0:T(8,128)(2,1)}, bf16[832,2...) custom-call(s32[2]{0:T(128)} %pad_add_fusion.refs_0_, ...), custom_call_target="tpu_custom_call" | custom-call | flops 1 | bytes 1 | tf_op jit(solution)/shard_map/expert/pallas_call | solution.py:663
  289.4 10.1 %weights.6.refs_8_ = bf16[16,512,512]{2,1,0:T(8,128)(2,1)} custom-call(s32[2]{0:T(128)} %pad_add_fusion.refs_0_, bf16[208,512]{1,0:T(8,128)(2,1)} %get-tuple-element.123.refs_1_, bf16[208,512]{1,0:T(8,128)(2,1)} %copy-done.4, bf16[208,512]{1,0:T(8,128)(2,1)} %copy-done.5, bf16[208,512]{1,0:T(8,128)(2,1)} %copy-done.6, ...), custom_call_target="tpu_custom_call" | custom-call | flops 1 | bytes 1 | tf_op jit(solution)/shard_map/weights/pallas_call | solution.py:663
  299.5 10.1 %weights.7.refs_24_ = bf16[16,512,512]{2,1,0:T(8,128)(2,1)} custom-call(s32[2]{0:T(128)} %pad_add_fusion.refs_0_, bf16[208,512]{1,0:T(8,128)(2,1)} %get-tuple-element.129.refs_1_, bf16[208,512]{1,0:T(8,128)(2,1)} %copy-done.7, bf16[208,512]{1,0:T(8,128)(2,1)} %copy-done.8, bf16[208,512]{1,0:T(8,128)(2,1)} %copy-done.9, ...), custom_call_target="tpu_custom_call", output_to_operand_aliasing={{}: (8, {})} | custom-call | flops 1 | bytes 1 | tf_op jit(solution)/shard_map/weights/pallas_call | solution.py:663
  314.7 4.5 collective-permute-done.39.refs_14_
  322.2 6.1 %collective-permute-done.40.refs_15_ = bf16[208,512]{1,0:T(8,128)(2,1)S(1)} collective-permute-done((bf16[208,512]{1,0:T(8,128)(2,1)S(1)}, bf16[208,512]{1,0:T(8,128)(2,1)S(1)}, u32[]{:S(2)}, u32[]{:S(2)}) %collective-permute-start.40) | collective-permute-done | bytes 213024 | tf_op jit(solution)/shard_map/ppermute | solution.py:793
  331.9 28.0 %backward.3 = (f32[4,197,512]{2,1,0:T(8,128)}, bf16[2,128,2176]{2,1,0:T(8,128)(2,1)}, bf16[2,128,2176]{2,1,0:T(8,128)(2,1)}) custom-call(s32[2]{0:T(128)} %pad_add_fusion.refs_0_, f32[4,208,512]{2,1,0:T(8,128)} %get-tuple-element.182.refs_7_.refs_1_, f32[4,197,512]{2,1,0:T(8,128)} %copy.39.refs_1_.refs_2_, ...), custom_call_target="tpu_custom_call" | custom-call | flops 12000000000 | bytes 30000000 | tf_op jit(solution)/shard_map/backward/pallas_call | solution.py:663
  368.3 7.9 %collective-permute-done.45.refs_1_ = bf16[128,2176]{1,0:T(8,128)(2,1)S(1)} collective-permute-done((bf16[128,2176]{1,0:T(8,128)(2,1)S(1)}, bf16[128,2176]{1,0:T(8,128)(2,1)S(1)}, u32[]{:S(2)}, u32[]{:S(2)}) %collective-permute-start.45) | collective-permute-done | bytes 557088 | tf_op jit(solution)/shard_map/ppermute | solution.py:635
  379.2 8.1 %collective-permute-done.44.refs_1_ = bf16[128,2176]{1,0:T(8,128)(2,1)S(1)} collective-permute-done((bf16[128,2176]{1,0:T(8,128)(2,1)}, bf16[128,2176]{1,0:T(8,128)(2,1)S(1)}, u32[]{:S(2)}, u32[]{:S(2)}) %collective-permute-start.44) | collective-permute-done | bytes 557088 | tf_op jit(solution)/shard_map/ppermute | solution.py:635
  391.4 34.9 %all_to_all.10 = bf16[8,2,16,2176]{3,2,1,0:T(8,128)(2,1)S(1)} all-to-all(bf16[8,2,16,2176]{3,2,1,0:T(8,128)(2,1)S(1)} %pad_maximum_fusion), channel_id=1, replica_groups={{0,4,8,12,16,20,24,28},{2,6,10,14,18,22,26,30},{1,5,9,13,17,21,25,29},{..., dimensions={0} | all-to-all | bytes 2228224 | tf_op jit(solution)/shard_map/all_to_all | solution.py:1000
  426.6 31.0 %all_to_all.11 = bf16[8,2,16,2176]{3,2,1,0:T(8,128)(2,1)S(1)} all-to-all(bf16[8,2,16,2176]{3,2,1,0:T(8,128)(2,1)S(1)} %broadcast_in_dim.2), channel_id=1, replica_groups={{0,4,8,12,16,20,24,28},{2,6,10,14,18,22,26,30},{1,5,9,13,17,21,25,29},{..., dimensions={0} | all-to-all | bytes 2228224 | tf_op jit(solution)/shard_map/all_to_all | solution.py:1004
  460.4 32.9 %reduce-scatter.3.cloned.1.call-done = bf16[2,512,512]{2,1,0:T(8,128)(2,1)} async-done(((bf16[16,512,512]{2,1,0:T(8,128)(2,1)}), bf16[2,512,512]{2,1,0:T(8,128)(2,1)}) %reduce-scatter.3.cloned.1.call-update) | async-done | bytes 1048592 | tf_op jit(solution)/shard_map/reduce_scatter | solution.py:1129
  (247 shorter events, 101.2 us)
Async XLA Ops:
  7.2 450.6 %reduce-scatter.5.cloned.1.call-start = ((), (), s32[]{:S(2)}) async-start(), calls=%async_computation.5 | async-start | bytes 9437184 | tf_op jit(solution)/shard_map/reduce_scatter | solution.py:1129
  42.3 10.5 %collective-permute-start.2 = (bf16[208,512]{1,0:T(8,128)(2,1)}, bf16[208,512]{1,0:T(8,128)(2,1)S(1)}, u32[]{:S(2)}, u32[]{:S(2)}) collective-permute-start(bf16[208,512]{1,0:T(8,128)(2,1)} %get-tuple-element.126), channel_id=1, source_target_pairs={{0,3},{1,2},{2,1},{3,0},{4,7},{5,6},{6,5},{7,4},{8,11},{9,10},{10,... | collective-permute-start | bytes 638984 | tf_op jit(solution)/shard_map/ppermute | solution.py:789
  42.4 21.2 %collective-permute-start.3 = (bf16[208,512]{1,0:T(8,128)(2,1)}, bf16[208,512]{1,0:T(8,128)(2,1)S(1)}, u32[]{:S(2)}, u32[]{:S(2)}) collective-permute-start(bf16[208,512]{1,0:T(8,128)(2,1)} %get-tuple-element.130), channel_id=1, source_target_pairs={{0,2},{1,3},{2,0},{3,1},{4,6},{5,7},{6,4},{7,5},{8,10},{9,11},{10,... | collective-permute-start | bytes 638984 | tf_op jit(solution)/shard_map/ppermute | solution.py:789
  42.5 21.0 %collective-permute-start.4 = (bf16[208,512]{1,0:T(8,128)(2,1)}, bf16[208,512]{1,0:T(8,128)(2,1)S(1)}, u32[]{:S(2)}, u32[]{:S(2)}) collective-permute-start(bf16[208,512]{1,0:T(8,128)(2,1)} %get-tuple-element.131), channel_id=1, source_target_pairs={{0,1},{1,0},{2,3},{3,2},{4,5},{5,4},{6,7},{7,6},{8,9},{9,8},{10,11... | collective-permute-start | bytes 638984 | tf_op jit(solution)/shard_map/ppermute | solution.py:789
  44.5 19.1 %collective-permute-start.5 = (bf16[208,512]{1,0:T(8,128)(2,1)}, bf16[208,512]{1,0:T(8,128)(2,1)S(1)}, u32[]{:S(2)}, u32[]{:S(2)}) collective-permute-start(bf16[208,512]{1,0:T(8,128)(2,1)} %get-tuple-element.132), channel_id=1, source_target_pairs={{0,3},{1,2},{2,1},{3,0},{4,7},{5,6},{6,5},{7,4},{8,11},{9,10},{10,... | collective-permute-start | bytes 638984 | tf_op jit(solution)/shard_map/ppermute | solution.py:789
  61.4 13.4 %collective-permute-start.6 = (bf16[208,512]{1,0:T(8,128)(2,1)}, bf16[208,512]{1,0:T(8,128)(2,1)S(1)}, u32[]{:S(2)}, u32[]{:S(2)}) collective-permute-start(bf16[208,512]{1,0:T(8,128)(2,1)} %get-tuple-element.134.refs_10_), channel_id=1, source_target_pairs={{2,0},{3,1},{0,2},{1,3},{6,4},{7,5},{4,6},{5,7},{10,8},{11,9},{8,1... | collective-permute-start | bytes 638984 | tf_op jit(solution)/shard_map/ppermute | solution.py:789
  61.6 19.1 %collective-permute-start.8 = (bf16[208,512]{1,0:T(8,128)(2,1)}, bf16[208,512]{1,0:T(8,128)(2,1)S(1)}, u32[]{:S(2)}, u32[]{:S(2)}) collective-permute-start(bf16[208,512]{1,0:T(8,128)(2,1)} %get-tuple-element.136.refs_11_), channel_id=1, source_target_pairs={{1,0},{0,1},{3,2},{2,3},{5,4},{4,5},{7,6},{6,7},{9,8},{8,9},{11,10... | collective-permute-start | bytes 638984 | tf_op jit(solution)/shard_map/ppermute | solution.py:789
  63.6 17.4 %collective-permute-start.10 = (bf16[208,512]{1,0:T(8,128)(2,1)}, bf16[208,512]{1,0:T(8,128)(2,1)S(1)}, u32[]{:S(2)}, u32[]{:S(2)}) collective-permute-start(bf16[208,512]{1,0:T(8,128)(2,1)} %get-tuple-element.138.refs_12_), channel_id=1, source_target_pairs={{3,0},{2,1},{1,2},{0,3},{7,4},{6,5},{5,6},{4,7},{11,8},{10,9},{9,1... | collective-permute-start | bytes 638984 | tf_op jit(solution)/shard_map/ppermute | solution.py:789
  74.7 10.5 %collective-permute-start.11 = (bf16[208,512]{1,0:T(8,128)(2,1)}, bf16[208,512]{1,0:T(8,128)(2,1)S(1)}, u32[]{:S(2)}, u32[]{:S(2)}) collective-permute-start(bf16[208,512]{1,0:T(8,128)(2,1)} %get-tuple-element.139.refs_12_), channel_id=1, source_target_pairs={{3,0},{2,1},{1,2},{0,3},{7,4},{6,5},{5,6},{4,7},{11,8},{10,9},{9,1... | collective-permute-start | bytes 638984 | tf_op jit(solution)/shard_map/ppermute | solution.py:789
  80.7 27.4 %collective-permute-start.15 = (bf16[416,512]{1,0:T(8,128)(2,1)}, bf16[416,512]{1,0:T(8,128)(2,1)S(1)}, u32[]{:S(2)}, u32[]{:S(2)}) collective-permute-start(bf16[416,512]{1,0:T(8,128)(2,1)} %get-tuple-element.147), channel_id=1, source_target_pairs={{0,2},{1,3},{2,0},{3,1},{4,6},{5,7},{6,4},{7,5},{8,10},{9,11},{10,... | collective-permute-start | bytes 1277960 | tf_op jit(solution)/shard_map/ppermute | solution.py:789
  80.9 28.9 %collective-permute-start.16 = (bf16[416,512]{1,0:T(8,128)(2,1)}, bf16[416,512]{1,0:T(8,128)(2,1)S(1)}, u32[]{:S(2)}, u32[]{:S(2)}) collective-permute-start(bf16[416,512]{1,0:T(8,128)(2,1)} %get-tuple-element.148), channel_id=1, source_target_pairs={{0,1},{1,0},{2,3},{3,2},{4,5},{5,4},{6,7},{7,6},{8,9},{9,8},{10,11... | collective-permute-start | bytes 1277960 | tf_op jit(solution)/shard_map/ppermute | solution.py:789
  82.9 27.1 %collective-permute-start.17 = (bf16[416,512]{1,0:T(8,128)(2,1)}, bf16[416,512]{1,0:T(8,128)(2,1)S(1)}, u32[]{:S(2)}, u32[]{:S(2)}) collective-permute-start(bf16[416,512]{1,0:T(8,128)(2,1)} %get-tuple-element.149), channel_id=1, source_target_pairs={{0,3},{1,2},{2,1},{3,0},{4,7},{5,6},{6,5},{7,4},{8,11},{9,10},{10,... | collective-permute-start | bytes 1277960 | tf_op jit(solution)/shard_map/ppermute | solution.py:789
  107.8 27.2 %collective-permute-start.12 = (bf16[208,512]{1,0:T(8,128)(2,1)}, bf16[208,512]{1,0:T(8,128)(2,1)S(1)}, u32[]{:S(2)}, u32[]{:S(2)}) collective-permute-start(bf16[208,512]{1,0:T(8,128)(2,1)} %get-tuple-element.144), channel_id=1, source_target_pairs={{0,2},{1,3},{2,0},{3,1},{4,6},{5,7},{6,4},{7,5},{8,10},{9,11},{10,... | collective-permute-start | bytes 638984 | tf_op jit(solution)/shard_map/ppermute | solution.py:789
  110.0 25.1 %collective-permute-start.13 = (bf16[208,512]{1,0:T(8,128)(2,1)}, bf16[208,512]{1,0:T(8,128)(2,1)S(1)}, u32[]{:S(2)}, u32[]{:S(2)}) collective-permute-start(bf16[208,512]{1,0:T(8,128)(2,1)} %get-tuple-element.145), channel_id=1, source_target_pairs={{0,1},{1,0},{2,3},{3,2},{4,5},{5,4},{6,7},{7,6},{8,9},{9,8},{10,11... | collective-permute-start | bytes 638984 | tf_op jit(solution)/shard_map/ppermute | solution.py:789
  111.7 23.4 %collective-permute-start.14 = (bf16[208,512]{1,0:T(8,128)(2,1)}, bf16[208,512]{1,0:T(8,128)(2,1)S(1)}, u32[]{:S(2)}, u32[]{:S(2)}) collective-permute-start(bf16[208,512]{1,0:T(8,128)(2,1)} %get-tuple-element.146), channel_id=1, source_target_pairs={{0,3},{1,2},{2,1},{3,0},{4,7},{5,6},{6,5},{7,4},{8,11},{9,10},{10,... | collective-permute-start | bytes 638984 | tf_op jit(solution)/shard_map/ppermute | solution.py:789
  170.1 323.1 %reduce-scatter.3.cloned.1.call-start = ((), (), s32[]{:S(2)}) async-start(), calls=%async_computation.4 | async-start | bytes 9437184 | tf_op jit(solution)/shard_map/reduce_scatter | solution.py:1129
  173.6 15.1 %collective-permute-start.27 = (bf16[208,512]{1,0:T(8,128)(2,1)S(1)}, bf16[208,512]{1,0:T(8,128)(2,1)S(1)}, u32[]{:S(2)}, u32[]{:S(2)}) collective-permute-start(bf16[208,512]{1,0:T(8,128)(2,1)S(1)} %copy-done.47), channel_id=1, source_target_pairs={{1,0},{0,1},{3,2},{2,3},{5,4},{4,5},{7,6},{6,7},{9,8},{8,9},{11,10... | collective-permute-start | bytes 638984 | tf_op jit(solution)/shard_map/ppermute | solution.py:793
  175.3 16.3 %collective-permute-start.29 = (bf16[208,512]{1,0:T(8,128)(2,1)S(1)}, bf16[208,512]{1,0:T(8,128)(2,1)S(1)}, u32[]{:S(2)}, u32[]{:S(2)}) collective-permute-start(bf16[208,512]{1,0:T(8,128)(2,1)S(1)} %copy-done.44), channel_id=1, source_target_pairs={{3,0},{2,1},{1,2},{0,3},{7,4},{6,5},{5,6},{4,7},{11,8},{10,9},{9,1... | collective-permute-start | bytes 638984 | tf_op jit(solution)/shard_map/ppermute | solution.py:793
  223.1 49.6 %collective-permute-start.36 = (bf16[2,128,2176]{2,1,0:T(8,128)(2,1)}, bf16[2,128,2176]{2,1,0:T(8,128)(2,1)S(1)}, u32[]{:S(2)}, u32[]{:S(2)}) collective-permute-start(bf16[2,128,2176]{2,1,0:T(8,128)(2,1)} %get-tuple-element.197), channel_id=1, source_target_pairs={{0,2},{2,0},{4,6},{6,4},{8,10},{10,8},{12,14},{14,12},{16,18},{18,... | collective-permute-start | bytes 3342344 | tf_op jit(solution)/shard_map/ppermute | solution.py:635
  224.2 26.9 %collective-permute-start.21 = (bf16[416,512]{1,0:T(8,128)(2,1)S(1)}, bf16[416,512]{1,0:T(8,128)(2,1)S(1)}, u32[]{:S(2)}, u32[]{:S(2)}) collective-permute-start(bf16[416,512]{1,0:T(8,128)(2,1)S(1)} %copy-done.36), channel_id=1, source_target_pairs={{2,0},{3,1},{0,2},{1,3},{6,4},{7,5},{4,6},{5,7},{10,8},{11,9},{8,1... | collective-permute-start | bytes 1277960 | tf_op jit(solution)/shard_map/ppermute | solution.py:789
  224.6 27.6 %collective-permute-start.22 = (bf16[416,512]{1,0:T(8,128)(2,1)}, bf16[416,512]{1,0:T(8,128)(2,1)S(1)}, u32[]{:S(2)}, u32[]{:S(2)}) collective-permute-start(bf16[416,512]{1,0:T(8,128)(2,1)} %get-tuple-element.161), channel_id=1, source_target_pairs={{1,0},{0,1},{3,2},{2,3},{5,4},{4,5},{7,6},{6,7},{9,8},{8,9},{11,10... | collective-permute-start | bytes 1277960 | tf_op jit(solution)/shard_map/ppermute | solution.py:789
  226.4 26.1 %collective-permute-start.23 = (bf16[416,512]{1,0:T(8,128)(2,1)S(1)}, bf16[416,512]{1,0:T(8,128)(2,1)S(1)}, u32[]{:S(2)}, u32[]{:S(2)}) collective-permute-start(bf16[416,512]{1,0:T(8,128)(2,1)S(1)} %copy-done.35), channel_id=1, source_target_pairs={{3,0},{2,1},{1,2},{0,3},{7,4},{6,5},{5,6},{4,7},{11,8},{10,9},{9,1... | collective-permute-start | bytes 1277960 | tf_op jit(solution)/shard_map/ppermute | solution.py:789
  227.3 23.0 %collective-permute-start.31 = (bf16[208,512]{1,0:T(8,128)(2,1)}, bf16[208,512]{1,0:T(8,128)(2,1)S(1)}, u32[]{:S(2)}, u32[]{:S(2)}) collective-permute-start(bf16[208,512]{1,0:T(8,128)(2,1)} %get-tuple-element.189), channel_id=1, source_target_pairs={{0,1},{1,0},{2,3},{3,2},{4,5},{5,4},{6,7},{7,6},{8,9},{9,8},{10,11... | collective-permute-start | bytes 638984 | tf_op jit(solution)/shard_map/ppermute | solution.py:789
  251.1 25.4 %collective-permute-start.33 = (bf16[208,512]{1,0:T(8,128)(2,1)}, bf16[208,512]{1,0:T(8,128)(2,1)S(1)}, u32[]{:S(2)}, u32[]{:S(2)}) collective-permute-start(bf16[208,512]{1,0:T(8,128)(2,1)} %get-tuple-element.193), channel_id=1, source_target_pairs={{0,2},{1,3},{2,0},{3,1},{4,6},{5,7},{6,4},{7,5},{8,10},{9,11},{10,... | collective-permute-start | bytes 638984 | tf_op jit(solution)/shard_map/ppermute | solution.py:789
  252.2 24.2 %collective-permute-start.34 = (bf16[208,512]{1,0:T(8,128)(2,1)}, bf16[208,512]{1,0:T(8,128)(2,1)S(1)}, u32[]{:S(2)}, u32[]{:S(2)}) collective-permute-start(bf16[208,512]{1,0:T(8,128)(2,1)} %get-tuple-element.194), channel_id=1, source_target_pairs={{0,1},{1,0},{2,3},{3,2},{4,5},{5,4},{6,7},{7,6},{8,9},{9,8},{10,11... | collective-permute-start | bytes 638984 | tf_op jit(solution)/shard_map/ppermute | solution.py:789
  252.5 23.9 %collective-permute-start.35 = (bf16[208,512]{1,0:T(8,128)(2,1)}, bf16[208,512]{1,0:T(8,128)(2,1)S(1)}, u32[]{:S(2)}, u32[]{:S(2)}) collective-permute-start(bf16[208,512]{1,0:T(8,128)(2,1)} %get-tuple-element.195), channel_id=1, source_target_pairs={{0,3},{1,2},{2,1},{3,0},{4,7},{5,6},{6,5},{7,4},{8,11},{9,10},{10,... | collective-permute-start | bytes 638984 | tf_op jit(solution)/shard_map/ppermute | solution.py:789
  313.3 15.1 %collective-permute-start.40 = (bf16[208,512]{1,0:T(8,128)(2,1)S(1)}, bf16[208,512]{1,0:T(8,128)(2,1)S(1)}, u32[]{:S(2)}, u32[]{:S(2)}) collective-permute-start(bf16[208,512]{1,0:T(8,128)(2,1)S(1)} %copy-done.50), channel_id=1, source_target_pairs={{1,0},{0,1},{3,2},{2,3},{5,4},{4,5},{7,6},{6,7},{9,8},{8,9},{11,10... | collective-permute-start | bytes 638984 | tf_op jit(solution)/shard_map/ppermute | solution.py:793
  314.2 17.0 %collective-permute-start.42 = (bf16[208,512]{1,0:T(8,128)(2,1)S(1)}, bf16[208,512]{1,0:T(8,128)(2,1)S(1)}, u32[]{:S(2)}, u32[]{:S(2)}) collective-permute-start(bf16[208,512]{1,0:T(8,128)(2,1)S(1)} %copy-done.48), channel_id=1, source_target_pairs={{3,0},{2,1},{1,2},{0,3},{7,4},{6,5},{5,6},{4,7},{11,8},{10,9},{9,1... | collective-permute-start | bytes 638984 | tf_op jit(solution)/shard_map/ppermute | solution.py:793
  360.7 15.5 %collective-permute-start.45 = (bf16[128,2176]{1,0:T(8,128)(2,1)S(1)}, bf16[128,2176]{1,0:T(8,128)(2,1)S(1)}, u32[]{:S(2)}, u32[]{:S(2)}) collective-permute-start(bf16[128,2176]{1,0:T(8,128)(2,1)S(1)} %copy-done.34), channel_id=1, source_target_pairs={{0,1},{1,0},{2,3},{3,2},{4,5},{5,4},{6,7},{7,6},{8,9},{9,8},{10,11... | collective-permute-start | bytes 1671176 | tf_op jit(solution)/shard_map/ppermute | solution.py:635
  367.0 20.3 %collective-permute-start.44 = (bf16[128,2176]{1,0:T(8,128)(2,1)}, bf16[128,2176]{1,0:T(8,128)(2,1)S(1)}, u32[]{:S(2)}, u32[]{:S(2)}) collective-permute-start(bf16[128,2176]{1,0:T(8,128)(2,1)} %get-tuple-element.216), channel_id=1, source_target_pairs={{0,1},{1,0},{2,3},{3,2},{4,5},{5,4},{6,7},{7,6},{8,9},{9,8},{10,11... | collective-permute-start | bytes 1671176 | tf_op jit(solution)/shard_map/ppermute | solution.py:635
  457.7 42.2 %collective-permute-start.46 = (bf16[2,128,2176]{2,1,0:T(8,128)(2,1)S(1)}, bf16[2,128,2176]{2,1,0:T(8,128)(2,1)}, u32[]{:S(2)}, u32[]{:S(2)}) collective-permute-start(bf16[2,128,2176]{2,1,0:T(8,128)(2,1)S(1)} %bitcast.12), channel_id=1, source_target_pairs={{0,2},{2,0},{4,6},{6,4},{8,10},{10,8},{12,14},{14,12},{16,18},{18,... | collective-permute-start | bytes 3342344 | tf_op jit(solution)/shard_map/ppermute | solution.py:635
  460.4 45.0 %collective-permute-start.48 = (bf16[1,512,512]{2,1,0:T(8,128)(2,1)S(1)}, bf16[1,512,512]{2,1,0:T(8,128)(2,1)}, u32[]{:S(2)}, u32[]{:S(2)}) collective-permute-start(bf16[1,512,512]{2,1,0:T(8,128)(2,1)S(1)} %get-tuple-element.249), channel_id=1, source_target_pairs={{0,2},{2,0},{4,6},{6,4},{8,10},{10,8},{12,14},{14,12},{16,18},{18,... | collective-permute-start | bytes 1572872 | tf_op jit(solution)/shard_map/ppermute | solution.py:635
  (86 other events, 617.4 us)
Sparse Core Ops, SparseCore 0:
  170.2 150.5 reduce-scatter.4
  324.9 168.2 reduce-scatter.2

commit v4 on v3

--- a/solution.py
+++ b/solution.py
@@ -14,7 +14,7 @@
 WIDE = 256
 F32 = jnp.float32
 BF16 = jnp.bfloat16
-VMEM_LIMIT = 60 * 1024 * 1024
+VMEM_LIMIT = 40 * 1024 * 1024
 
 
 def round_up(value, multiple):

time: 526 us -> 515 us (0.979)
  Pallas kernels: 241 us -> 197 us
  local copies, waits for them, and re-layouts: 31.7 us -> 55.9 us
  blocking collectives: 66 us -> 77.8 us
    pallas_call x23, Pallas kernels: 241 us -> 197 us  [__call__(): pl.pallas_call(body, grid_spec=pltpu.PrefetchScalarGridSpec(num_scalar_pr...]
    unnamed x142 -> x260, local copies, waits for them, and re-layouts: 26.1 us -> 50.2 us
    reduce_scatter x2, waiting for transfers between devices: 32.9 us -> 19.6 us  [summed(): lax.psum_scatter(wire, 'rep', scatter_dimension=0, axis_index_groups=grou...]
    all_to_all x1, blocking collectives: 31 us -> 42.3 us  [dense_over_chips(): lax.all_to_all(jnp.broadcast_to(share, parts.shape), 'rep', split_axis=0,...]
    ppermute x7, waiting for transfers between devices: 17.3 us -> 22.8 us  [swap(): return lax.ppermute(values, axis, [(r, r ^ distance) for r in range(total)])]
  transfers between devices with their start and end apart: 51 -> 51, of which waited for: 19 -> 22; matrix products, arithmetic and copies ran while one was open for 3% -> 3% of each run, Pallas kernels for 35% -> 29%
where the time goes in v4:
time: 515 us; the launch traced here: 506 us
  Pallas kernels  197 us (38%)
  waiting for transfers between devices  120 us (23%)
  blocking collectives  77.8 us (15%)
  local copies, waits for them, and re-layouts  55.9 us (11%)
  starting transfers between devices  37.6 us (7%)
  between operations  15.8 us (3%)
    pallas_call x23, Pallas kernels, __call__(): pl.pallas_call(body, grid_spec=pltpu.PrefetchScalarGridSpec(num_scalar_pr...  197 us
    unnamed x260, local copies, waits for them, and re-layouts  50.2 us
    ppermute x30, waiting for transfers between devices, move(): lax.ppermute(part, axes, shifted(d, back))  43.7 us
    all_to_all x1, blocking collectives, dense_over_chips(): lax.all_to_all(jnp.broadcast_to(share, parts.shape), 'rep', split_axis=0,...  42.3 us
    all_to_all x1, blocking collectives, dense_over_chips(): lax.all_to_all(parts, 'rep', split_axis=0, concat_axis=0, axis_index_grou...  35.5 us
    ppermute x12, waiting for transfers between devices, go_back(): return part if d == 0 else lax.ppermute(part, axes, shifted(d, True))  33.8 us
    ppermute x30, starting transfers between devices, move(): lax.ppermute(part, axes, shifted(d, back))  23.6 us
    ppermute x7, waiting for transfers between devices, swap(): return lax.ppermute(values, axis, [(r, r ^ distance) for r in range(total)])  22.8 us
  transfers between devices with their start and end apart: 51, of which 22 were waited for; matrix products, arithmetic and copies ran while one was open for 3% of the time, Pallas kernels for 29%

profile of v4, /device:TPU:0, one launch (start us, length us, event | category | flops | bytes accessed | tf_op | source)
XLA Modules:
  0.0 505.8 jit_solution(17811572591642841383)
XLA Ops:
  12.1 5.5 %route.1 = (s32[2,8,1024]{2,1,0:T(8,128)S(1)}, s32[2,4,208,128]{3,2,1,0:T(8,128)S(1)}) custom-call(s32[2]{0:T(128)S(1)} %pad_add_fusion.refs_0_, s32[2,788,2]{2,1,0:T(8,128)S(1)} %copy.37.refs_1_, s32[2,788,2]{2,1,0:T(8,128)S(1)} %copy.38.refs_2_), custom_call_target="tpu_custom_call" | custom-call | flops 40000000 | bytes 1000000 | tf_op jit(solution)/shard_map/route/pallas_call | solution.py:663
  19.2 15.6 %forward.2 = (bf16[4,208,1536]{2,1,0:T(8,128)(2,1)S(1)}, bf16[4,8,208,208]{3,2,1,0:T(8,128)(2,1)}, bf16[4,208,512]{2,1,0:T(8,128)(2,1)S(1)}, f32[4,208,512]{2,1,...) custom-call(s32[2]{0:T(128)S(1)} %pad_add_fusion.refs_0_, ...), custom_call_target="tpu_custom_call" | custom-call | flops 6000000000 | bytes 20000000 | tf_op jit(solution)/shard_map/forward/pallas_call | solution.py:663
  41.0 4.0 collective-permute-done.1.refs_3_
  44.9 4.0 collective-permute-done.2.refs_4_
  49.0 6.6 %expert.6 = (bf16[208,512]{1,0:T(8,128)(2,1)S(1)}, bf16[208,512]{1,0:T(8,128)(2,1)S(1)}, bf16[208,512]{1,0:T(8,128)(2,1)S(1)}, bf16[208,512]{1,0:T(8,128)(2,1)S(1)}) custom-call(s32[2]{0:T(128)S(1)} %pad_add_fusion.refs_0_, bf16[208,512]{1,0:T(8,128)(2,1)S(1)} %get-tuple-element.123.refs_1_, bf16[208,512]{1,0:T(8,128)(2,1)S(1)} %collective-permute-done.refs_2_, ...), custom_call_target="tpu_custom_call" | custom-call | flops 1 | bytes 1 | tf_op jit(solution)/shard_map/expert/pallas_call | solution.py:663
  58.1 6.8 %expert.7 = (bf16[208,512]{1,0:T(8,128)(2,1)S(1)}, bf16[208,512]{1,0:T(8,128)(2,1)S(1)}, bf16[208,512]{1,0:T(8,128)(2,1)S(1)}, bf16[208,512]{1,0:T(8,128)(2,1)S(1)}) custom-call(s32[2]{0:T(128)S(1)} %pad_add_fusion.refs_0_, bf16[208,512]{1,0:T(8,128)(2,1)S(1)} %get-tuple-element.129.refs_1_, bf16[208,512]{1,0:T(8,128)(2,1)S(1)} %collective-permute-done.3.refs_2_, ...), custom_call_target="tpu_custom_call" | custom-call | flops 1 | bytes 1 | tf_op jit(solution)/shard_map/expert/pallas_call | solution.py:663
  73.3 4.1 collective-permute-done.11.refs_11_
  77.4 19.4 %forward.3 = (f32[4,208,512]{2,1,0:T(8,128)S(1)}, bf16[4,208,1536]{2,1,0:T(8,128)(2,1)}, bf16[4,8,208,208]{3,2,1,0:T(8,128)(2,1)}, bf16[4,208,512]{2,1,0:T(8,128...) custom-call(s32[2]{0:T(128)S(1)} %pad_add_fusion.refs_0_, ...), custom_call_target="tpu_custom_call" | custom-call | flops 6000000000 | bytes 20000000 | tf_op jit(solution)/shard_map/forward/pallas_call | solution.py:663
  102.7 4.3 collective-permute-done.19.refs_3_
  107.0 4.0 collective-permute-done.20.refs_4_
  111.0 11.8 %expert.8 = (bf16[208,512]{1,0:T(8,128)(2,1)S(1)}, bf16[208,512]{1,0:T(8,128)(2,1)S(1)}, bf16[208,512]{1,0:T(8,128)(2,1)S(1)}, bf16[208,512]{1,0:T(8,128)(2,1)S(...) custom-call(s32[2]{0:T(128)S(1)} %pad_add_fusion.refs_0_, ...), custom_call_target="tpu_custom_call" | custom-call | flops 1 | bytes 1 | tf_op jit(solution)/shard_map/expert/pallas_call | solution.py:663
  129.8 11.4 %expert.9 = (bf16[416,512]{1,0:T(8,128)(2,1)S(1)}, bf16[416,512]{1,0:T(8,128)(2,1)S(1)}, bf16[416,512]{1,0:T(8,128)(2,1)S(1)}, bf16[416,512]{1,0:T(8,128)(2,1)S(...) custom-call(s32[2]{0:T(128)S(1)} %pad_add_fusion.refs_0_, ...), custom_call_target="tpu_custom_call" | custom-call | flops 1 | bytes 1 | tf_op jit(solution)/shard_map/expert/pallas_call | solution.py:663
  141.4 8.3 %weights.4.refs_8_ = bf16[16,512,512]{2,1,0:T(8,128)(2,1)} custom-call(s32[2]{0:T(128)S(1)} %pad_add_fusion.refs_0_, bf16[208,512]{1,0:T(8,128)(2,1)S(1)} %get-tuple-element.150.refs_1_, bf16[208,512]{1,0:T(8,128)(2,1)S(1)} %collective-permute-done.18.refs_2_, bf16[208,512]{1,0:T(8,128)(2,1)S(1)} %collective-permute-done.19.refs_3_, ...), custom_call_target="tpu_custom_call" | custom-call | flops 1 | bytes 1 | tf_op jit(solution)/shard_map/weights/pallas_call | solution.py:663
  149.7 8.4 %weights.5.refs_25_ = bf16[16,512,512]{2,1,0:T(8,128)(2,1)} custom-call(s32[2]{0:T(128)S(1)} %pad_add_fusion.refs_0_, bf16[208,512]{1,0:T(8,128)(2,1)S(1)} %copy-done.40, bf16[208,512]{1,0:T(8,128)(2,1)S(1)} %copy-done.42, bf16[208,512]{1,0:T(8,128)(2,1)S(1)} %collective-permute-done.13.refs_3_, ...), custom_call_target="tpu_custom_call", output_to_operand_aliasing={{}: (8, {})} | custom-call | flops 1 | bytes 1 | tf_op jit(solution)/shard_map/weights/pallas_call | solution.py:663
  162.9 4.2 collective-permute-done.26.refs_14_
  167.1 3.9 collective-permute-done.28.refs_16_
  171.0 5.2 %collective-permute-done.27.refs_15_ = bf16[208,512]{1,0:T(8,128)(2,1)S(1)} collective-permute-done((bf16[208,512]{1,0:T(8,128)(2,1)}, bf16[208,512]{1,0:T(8,128)(2,1)S(1)}, u32[]{:S(2)}, u32[]{:S(2)}) %collective-permute-start.27) | collective-permute-done | bytes 213024 | tf_op jit(solution)/shard_map/ppermute | solution.py:793
  176.2 3.9 collective-permute-done.29.refs_17_
  187.8 28.4 %backward.2 = (f32[4,208,512]{2,1,0:T(8,128)S(1)}, bf16[2,128,2176]{2,1,0:T(8,128)(2,1)S(1)}, bf16[2,128,2176]{2,1,0:T(8,128)(2,1)}, bf16[208,512]{1,0:T(8,128)(...) custom-call(s32[2]{0:T(128)S(1)} %pad_add_fusion.refs_0_, ...), custom_call_target="tpu_custom_call" | custom-call | flops 12000000000 | bytes 30000000 | tf_op jit(solution)/shard_map/backward/pallas_call | solution.py:663
  221.1 21.7 %collective-permute-done.31.refs_7_ = bf16[208,512]{1,0:T(8,128)(2,1)S(1)} collective-permute-done((bf16[208,512]{1,0:T(8,128)(2,1)S(1)}, bf16[208,512]{1,0:T(8,128)(2,1)S(1)}, u32[]{:S(2)}, u32[]{:S(2)}) %collective-permute-start.31) | collective-permute-done | bytes 213024 | tf_op jit(solution)/shard_map/ppermute | solution.py:789
  250.1 9.6 %expert.10 = (bf16[208,512]{1,0:T(8,128)(2,1)S(1)}, bf16[208,512]{1,0:T(8,128)(2,1)S(1)}, bf16[208,512]{1,0:T(8,128)(2,1)S(1)}, bf16[208,512]{1,0:T(8,128)(2,1)S...) custom-call(s32[2]{0:T(128)S(1)} %pad_add_fusion.refs_0_, ...), custom_call_target="tpu_custom_call" | custom-call | flops 1 | bytes 1 | tf_op jit(solution)/shard_map/expert/pallas_call | solution.py:663
  262.9 9.8 %expert.11 = (bf16[208,512]{1,0:T(8,128)(2,1)S(1)}, bf16[208,512]{1,0:T(8,128)(2,1)S(1)}, bf16[208,512]{1,0:T(8,128)(2,1)S(1)}, bf16[208,512]{1,0:T(8,128)(2,1)S...) custom-call(s32[2]{0:T(128)S(1)} %pad_add_fusion.refs_0_, ...), custom_call_target="tpu_custom_call" | custom-call | flops 1 | bytes 1 | tf_op jit(solution)/shard_map/expert/pallas_call | solution.py:663
  274.6 8.3 %weights.6.refs_8_ = bf16[16,512,512]{2,1,0:T(8,128)(2,1)} custom-call(s32[2]{0:T(128)S(1)} %pad_add_fusion.refs_0_, bf16[208,512]{1,0:T(8,128)(2,1)S(1)} %get-tuple-element.123.refs_1_, bf16[208,512]{1,0:T(8,128)(2,1)S(1)} %collective-permute-done.refs_2_, bf16[208,512]{1,0:T(8,128)(2,1)S(1)} %collective-permute-done.1.refs_3_, ...), custom_call_target="tpu_custom_call" | custom-call | flops 1 | bytes 1 | tf_op jit(solution)/shard_map/weights/pallas_call | solution.py:663
  285.0 8.3 %weights.7.refs_24_ = bf16[16,512,512]{2,1,0:T(8,128)(2,1)} custom-call(s32[2]{0:T(128)S(1)} %pad_add_fusion.refs_0_, bf16[208,512]{1,0:T(8,128)(2,1)S(1)} %get-tuple-element.129.refs_1_, bf16[208,512]{1,0:T(8,128)(2,1)S(1)} %copy-done.13, bf16[208,512]{1,0:T(8,128)(2,1)S(1)} %copy-done.15, ...), custom_call_target="tpu_custom_call", output_to_operand_aliasing={{}: (8, {})} | custom-call | flops 1 | bytes 1 | tf_op jit(solution)/shard_map/weights/pallas_call | solution.py:663
  298.5 4.5 collective-permute-done.39.refs_14_
  306.5 5.7 %collective-permute-done.40.refs_15_ = bf16[208,512]{1,0:T(8,128)(2,1)S(1)} collective-permute-done((bf16[208,512]{1,0:T(8,128)(2,1)S(1)}, bf16[208,512]{1,0:T(8,128)(2,1)S(1)}, u32[]{:S(2)}, u32[]{:S(2)}) %collective-permute-start.40) | collective-permute-done | bytes 213024 | tf_op jit(solution)/shard_map/ppermute | solution.py:793
  325.7 25.1 %backward.3 = (f32[4,197,512]{2,1,0:T(8,128)S(1)}, bf16[2,128,2176]{2,1,0:T(8,128)(2,1)S(1)}, bf16[2,128,2176]{2,1,0:T(8,128)(2,1)S(1)}) custom-call(s32[2]{0:T(128)S(1)} %pad_add_fusion.refs_0_, f32[4,208,512]{2,1,0:T(8,128)S(1)} %copy-done.29, f32[4,197,512]{2,1,0:T(8,128)S(1)} %copy-done.34, bf16[4,208,1536]{2,1,0:T(8,128)(2,1)} %copy-done.7, ...), custom_call_target="tpu_custom_call" | custom-call | flops 12000000000 | bytes 30000000 | tf_op jit(solution)/shard_map/backward/pallas_call | solution.py:663
  355.9 11.1 %collective-permute-done.45.refs_1_ = bf16[128,2176]{1,0:T(8,128)(2,1)S(1)} collective-permute-done((bf16[128,2176]{1,0:T(8,128)(2,1)S(1)}, bf16[128,2176]{1,0:T(8,128)(2,1)S(1)}, u32[]{:S(2)}, u32[]{:S(2)}) %collective-permute-start.45) | collective-permute-done | bytes 557088 | tf_op jit(solution)/shard_map/ppermute | solution.py:635
  367.1 10.9 %collective-permute-done.44.refs_1_ = bf16[128,2176]{1,0:T(8,128)(2,1)S(1)} collective-permute-done((bf16[128,2176]{1,0:T(8,128)(2,1)S(1)}, bf16[128,2176]{1,0:T(8,128)(2,1)S(1)}, u32[]{:S(2)}, u32[]{:S(2)}) %collective-permute-start.44) | collective-permute-done | bytes 557088 | tf_op jit(solution)/shard_map/ppermute | solution.py:635
  379.1 35.5 %all_to_all.10 = bf16[8,2,16,2176]{3,2,1,0:T(8,128)(2,1)} all-to-all(bf16[8,2,16,2176]{3,2,1,0:T(8,128)(2,1)S(1)} %pad_maximum_fusion), channel_id=1, replica_groups={{0,4,8,12,16,20,24,28},{2,6,10,14,18,22,26,30},{1,5,9,13,17,21,25,29},{..., dimensions={0} | all-to-all | bytes 2228224 | tf_op jit(solution)/shard_map/all_to_all | solution.py:1000
  416.2 42.3 %all_to_all.11 = bf16[8,2,16,2176]{3,2,1,0:T(8,128)(2,1)S(1)} all-to-all(bf16[8,2,16,2176]{3,2,1,0:T(8,128)(2,1)S(1)} %broadcast_in_dim.2), channel_id=1, replica_groups={{0,4,8,12,16,20,24,28},{2,6,10,14,18,22,26,30},{1,5,9,13,17,21,25,29},{..., dimensions={0} | all-to-all | bytes 2228224 | tf_op jit(solution)/shard_map/all_to_all | solution.py:1004
  462.3 19.6 %reduce-scatter.3.cloned.1.call-done = bf16[2,512,512]{2,1,0:T(8,128)(2,1)} async-done(((bf16[16,512,512]{2,1,0:T(8,128)(2,1)}), bf16[2,512,512]{2,1,0:T(8,128)(2,1)}) %reduce-scatter.3.cloned.1.call-update) | async-done | bytes 1048592 | tf_op jit(solution)/shard_map/reduce_scatter | solution.py:1129
  (365 shorter events, 117.9 us)
Async XLA Ops:
  7.2 452.3 %reduce-scatter.5.cloned.1.call-start = ((), (), s32[]{:S(2)}) async-start(), calls=%async_computation.5 | async-start | bytes 9437184 | tf_op jit(solution)/shard_map/reduce_scatter | solution.py:1129
  38.9 19.1 %collective-permute-start.3 = (bf16[208,512]{1,0:T(8,128)(2,1)S(1)}, bf16[208,512]{1,0:T(8,128)(2,1)S(1)}, u32[]{:S(2)}, u32[]{:S(2)}) collective-permute-start(bf16[208,512]{1,0:T(8,128)(2,1)S(1)} %get-tuple-element.130), channel_id=1, source_target_pairs={{0,2},{1,3},{2,0},{3,1},{4,6},{5,7},{6,4},{7,5},{8,10},{9,11},{10,... | collective-permute-start | bytes 638984 | tf_op jit(solution)/shard_map/ppermute | solution.py:789
  39.0 19.0 %collective-permute-start.4 = (bf16[208,512]{1,0:T(8,128)(2,1)S(1)}, bf16[208,512]{1,0:T(8,128)(2,1)S(1)}, u32[]{:S(2)}, u32[]{:S(2)}) collective-permute-start(bf16[208,512]{1,0:T(8,128)(2,1)S(1)} %get-tuple-element.131), channel_id=1, source_target_pairs={{0,1},{1,0},{2,3},{3,2},{4,5},{5,4},{6,7},{7,6},{8,9},{9,8},{10,11... | collective-permute-start | bytes 638984 | tf_op jit(solution)/shard_map/ppermute | solution.py:789
  41.0 17.1 %collective-permute-start.5 = (bf16[208,512]{1,0:T(8,128)(2,1)S(1)}, bf16[208,512]{1,0:T(8,128)(2,1)S(1)}, u32[]{:S(2)}, u32[]{:S(2)}) collective-permute-start(bf16[208,512]{1,0:T(8,128)(2,1)S(1)} %get-tuple-element.132), channel_id=1, source_target_pairs={{0,3},{1,2},{2,1},{3,0},{4,7},{5,6},{6,5},{7,4},{8,11},{9,10},{10,... | collective-permute-start | bytes 638984 | tf_op jit(solution)/shard_map/ppermute | solution.py:789
  55.6 11.6 %collective-permute-start.6 = (bf16[208,512]{1,0:T(8,128)(2,1)S(1)}, bf16[208,512]{1,0:T(8,128)(2,1)S(1)}, u32[]{:S(2)}, u32[]{:S(2)}) collective-permute-start(bf16[208,512]{1,0:T(8,128)(2,1)S(1)} %get-tuple-element.134.refs_10_), channel_id=1, source_target_pairs={{2,0},{3,1},{0,2},{1,3},{6,4},{7,5},{4,6},{5,7},{10,8},{11,9},{8,1... | collective-permute-start | bytes 638984 | tf_op jit(solution)/shard_map/ppermute | solution.py:789
  56.0 14.3 %collective-permute-start.8 = (bf16[208,512]{1,0:T(8,128)(2,1)S(1)}, bf16[208,512]{1,0:T(8,128)(2,1)S(1)}, u32[]{:S(2)}, u32[]{:S(2)}) collective-permute-start(bf16[208,512]{1,0:T(8,128)(2,1)S(1)} %get-tuple-element.136.refs_11_), channel_id=1, source_target_pairs={{1,0},{0,1},{3,2},{2,3},{5,4},{4,5},{7,6},{6,7},{9,8},{8,9},{11,10... | collective-permute-start | bytes 638984 | tf_op jit(solution)/shard_map/ppermute | solution.py:789
  58.0 12.6 %collective-permute-start.10 = (bf16[208,512]{1,0:T(8,128)(2,1)S(1)}, bf16[208,512]{1,0:T(8,128)(2,1)S(1)}, u32[]{:S(2)}, u32[]{:S(2)}) collective-permute-start(bf16[208,512]{1,0:T(8,128)(2,1)S(1)} %get-tuple-element.138.refs_12_), channel_id=1, source_target_pairs={{3,0},{2,1},{1,2},{0,3},{7,4},{6,5},{5,6},{4,7},{11,8},{10,9},{9,1... | collective-permute-start | bytes 638984 | tf_op jit(solution)/shard_map/ppermute | solution.py:789
  67.2 10.2 %collective-permute-start.11 = (bf16[208,512]{1,0:T(8,128)(2,1)S(1)}, bf16[208,512]{1,0:T(8,128)(2,1)S(1)}, u32[]{:S(2)}, u32[]{:S(2)}) collective-permute-start(bf16[208,512]{1,0:T(8,128)(2,1)S(1)} %get-tuple-element.139.refs_12_), channel_id=1, source_target_pairs={{3,0},{2,1},{1,2},{0,3},{7,4},{6,5},{5,6},{4,7},{11,8},{10,9},{9,1... | collective-permute-start | bytes 638984 | tf_op jit(solution)/shard_map/ppermute | solution.py:789
  70.3 28.7 %collective-permute-start.15 = (bf16[416,512]{1,0:T(8,128)(2,1)S(1)}, bf16[416,512]{1,0:T(8,128)(2,1)S(1)}, u32[]{:S(2)}, u32[]{:S(2)}) collective-permute-start(bf16[416,512]{1,0:T(8,128)(2,1)S(1)} %get-tuple-element.147), channel_id=1, source_target_pairs={{0,2},{1,3},{2,0},{3,1},{4,6},{5,7},{6,4},{7,5},{8,10},{9,11},{10,... | collective-permute-start | bytes 1277960 | tf_op jit(solution)/shard_map/ppermute | solution.py:789
  70.5 30.3 %collective-permute-start.16 = (bf16[416,512]{1,0:T(8,128)(2,1)S(1)}, bf16[416,512]{1,0:T(8,128)(2,1)S(1)}, u32[]{:S(2)}, u32[]{:S(2)}) collective-permute-start(bf16[416,512]{1,0:T(8,128)(2,1)S(1)} %get-tuple-element.148), channel_id=1, source_target_pairs={{0,1},{1,0},{2,3},{3,2},{4,5},{5,4},{6,7},{7,6},{8,9},{9,8},{10,11... | collective-permute-start | bytes 1277960 | tf_op jit(solution)/shard_map/ppermute | solution.py:789
  72.5 28.5 %collective-permute-start.17 = (bf16[416,512]{1,0:T(8,128)(2,1)S(1)}, bf16[416,512]{1,0:T(8,128)(2,1)S(1)}, u32[]{:S(2)}, u32[]{:S(2)}) collective-permute-start(bf16[416,512]{1,0:T(8,128)(2,1)S(1)} %get-tuple-element.149), channel_id=1, source_target_pairs={{0,3},{1,2},{2,1},{3,0},{4,7},{5,6},{6,5},{7,4},{8,11},{9,10},{10,... | collective-permute-start | bytes 1277960 | tf_op jit(solution)/shard_map/ppermute | solution.py:789
  98.8 26.3 %collective-permute-start.12 = (bf16[208,512]{1,0:T(8,128)(2,1)S(1)}, bf16[208,512]{1,0:T(8,128)(2,1)S(1)}, u32[]{:S(2)}, u32[]{:S(2)}) collective-permute-start(bf16[208,512]{1,0:T(8,128)(2,1)S(1)} %get-tuple-element.144), channel_id=1, source_target_pairs={{0,2},{1,3},{2,0},{3,1},{4,6},{5,7},{6,4},{7,5},{8,10},{9,11},{10,... | collective-permute-start | bytes 638984 | tf_op jit(solution)/shard_map/ppermute | solution.py:789
  101.0 24.2 %collective-permute-start.13 = (bf16[208,512]{1,0:T(8,128)(2,1)S(1)}, bf16[208,512]{1,0:T(8,128)(2,1)S(1)}, u32[]{:S(2)}, u32[]{:S(2)}) collective-permute-start(bf16[208,512]{1,0:T(8,128)(2,1)S(1)} %get-tuple-element.145), channel_id=1, source_target_pairs={{0,1},{1,0},{2,3},{3,2},{4,5},{5,4},{6,7},{7,6},{8,9},{9,8},{10,11... | collective-permute-start | bytes 638984 | tf_op jit(solution)/shard_map/ppermute | solution.py:789
  102.7 22.5 %collective-permute-start.14 = (bf16[208,512]{1,0:T(8,128)(2,1)S(1)}, bf16[208,512]{1,0:T(8,128)(2,1)S(1)}, u32[]{:S(2)}, u32[]{:S(2)}) collective-permute-start(bf16[208,512]{1,0:T(8,128)(2,1)S(1)} %get-tuple-element.146), channel_id=1, source_target_pairs={{0,3},{1,2},{2,1},{3,0},{4,7},{5,6},{6,5},{7,4},{8,11},{9,10},{10,... | collective-permute-start | bytes 638984 | tf_op jit(solution)/shard_map/ppermute | solution.py:789
  158.2 323.7 %reduce-scatter.3.cloned.1.call-start = ((), (), s32[]{:S(2)}) async-start(), calls=%async_computation.4 | async-start | bytes 9437184 | tf_op jit(solution)/shard_map/reduce_scatter | solution.py:1129
  160.6 10.4 %collective-permute-start.28 = (bf16[208,512]{1,0:T(8,128)(2,1)S(1)}, bf16[208,512]{1,0:T(8,128)(2,1)S(1)}, u32[]{:S(2)}, u32[]{:S(2)}) collective-permute-start(bf16[208,512]{1,0:T(8,128)(2,1)S(1)} %copy-done.94), channel_id=1, source_target_pairs={{3,0},{2,1},{1,2},{0,3},{7,4},{6,5},{5,6},{4,7},{11,8},{10,9},{9,1... | collective-permute-start | bytes 638984 | tf_op jit(solution)/shard_map/ppermute | solution.py:793
  161.2 15.0 %collective-permute-start.27 = (bf16[208,512]{1,0:T(8,128)(2,1)}, bf16[208,512]{1,0:T(8,128)(2,1)S(1)}, u32[]{:S(2)}, u32[]{:S(2)}) collective-permute-start(bf16[208,512]{1,0:T(8,128)(2,1)} %copy-done.99), channel_id=1, source_target_pairs={{1,0},{0,1},{3,2},{2,3},{5,4},{4,5},{7,6},{6,7},{9,8},{8,9},{11,10... | collective-permute-start | bytes 638984 | tf_op jit(solution)/shard_map/ppermute | solution.py:793
  162.8 17.4 %collective-permute-start.29 = (bf16[208,512]{1,0:T(8,128)(2,1)}, bf16[208,512]{1,0:T(8,128)(2,1)S(1)}, u32[]{:S(2)}, u32[]{:S(2)}) collective-permute-start(bf16[208,512]{1,0:T(8,128)(2,1)} %copy-done.97), channel_id=1, source_target_pairs={{3,0},{2,1},{1,2},{0,3},{7,4},{6,5},{5,6},{4,7},{11,8},{10,9},{9,1... | collective-permute-start | bytes 638984 | tf_op jit(solution)/shard_map/ppermute | solution.py:793
  216.2 44.9 %collective-permute-start.36 = (bf16[2,128,2176]{2,1,0:T(8,128)(2,1)}, bf16[2,128,2176]{2,1,0:T(8,128)(2,1)S(1)}, u32[]{:S(2)}, u32[]{:S(2)}) collective-permute-start(bf16[2,128,2176]{2,1,0:T(8,128)(2,1)} %get-tuple-element.197), channel_id=1, source_target_pairs={{0,2},{2,0},{4,6},{6,4},{8,10},{10,8},{12,14},{14,12},{16,18},{18,... | collective-permute-start | bytes 3342344 | tf_op jit(solution)/shard_map/ppermute | solution.py:635
  216.8 26.6 %collective-permute-start.21 = (bf16[416,512]{1,0:T(8,128)(2,1)S(1)}, bf16[416,512]{1,0:T(8,128)(2,1)S(1)}, u32[]{:S(2)}, u32[]{:S(2)}) collective-permute-start(bf16[416,512]{1,0:T(8,128)(2,1)S(1)} %copy-done.82), channel_id=1, source_target_pairs={{2,0},{3,1},{0,2},{1,3},{6,4},{7,5},{4,6},{5,7},{10,8},{11,9},{8,1... | collective-permute-start | bytes 1277960 | tf_op jit(solution)/shard_map/ppermute | solution.py:789
  217.3 27.4 %collective-permute-start.22 = (bf16[416,512]{1,0:T(8,128)(2,1)S(1)}, bf16[416,512]{1,0:T(8,128)(2,1)S(1)}, u32[]{:S(2)}, u32[]{:S(2)}) collective-permute-start(bf16[416,512]{1,0:T(8,128)(2,1)S(1)} %copy-done.80), channel_id=1, source_target_pairs={{1,0},{0,1},{3,2},{2,3},{5,4},{4,5},{7,6},{6,7},{9,8},{8,9},{11,10... | collective-permute-start | bytes 1277960 | tf_op jit(solution)/shard_map/ppermute | solution.py:789
  219.0 25.9 %collective-permute-start.23 = (bf16[416,512]{1,0:T(8,128)(2,1)S(1)}, bf16[416,512]{1,0:T(8,128)(2,1)S(1)}, u32[]{:S(2)}, u32[]{:S(2)}) collective-permute-start(bf16[416,512]{1,0:T(8,128)(2,1)S(1)} %copy-done.78), channel_id=1, source_target_pairs={{3,0},{2,1},{1,2},{0,3},{7,4},{6,5},{5,6},{4,7},{11,8},{10,9},{9,1... | collective-permute-start | bytes 1277960 | tf_op jit(solution)/shard_map/ppermute | solution.py:789
  219.3 23.5 %collective-permute-start.31 = (bf16[208,512]{1,0:T(8,128)(2,1)S(1)}, bf16[208,512]{1,0:T(8,128)(2,1)S(1)}, u32[]{:S(2)}, u32[]{:S(2)}) collective-permute-start(bf16[208,512]{1,0:T(8,128)(2,1)S(1)} %get-tuple-element.189), channel_id=1, source_target_pairs={{0,1},{1,0},{2,3},{3,2},{4,5},{5,4},{6,7},{7,6},{8,9},{9,8},{10,11... | collective-permute-start | bytes 638984 | tf_op jit(solution)/shard_map/ppermute | solution.py:789
  243.5 18.7 %collective-permute-start.33 = (bf16[208,512]{1,0:T(8,128)(2,1)}, bf16[208,512]{1,0:T(8,128)(2,1)S(1)}, u32[]{:S(2)}, u32[]{:S(2)}) collective-permute-start(bf16[208,512]{1,0:T(8,128)(2,1)} %get-tuple-element.193), channel_id=1, source_target_pairs={{0,2},{1,3},{2,0},{3,1},{4,6},{5,7},{6,4},{7,5},{8,10},{9,11},{10,... | collective-permute-start | bytes 638984 | tf_op jit(solution)/shard_map/ppermute | solution.py:789
  244.6 17.6 %collective-permute-start.34 = (bf16[208,512]{1,0:T(8,128)(2,1)S(1)}, bf16[208,512]{1,0:T(8,128)(2,1)S(1)}, u32[]{:S(2)}, u32[]{:S(2)}) collective-permute-start(bf16[208,512]{1,0:T(8,128)(2,1)S(1)} %get-tuple-element.194), channel_id=1, source_target_pairs={{0,1},{1,0},{2,3},{3,2},{4,5},{5,4},{6,7},{7,6},{8,9},{9,8},{10,11... | collective-permute-start | bytes 638984 | tf_op jit(solution)/shard_map/ppermute | solution.py:789
  244.9 17.3 %collective-permute-start.35 = (bf16[208,512]{1,0:T(8,128)(2,1)S(1)}, bf16[208,512]{1,0:T(8,128)(2,1)S(1)}, u32[]{:S(2)}, u32[]{:S(2)}) collective-permute-start(bf16[208,512]{1,0:T(8,128)(2,1)S(1)} %get-tuple-element.195), channel_id=1, source_target_pairs={{0,3},{1,2},{2,1},{3,0},{4,7},{5,6},{6,5},{7,4},{8,11},{9,10},{10,... | collective-permute-start | bytes 638984 | tf_op jit(solution)/shard_map/ppermute | solution.py:789
  297.1 15.1 %collective-permute-start.40 = (bf16[208,512]{1,0:T(8,128)(2,1)S(1)}, bf16[208,512]{1,0:T(8,128)(2,1)S(1)}, u32[]{:S(2)}, u32[]{:S(2)}) collective-permute-start(bf16[208,512]{1,0:T(8,128)(2,1)S(1)} %copy-done.104), channel_id=1, source_target_pairs={{1,0},{0,1},{3,2},{2,3},{5,4},{4,5},{7,6},{6,7},{9,8},{8,9},{11,10... | collective-permute-start | bytes 638984 | tf_op jit(solution)/shard_map/ppermute | solution.py:793
  298.5 16.6 %collective-permute-start.42 = (bf16[208,512]{1,0:T(8,128)(2,1)S(1)}, bf16[208,512]{1,0:T(8,128)(2,1)S(1)}, u32[]{:S(2)}, u32[]{:S(2)}) collective-permute-start(bf16[208,512]{1,0:T(8,128)(2,1)S(1)} %copy-done.101), channel_id=1, source_target_pairs={{3,0},{2,1},{1,2},{0,3},{7,4},{6,5},{5,6},{4,7},{11,8},{10,9},{9,1... | collective-permute-start | bytes 638984 | tf_op jit(solution)/shard_map/ppermute | solution.py:793
  351.5 15.5 %collective-permute-start.45 = (bf16[128,2176]{1,0:T(8,128)(2,1)S(1)}, bf16[128,2176]{1,0:T(8,128)(2,1)S(1)}, u32[]{:S(2)}, u32[]{:S(2)}) collective-permute-start(bf16[128,2176]{1,0:T(8,128)(2,1)S(1)} %copy-done.76), channel_id=1, source_target_pairs={{0,1},{1,0},{2,3},{3,2},{4,5},{5,4},{6,7},{7,6},{8,9},{9,8},{10,11... | collective-permute-start | bytes 1671176 | tf_op jit(solution)/shard_map/ppermute | solution.py:635
  354.2 23.9 %collective-permute-start.44 = (bf16[128,2176]{1,0:T(8,128)(2,1)S(1)}, bf16[128,2176]{1,0:T(8,128)(2,1)S(1)}, u32[]{:S(2)}, u32[]{:S(2)}) collective-permute-start(bf16[128,2176]{1,0:T(8,128)(2,1)S(1)} %get-tuple-element.216), channel_id=1, source_target_pairs={{0,1},{1,0},{2,3},{3,2},{4,5},{5,4},{6,7},{7,6},{8,9},{9,8},{10,11... | collective-permute-start | bytes 1671176 | tf_op jit(solution)/shard_map/ppermute | solution.py:635
  459.5 29.1 %collective-permute-start.46 = (bf16[2,128,2176]{2,1,0:T(8,128)(2,1)}, bf16[2,128,2176]{2,1,0:T(8,128)(2,1)}, u32[]{:S(2)}, u32[]{:S(2)}) collective-permute-start(bf16[2,128,2176]{2,1,0:T(8,128)(2,1)} %bitcast.7.refs_1_), channel_id=1, source_target_pairs={{0,2},{2,0},{4,6},{6,4},{8,10},{10,8},{12,14},{14,12},{16,18},{18,... | collective-permute-start | bytes 3342344 | tf_op jit(solution)/shard_map/ppermute | solution.py:635
  461.8 31.4 %collective-permute-start.48 = (bf16[1,512,512]{2,1,0:T(8,128)(2,1)}, bf16[1,512,512]{2,1,0:T(8,128)(2,1)}, u32[]{:S(2)}, u32[]{:S(2)}) collective-permute-start(bf16[1,512,512]{2,1,0:T(8,128)(2,1)} %get-tuple-element.249), channel_id=1, source_target_pairs={{0,2},{2,0},{4,6},{6,4},{8,10},{10,8},{12,14},{14,12},{16,18},{18,... | collective-permute-start | bytes 1572872 | tf_op jit(solution)/shard_map/ppermute | solution.py:635
  (145 other events, 1454.3 us)
Sparse Core Ops, SparseCore 0:
  158.3 150.7 reduce-scatter.4
  313.1 168.7 reduce-scatter.2
